TPU v7x, 32 devices: a whole 2x2x4 slice. The times are simulated.
32 devices in a mesh: tok: 16 (over z, x, core), blk: 2 (over y).
Axes of the slice: x: 2, y: 2, z: 4, core: 2. Of those that a mesh axis runs over, the one named last changes fastest.
Arguments:
- tokens: bfloat16 [83968, 512], P(('tok', 'blk')), may hold values from -6 to 6
- cotangent: float32 [83968, 512], P(('tok', 'blk')), may hold values from -6 to 6
- grid_class: int32 [1024], P('tok'), may hold values from 0 to 2, as said below
- qkv_weight: float32 [2, 512, 1536], P(None, 'tok', 'blk'), may hold values from -0.25 to 0.25
- proj_weight: float32 [2, 512, 512], P(None, 'blk', 'tok'), may hold values from -0.25 to 0.25
- up_weight: float32 [2, 512, 2048], P(None, 'tok', 'blk'), may hold values from -0.25 to 0.25
- down_weight: float32 [2, 2048, 512], P(None, 'blk', 'tok'), may hold values from -0.125 to 0.125
- norm_params: float32 [2, 4, 512], replicated, may hold values from -1 to 1.6, as said below
- cpe_weight: float32 [2, 9, 512], replicated, may hold values from -2 to 2
- crpe_weight: float32 [2, 49, 512], replicated, may hold values from -0.9 to 0.9
- qkv_moment: float32 [2, 512, 1536], P(None, 'tok', 'blk'), may hold values from -695.45355 to 695.45355
- proj_moment: float32 [2, 512, 512], P(None, 'blk', 'tok'), may hold values from -695.45355 to 695.45355
- up_moment: float32 [2, 512, 2048], P(None, 'tok', 'blk'), may hold values from -695.45355 to 695.45355
- down_moment: float32 [2, 2048, 512], P(None, 'blk', 'tok'), may hold values from -695.45355 to 695.45355
- norm_moment: float32 [2, 4, 512], replicated, may hold values from -1043.1804 to 1043.1804
- cpe_moment: float32 [2, 9, 512], replicated, may hold values from -1043.1804 to 1043.1804
- crpe_moment: float32 [2, 49, 512], replicated, may hold values from -521.5902 to 521.5902
Outputs:
- block_out: bfloat16 [83968, 512], P(('tok', 'blk'))
- tokens_grad: float32 [83968, 512], P(('tok', 'blk'))
- qkv_moment_new: float32 [2, 512, 1536], P(None, 'tok', 'blk')
- qkv_new: float32 [2, 512, 1536], P(None, 'tok', 'blk')
- qkv_copy: bfloat16 [2, 512, 1536], P(None, 'tok', 'blk')
- proj_moment_new: float32 [2, 512, 512], P(None, 'blk', 'tok')
- proj_new: float32 [2, 512, 512], P(None, 'blk', 'tok')
- proj_copy: bfloat16 [2, 512, 512], P(None, 'blk', 'tok')
- up_moment_new: float32 [2, 512, 2048], P(None, 'tok', 'blk')
- up_new: float32 [2, 512, 2048], P(None, 'tok', 'blk')
- up_copy: bfloat16 [2, 512, 2048], P(None, 'tok', 'blk')
- down_moment_new: float32 [2, 2048, 512], P(None, 'blk', 'tok')
- down_new: float32 [2, 2048, 512], P(None, 'blk', 'tok')
- down_copy: bfloat16 [2, 2048, 512], P(None, 'blk', 'tok')
- norm_moment_new: float32 [2, 4, 512], replicated
- norm_new: float32 [2, 4, 512], replicated
- cpe_moment_new: float32 [2, 9, 512], replicated
- cpe_new: float32 [2, 9, 512], replicated
- crpe_moment_new: float32 [2, 49, 512], replicated
- crpe_new: float32 [2, 49, 512], replicated
Inputs may be any that keep to these rules, and one draw needn't show every extreme that they name: `grid_class`: grid class c is an image of (5 + 2c) x (5 + 2c) patches; images lie 64 to an index of tok in order, and larger classes grow more common with that index. `norm_params`: rows 0 and 2 of each layer are gains of the two norms, rows 1 and 3 their shifts.
All inputs are finite; a program needn't handle non-finite values.
Results may differ from a plain program's by a relative error of at most 0.023.
Values may be sent and summed in bfloat16 or wider, within the bound.
A program may use at most 960 MiB of HBM per device.

v0:
```python
import math

import jax
import jax.numpy as jnp
from jax import lax
from jax.sharding import PartitionSpec as P

HEADS = 8
GROUPS = 8


FULL_PRECISION = lax.Precision.HIGHEST
SCHULZ_COEFFS = (3.4445, -4.775, 2.0315)
MUON_RATES = (0.8, 0.8, 0.8, 0.4)
SMALL_RATES = (0.3, 0.3, 0.15)


def spatial_masks(grid_class):
    extent = 5 + 2 * grid_class
    across = (jnp.arange(9, dtype=jnp.int32)[None, :] < extent[:, None]).astype(jnp.float32)
    cell_mask = across[:, :, None] * across[:, None, :]
    images = grid_class.shape[0]
    key_mask = jnp.concatenate(
        [jnp.ones((images, 1), jnp.float32), cell_mask.reshape(images, 81)], axis=1
    )
    return (cell_mask, key_mask)


def tap_mask(head_ids):
    radius = jnp.where(head_ids < 2, 1, jnp.where(head_ids < 5, 2, 3))
    offsets = jnp.abs(jnp.arange(7, dtype=jnp.int32) - 3)
    within = (offsets[:, None] <= radius[None, :]).astype(jnp.float32)
    return (within[:, None, :] * within[None, :, :]).reshape(49, head_ids.shape[0])


def depthwise(grid_cells, kernel, extent):
    margin = extent // 2
    padded = jnp.pad(grid_cells, ((0, 0), (margin, margin), (margin, margin), (0, 0)))
    summed = jnp.zeros_like(grid_cells)
    for row_at in range(extent):
        for col_at in range(extent):
            summed = (
                summed
                + padded[:, row_at : row_at + 9, col_at : col_at + 9, :]
                * kernel[row_at * extent + col_at]
            )
    return summed


def position_conv(stream, kernel, cell_mask):
    images, slot_len, channels = stream.shape
    grid_cells = stream[:, 1:, :].reshape(images, 9, 9, channels) * cell_mask[..., None]
    conv_out = depthwise(grid_cells, kernel, 3) * cell_mask[..., None]
    return stream + jnp.concatenate(
        [jnp.zeros((images, 1, channels), jnp.float32), conv_out.reshape(images, 81, channels)],
        axis=1,
    )


def layer_norm(values, norm_gain, norm_shift):
    center = values - jnp.mean(values, axis=-1, keepdims=True)
    spread = jnp.mean(center * center, axis=-1, keepdims=True)
    return center * lax.rsqrt(spread + 1e-06) * norm_gain + norm_shift


def factor_attention(packed, kernel, cell_mask, key_mask):
    images, slot_len, head_count, triple, head_dim = packed.shape
    query_rows = packed[:, :, :, 0]
    key_rows = packed[:, :, :, 1]
    value_rows = packed[:, :, :, 2]
    key_live = key_mask[:, :, None, None]
    top_key = jnp.max(jnp.where(key_live > 0, key_rows, -1e30), axis=1, keepdims=True)
    shifted = jnp.where(key_live > 0, key_rows - top_key, -60.0)
    weights_raw = jnp.exp(shifted) * key_live
    key_weights = weights_raw / jnp.sum(weights_raw, axis=1, keepdims=True)
    context = jnp.einsum("nthc,nthd->nhcd", key_weights, value_rows, precision=FULL_PRECISION)
    factor = jnp.einsum(
        "nthc,nhcd->nthd", query_rows, context, precision=FULL_PRECISION
    ) * head_dim ** (-0.5)
    grid_cells = (
        value_rows[:, 1:].reshape(images, 9, 9, head_count * head_dim) * cell_mask[..., None]
    )
    conv_out = (
        depthwise(grid_cells, kernel.reshape(49, head_count * head_dim), 7) * cell_mask[..., None]
    )
    relative = query_rows[:, 1:] * conv_out.reshape(images, 81, head_count, head_dim)
    relative = jnp.concatenate([jnp.zeros_like(query_rows[:, :1]), relative], axis=1)
    return (factor + relative).reshape(images, slot_len, head_count * head_dim)


def attend(packed_rows, kernel_raw, tap_weights, cell_mask, key_mask):
    images = cell_mask.shape[0]
    head_count = tap_weights.shape[1]
    head_dim = kernel_raw.shape[1] // head_count
    total_rows = packed_rows.shape[0]
    kernel = kernel_raw.reshape(49, head_count, head_dim) * tap_weights[:, :, None]
    mixed_heads = factor_attention(
        packed_rows.reshape(images, total_rows // images, head_count, 3, head_dim),
        kernel,
        cell_mask,
        key_mask,
    )
    return mixed_heads.reshape(total_rows, head_count * head_dim)


def front_part(stream, norm_gain, norm_shift, kernel, cell_mask):
    images = cell_mask.shape[0]
    after_conv = position_conv(
        stream.reshape(images, stream.shape[0] // images, stream.shape[1]), kernel, cell_mask
    ).reshape(stream.shape)
    return (layer_norm(after_conv, norm_gain, norm_shift), after_conv)


def gelu_exact(values):
    return jax.nn.gelu(values, approximate=False)


def orthogonalize(matrix):
    is_tall = matrix.shape[0] > matrix.shape[1]
    current = matrix.T if is_tall else matrix
    current = current / (jnp.sqrt(jnp.sum(current * current)) + 1e-07)
    first_coef, second_coef, third_coef = SCHULZ_COEFFS
    for sweep_at in range(5):
        gram_matrix = jnp.dot(current, current.T, precision=FULL_PRECISION)
        polynomial = second_coef * gram_matrix + third_coef * jnp.dot(
            gram_matrix, gram_matrix, precision=FULL_PRECISION
        )
        current = first_coef * current + jnp.dot(polynomial, current, precision=FULL_PRECISION)
    return current.T if is_tall else current


def column_blocks(matrix, pieces):
    layers, height, breadth = matrix.shape
    return (
        matrix.reshape(layers, height, pieces, breadth // pieces)
        .transpose(0, 2, 1, 3)
        .reshape(layers * pieces, height, breadth // pieces)
    )


def from_column_blocks(blocks, layers, pieces):
    block_count, height, narrow = blocks.shape
    return (
        blocks.reshape(layers, pieces, height, narrow)
        .transpose(0, 2, 1, 3)
        .reshape(layers, height, pieces * narrow)
    )


def row_blocks(matrix, pieces):
    return matrix.reshape(matrix.shape[0] * pieces, matrix.shape[1] // pieces, matrix.shape[2])


def from_row_blocks(blocks, layers, pieces):
    return blocks.reshape(layers, pieces * blocks.shape[1], blocks.shape[2])


def block_scale(height, breadth):
    return math.sqrt(max(1.0, height / breadth))


def normalized_step(param_vals, moment, grads_in, rate, axes):
    fresh = 0.5 * moment + grads_in
    level = jnp.sqrt(jnp.mean(fresh * fresh, axis=axes, keepdims=True))
    return (fresh, param_vals - rate * fresh / (level + 1e-06))


def contract_rows(former, latter):
    return lax.dot_general(
        former, latter, (((0,), (0,)), ((), ())), preferred_element_type=jnp.float32
    )


def contract_cols(former, latter):
    return lax.dot_general(
        former, latter, (((1,), (1,)), ((), ())), preferred_element_type=jnp.float32
    )


def row_product(source, matrix):
    return jnp.dot(source, matrix, preferred_element_type=jnp.float32)


def row_back(source, matrix):
    return contract_cols(source, matrix)


def fold_back(source, matrix, incoming):
    weight_sum = contract_rows(source, incoming)
    back_rows = contract_cols(incoming, matrix)
    return (weight_sum, back_rows)


def place_moment(grads_full, moment, axis_at, tok_at):
    extent = moment.shape[axis_at]
    placed = lax.dynamic_update_slice_in_dim(
        jnp.zeros_like(grads_full), 0.5 * moment, tok_at * extent, axis_at
    )
    return grads_full + placed


def own_rows(whole, axis_at, extent, tok_at):
    return lax.dynamic_slice_in_dim(whole, tok_at * extent, extent, axis_at)


def on_device(
    tokens,
    cotangent,
    grid_class,
    qkv_weight,
    proj_weight,
    up_weight,
    down_weight,
    norm_params,
    cpe_weight,
    crpe_weight,
    qkv_moment,
    proj_moment,
    up_moment,
    down_moment,
    norm_moment,
    cpe_moment,
    crpe_moment,
):
    own_count, channels = tokens.shape
    blk_count = lax.axis_size("blk")
    blk_at = lax.axis_index("blk")
    tok_at = lax.axis_index("tok")
    layer_count = qkv_weight.shape[0]
    images_own = grid_class.shape[0] // blk_count
    head_dim = channels // HEADS
    heads_own = HEADS // blk_count
    groups_own = GROUPS // blk_count
    group_width = up_weight.shape[2] // groups_own
    own_class = lax.dynamic_slice_in_dim(grid_class, blk_at * images_own, images_own)
    cells_own, keys_own = spatial_masks(own_class)
    cells_all, keys_all = spatial_masks(grid_class)
    taps_own = tap_mask(blk_at * heads_own + jnp.arange(heads_own, dtype=jnp.int32))
    gathered = (
        lax.all_gather(qkv_weight.astype(jnp.bfloat16), "tok", axis=1, tiled=True),
        lax.all_gather(proj_weight.astype(jnp.bfloat16), "tok", axis=2, tiled=True),
        lax.all_gather(up_weight.astype(jnp.bfloat16), "tok", axis=1, tiled=True),
        lax.all_gather(down_weight.astype(jnp.bfloat16), "tok", axis=2, tiled=True),
    )
    stream = tokens.astype(jnp.float32)
    saved = []
    for layer_at in range(layer_count):
        w_query = gathered[0][layer_at]
        w_proj = gathered[1][layer_at]
        w_up = gathered[2][layer_at]
        w_down = gathered[3][layer_at]
        normed, after_conv = front_part(
            stream,
            norm_params[layer_at, 0],
            norm_params[layer_at, 1],
            cpe_weight[layer_at],
            cells_own,
        )
        normed = normed.astype(jnp.bfloat16)
        rows_in = lax.all_gather(normed, "blk", axis=0, tiled=True)
        kernel_use = lax.dynamic_slice_in_dim(
            crpe_weight[layer_at], blk_at * heads_own * head_dim, heads_own * head_dim, 1
        )
        masks_use = (taps_own, cells_all, keys_all)
        packed = jnp.dot(rows_in, w_query, preferred_element_type=jnp.float32).astype(jnp.bfloat16)
        mixed_heads = attend(
            packed.astype(jnp.float32), kernel_use, masks_use[0], masks_use[1], masks_use[2]
        ).astype(jnp.bfloat16)
        attention = lax.psum_scatter(
            row_product(mixed_heads, w_proj).astype(jnp.bfloat16),
            "blk",
            scatter_dimension=0,
            tiled=True,
        ).astype(jnp.float32)
        after_att = after_conv + attention
        normed_mid = layer_norm(
            after_att, norm_params[layer_at, 2], norm_params[layer_at, 3]
        ).astype(jnp.bfloat16)
        mid_rows = lax.all_gather(normed_mid, "blk", axis=0, tiled=True)
        hidden = jnp.dot(mid_rows, w_up, preferred_element_type=jnp.float32)
        active = gelu_exact(hidden).astype(jnp.bfloat16)
        feed = lax.psum_scatter(
            row_product(active, w_down).astype(jnp.bfloat16), "blk", scatter_dimension=0, tiled=True
        ).astype(jnp.float32)
        saved.append(
            (
                stream,
                after_att,
                rows_in,
                packed,
                kernel_use,
                masks_use,
                mixed_heads,
                mid_rows,
                hidden,
                active,
                w_query,
                w_proj,
                w_up,
                w_down,
            )
        )
        stream = after_att + feed
    block_out = stream.astype(jnp.bfloat16)
    upstream = cotangent * keys_own.reshape(own_count)[:, None]
    collected = []
    for layer_at in reversed(range(layer_count)):
        (
            layer_in,
            after_att,
            rows_in,
            packed,
            kernel_use,
            masks_use,
            mixed_heads,
            mid_rows,
            hidden,
            active,
            w_query,
            w_proj,
            w_up,
            w_down,
        ) = saved[layer_at]
        down_in = upstream.astype(jnp.bfloat16)
        grad_down, grad_active = fold_back(
            active, w_down, lax.all_gather(down_in, "blk", axis=0, tiled=True)
        )
        grad_hidden = jax.vjp(gelu_exact, hidden)[1](grad_active)[0].astype(jnp.bfloat16)
        grad_up = contract_rows(mid_rows, grad_hidden)
        grad_mid = lax.psum_scatter(
            row_back(grad_hidden, w_up).astype(jnp.bfloat16), "blk", scatter_dimension=0, tiled=True
        ).astype(jnp.float32)
        grad_att, grad_gain_mid, grad_shift_mid = jax.vjp(
            layer_norm, after_att, norm_params[layer_at, 2], norm_params[layer_at, 3]
        )[1](grad_mid)
        grad_att = grad_att + upstream
        att_in = grad_att.astype(jnp.bfloat16)
        grad_proj, grad_mixed = fold_back(
            mixed_heads, w_proj, lax.all_gather(att_in, "blk", axis=0, tiled=True)
        )
        attend_pull = jax.vjp(
            lambda packed_vals, kernel_vals: attend(
                packed_vals, kernel_vals, masks_use[0], masks_use[1], masks_use[2]
            ),
            packed.astype(jnp.float32),
            kernel_use,
        )[1]
        grad_packed, grad_kernel = attend_pull(grad_mixed)
        grad_packed = grad_packed.astype(jnp.bfloat16)
        grad_query = contract_rows(rows_in, grad_packed)
        grad_rows = lax.psum_scatter(
            row_back(grad_packed, w_query).astype(jnp.bfloat16),
            "blk",
            scatter_dimension=0,
            tiled=True,
        ).astype(jnp.float32)
        grad_kernel = lax.dynamic_update_slice_in_dim(
            jnp.zeros((49, channels), jnp.float32), grad_kernel, blk_at * heads_own * head_dim, 1
        )
        front_pull = jax.vjp(
            lambda stream_vals, gain_vals, shift_vals, conv_vals: front_part(
                stream_vals, gain_vals, shift_vals, conv_vals, cells_own
            ),
            layer_in,
            norm_params[layer_at, 0],
            norm_params[layer_at, 1],
            cpe_weight[layer_at],
        )[1]
        upstream, grad_gain_in, grad_shift_in, grad_conv = front_pull((grad_rows, grad_att))
        collected.append(
            (
                grad_query,
                grad_proj,
                grad_up,
                grad_down,
                jnp.stack([grad_gain_in, grad_shift_in, grad_gain_mid, grad_shift_mid]),
                grad_conv,
                grad_kernel,
            )
        )
    collected = collected[::-1]
    stacked = [jnp.stack([per_layer[slot_at] for per_layer in collected]) for slot_at in range(7)]
    norm_grads, conv_grads, kernel_grads = (
        lax.psum(stacked[4].astype(jnp.bfloat16), "blk").astype(jnp.float32),
        lax.psum(stacked[5].astype(jnp.bfloat16), "blk").astype(jnp.float32),
        lax.psum(stacked[6].astype(jnp.bfloat16), "blk").astype(jnp.float32),
    )
    summed = (
        lax.psum(
            place_moment(stacked[0], qkv_moment, 1, tok_at).astype(jnp.bfloat16), "tok"
        ).astype(jnp.float32),
        lax.psum(
            place_moment(stacked[1], proj_moment, 2, tok_at).astype(jnp.bfloat16), "tok"
        ).astype(jnp.float32),
        lax.psum(place_moment(stacked[2], up_moment, 1, tok_at).astype(jnp.bfloat16), "tok").astype(
            jnp.float32
        ),
        lax.psum(
            place_moment(stacked[3], down_moment, 2, tok_at).astype(jnp.bfloat16), "tok"
        ).astype(jnp.float32),
        lax.psum(norm_grads.astype(jnp.bfloat16), "tok").astype(jnp.float32),
        lax.psum(conv_grads.astype(jnp.bfloat16), "tok").astype(jnp.float32),
        lax.psum(kernel_grads.astype(jnp.bfloat16), "tok").astype(jnp.float32),
    )
    blocked = (
        column_blocks(summed[0], heads_own),
        row_blocks(summed[1], heads_own),
        column_blocks(summed[2], groups_own),
        row_blocks(summed[3], groups_own),
    )
    row_sizes = (
        qkv_weight.shape[1],
        proj_weight.shape[2],
        up_weight.shape[1],
        down_weight.shape[2],
    )
    row_axes = (1, 2, 1, 2)
    ortho = [jax.vmap(orthogonalize)(matrices) for matrices in blocked]
    ortho_full = (
        from_column_blocks(ortho[0], layer_count, heads_own),
        from_row_blocks(ortho[1], layer_count, heads_own),
        from_column_blocks(ortho[2], layer_count, groups_own),
        from_row_blocks(ortho[3], layer_count, groups_own),
    )
    ortho_rows = tuple(
        (
            own_rows(ortho_full[kind_at], row_axes[kind_at], row_sizes[kind_at], tok_at)
            for kind_at in range(4)
        )
    )
    scales = (
        block_scale(channels, 3 * head_dim),
        block_scale(head_dim, channels),
        block_scale(channels, group_width),
        block_scale(group_width, channels),
    )
    weights_old = (qkv_weight, proj_weight, up_weight, down_weight)
    results = []
    for kind_at in range(4):
        moment_rows = own_rows(summed[kind_at], row_axes[kind_at], row_sizes[kind_at], tok_at)
        new_rows = (
            weights_old[kind_at] - MUON_RATES[kind_at] * scales[kind_at] * ortho_rows[kind_at]
        )
        results.extend([moment_rows, new_rows, new_rows.astype(jnp.bfloat16)])
    norm_fresh, norm_new = normalized_step(
        norm_params, norm_moment, summed[4], SMALL_RATES[0], (2,)
    )
    conv_fresh, conv_new = normalized_step(
        cpe_weight, cpe_moment, summed[5], SMALL_RATES[1], (1, 2)
    )
    head_shape = (layer_count, 49, HEADS, head_dim)
    kernel_fresh, kernel_new = normalized_step(
        crpe_weight.reshape(head_shape),
        crpe_moment.reshape(head_shape),
        summed[6].reshape(head_shape),
        SMALL_RATES[2],
        (1, 3),
    )
    return (
        block_out,
        upstream,
        results[0],
        results[1],
        results[2],
        results[3],
        results[4],
        results[5],
        results[6],
        results[7],
        results[8],
        results[9],
        results[10],
        results[11],
        norm_fresh,
        norm_new,
        conv_fresh,
        conv_new,
        kernel_fresh.reshape(crpe_weight.shape),
        kernel_new.reshape(crpe_weight.shape),
    )


def solution(mesh):
    in_specs = (
        P(("tok", "blk"), None),
        P(("tok", "blk"), None),
        P("tok"),
        P(None, "tok", "blk"),
        P(None, "blk", "tok"),
        P(None, "tok", "blk"),
        P(None, "blk", "tok"),
        P(),
        P(),
        P(),
        P(None, "tok", "blk"),
        P(None, "blk", "tok"),
        P(None, "tok", "blk"),
        P(None, "blk", "tok"),
        P(),
        P(),
        P(),
    )
    out_specs = (
        P(("tok", "blk"), None),
        P(("tok", "blk"), None),
        P(None, "tok", "blk"),
        P(None, "tok", "blk"),
        P(None, "tok", "blk"),
        P(None, "blk", "tok"),
        P(None, "blk", "tok"),
        P(None, "blk", "tok"),
        P(None, "tok", "blk"),
        P(None, "tok", "blk"),
        P(None, "tok", "blk"),
        P(None, "blk", "tok"),
        P(None, "blk", "tok"),
        P(None, "blk", "tok"),
        P(),
        P(),
        P(),
        P(),
        P(),
        P(),
    )
    return jax.shard_map(
        on_device, mesh=mesh, in_specs=in_specs, out_specs=out_specs, check_vma=False
    )
```

profile of v0, /device:TPU:0, one launch (start us, length us, event | category | flops | bytes accessed | tf_op | source)
XLA Modules:
  0.0 3634.1 jit_solution(9549570428026390067)
XLA Ops:
  85.0 24.6 all_gather.38
  109.6 31.3 all-gather.12.cloned.1.call-done
  151.1 40.0 %reshape.1542 = bf16[64,82,4,3,64]{4,3,2,1,0:T(4,128)(2,1)} reshape(bf16[5248,768]{1,0:T(8,128)(2,1)} %convolution_convert_fusion.1) | data formatting | bytes 16121856 | tf_op jit(solution)/shard_map/reshape | solution.py:98
  191.1 31.1 copy.307
  313.5 70.4 %add_multiply_fusion.2 = f32[64,9,9,256]{3,0,2,1:T(8,128)} fusion(f32[64,9,9,256]{3,0,2,1:T(8,128)} %broadcast_multiply_fusion.110, f32[256]{0:T(256)S(1)} %mul.3956, f32[256]{0:T(256)} %mul.3953, f32[256]{0:T(256)} %mul.3950, f32[256]{0:T(256)} %mul.3947, f32[256]{0:T(256)} %mul.3944, f32[256]{0:T(256)} %mul.3941, f32[256]{0:T(256)} %mul.3938, ...), kind=kLoop, calls=%fused_computation.420 | loop fusion | flops 130056192 | bytes 10687744 | tf_op jit(solution)/shard_map/mul | solution.py:84
  419.1 17.9 fusion.29
  457.0 65.6 %reduce-scatter.9.cloned.1.call-done = bf16[2624,512]{1,0:T(8,128)(2,1)} async-done(((bf16[5248,512]{1,0:T(8,128)(2,1)}), bf16[2624,512]{1,0:T(8,128)(2,1)}) %reduce-scatter.9.cloned.1.call-update) | async-done | bytes 2686992 | tf_op jit(solution)/shard_map/reduce_scatter | solution.py:269
  532.5 34.5 all-gather.18.cloned.1.call-done
  566.9 70.9 %all-gather.16.cloned.1.call-done = bf16[5248,512]{1,0:T(8,128)(2,1)} async-done(((bf16[2624,512]{1,0:T(8,128)(2,1)}), bf16[5248,512]{1,0:T(8,128)(2,1)}) %all-gather.16.cloned.1.call-update) | async-done | bytes 5373968 | tf_op jit(solution)/shard_map/all_gather | solution.py:279
  637.8 54.1 %multiply_convert_fusion.1 = (bf16[5248,1024]{1,0:T(8,128)(2,1)}, f32[5248,1024]{1,0:T(8,128)}, f32[5248,1024]{1,0:T(8,128)}) fusion(bf16[5248,512]{1,0:T(8,128)(2,1)} %all-gather.16.cloned.1.call-done, bf16[2,512,1024]{2,1,0:T(8,128)(2,1)} %all-gather.18.cloned.1.call-done), kind=kOutput, calls=%fused_computation.117 | convolution fusion | flops 5852233728 | bytes 60162048 | tf_op jit(solution)/shard_map/dot_general | solution.py:280
  702.3 67.2 %reduce-scatter.11.cloned.1.call-done = bf16[2624,512]{1,0:T(8,128)(2,1)} async-done(((bf16[5248,512]{1,0:T(8,128)(2,1)}), bf16[2624,512]{1,0:T(8,128)(2,1)}) %reduce-scatter.11.cloned.1.call-update) | async-done | bytes 2686992 | tf_op jit(solution)/shard_map/reduce_scatter | solution.py:282
  844.6 59.2 %all-gather.22.cloned.1.call-done = bf16[5248,512]{1,0:T(8,128)(2,1)} async-done(((bf16[2624,512]{1,0:T(8,128)(2,1)}), bf16[5248,512]{1,0:T(8,128)(2,1)}) %all-gather.22.cloned.1.call-update) | async-done | bytes 5373968 | tf_op jit(solution)/shard_map/all_gather | solution.py:260
  912.8 39.8 %reshape.1543 = bf16[64,82,4,3,64]{4,3,2,1,0:T(4,128)(2,1)} reshape(bf16[5248,768]{1,0:T(8,128)(2,1)} %convolution_convert_fusion) | data formatting | bytes 16121856 | tf_op jit(solution)/shard_map/reshape | solution.py:98
  952.6 31.2 copy.318
  1074.9 73.3 %add_multiply_fusion = f32[64,9,9,256]{3,0,2,1:T(8,128)} fusion(f32[64,9,9,256]{3,0,2,1:T(8,128)} %broadcast_multiply_fusion.109, f32[256]{0:T(256)S(1)} %mul.4154, f32[256]{0:T(256)S(1)} %mul.4151, f32[256]{0:T(256)} %mul.4148, f32[256]{0:T(256)} %mul.4145, f32[256]{0:T(256)} %mul.4142, f32[256]{0:T(256)} %mul.4139, f32[256]{0:T(256)} %mul.4136, ...), kind=kLoop, calls=%fused_computation.418 | loop fusion | flops 130056192 | bytes 10687744 | tf_op jit(solution)/shard_map/mul | solution.py:84
  1219.7 67.2 %reduce-scatter.13.cloned.1.call-done = bf16[2624,512]{1,0:T(8,128)(2,1)} async-done(((bf16[5248,512]{1,0:T(8,128)(2,1)}), bf16[2624,512]{1,0:T(8,128)(2,1)}) %reduce-scatter.13.cloned.1.call-update) | async-done | bytes 2686992 | tf_op jit(solution)/shard_map/reduce_scatter | solution.py:269
  1301.6 64.5 %all-gather.24.cloned.1.call-done = bf16[5248,512]{1,0:T(8,128)(2,1)} async-done(((bf16[2624,512]{1,0:T(8,128)(2,1)}), bf16[5248,512]{1,0:T(8,128)(2,1)}) %all-gather.24.cloned.1.call-update) | async-done | bytes 5373968 | tf_op jit(solution)/shard_map/all_gather | solution.py:279
  1366.1 54.6 %multiply_convert_fusion = (bf16[5248,1024]{1,0:T(8,128)(2,1)}, f32[5248,1024]{1,0:T(8,128)}, f32[5248,1024]{1,0:T(8,128)}) fusion(bf16[5248,512]{1,0:T(8,128)(2,1)} %all-gather.24.cloned.1.call-done, bf16[2,512,1024]{2,1,0:T(8,128)(2,1)S(1)} %copy-done.352), kind=kOutput, calls=%fused_computation.104 | convolution fusion | flops 5852233728 | bytes 60162048 | tf_op jit(solution)/shard_map/dot_general | solution.py:280
  1437.8 23.8 add_convert_fusion.3
  1487.0 53.6 %reduce-scatter.17.cloned.1.call-done = bf16[2624,512]{1,0:T(8,128)(2,1)} async-done(((bf16[5248,512]{1,0:T(8,128)(2,1)}), bf16[2624,512]{1,0:T(8,128)(2,1)}) %reduce-scatter.17.cloned.1.call-update) | async-done | bytes 2686992 | tf_op jit(solution)/shard_map/reduce_scatter | solution.py:330
  1546.6 63.4 %reduce-scatter.15.cloned.1.call-done = bf16[2624,512]{1,0:T(8,128)(2,1)} async-done(((bf16[5248,512]{1,0:T(8,128)(2,1)}), bf16[2624,512]{1,0:T(8,128)(2,1)}) %reduce-scatter.15.cloned.1.call-update) | async-done | bytes 2686992 | tf_op jit(solution)/shard_map/reduce_scatter | solution.py:282
  1624.6 69.2 %all-gather.28.cloned.1.call-done = bf16[5248,512]{1,0:T(8,128)(2,1)} async-done(((bf16[2624,512]{1,0:T(8,128)(2,1)}), bf16[5248,512]{1,0:T(8,128)(2,1)}) %all-gather.28.cloned.1.call-update) | async-done | bytes 5373968 | tf_op jit(solution)/shard_map/all_gather | solution.py:339
  1754.3 25.4 multiply_reduce_fusion.55
  1779.9 22.8 broadcast_multiply_fusion.2
  1803.0 31.7 broadcast_multiply_fusion.1
  1834.9 31.0 broadcast_multiply_fusion
  1899.9 92.9 %pad_add_fusion.1 = f32[64,15,15,256]{3,0,2,1:T(8,128)S(1)} fusion(f32[64,9,9,256]{3,0,2,1:T(8,128)} %get-tuple-element.405, f32[64,9,9,256]{3,0,2,1:T(8,128)} %get-tuple-element.406, f32[64,9,9,256]{3,0,2,1:T(8,128)} %get-tuple-element.407, f32[64,9,9,256]{3,0,2,1:T(8,128)} %get-tuple-element.408, f32[64,9,9,256]{3,0,2,1:T(8,128)} %get-tuple-element.409, ...), kind=kLoop, calls=%fused_computation.133 | loop fusion | flops 154828800 | bytes 243007488 | tf_op jit(solution)/shard_map/transpose(jvp())/add_any | solution.py:44
  2076.6 21.7 convert_element_type.278
  2107.9 67.2 %reduce-scatter.19.cloned.1.call-done = bf16[2624,512]{1,0:T(8,128)(2,1)} async-done(((bf16[5248,512]{1,0:T(8,128)(2,1)}), bf16[2624,512]{1,0:T(8,128)(2,1)}) %reduce-scatter.19.cloned.1.call-update) | async-done | bytes 2686992 | tf_op jit(solution)/shard_map/reduce_scatter | solution.py:351
  2209.9 19.0 broadcast_multiply_fusion.49
  2268.4 70.1 %all-gather.30.cloned.1.call-done = bf16[5248,512]{1,0:T(8,128)(2,1)} async-done(((bf16[2624,512]{1,0:T(8,128)(2,1)}), bf16[5248,512]{1,0:T(8,128)(2,1)}) %all-gather.30.cloned.1.call-update) | async-done | bytes 5373968 | tf_op jit(solution)/shard_map/all_gather | solution.py:326
  2338.6 21.8 add_convert_fusion.2
  2399.6 28.6 multiply_reduce_fusion.56
  2428.2 25.5 multiply_reduce_fusion.57
  2508.5 31.9 all-gather.32.cloned.1.call-done
  2552.6 23.8 multiply_reduce_fusion.1
  2610.4 28.1 multiply_reduce_fusion.104
  2638.6 22.0 multiply_reduce_fusion.105
  2660.6 22.6 multiply_reduce_fusion.103
  2683.3 22.7 broadcast_multiply_fusion.60
  2706.3 31.7 broadcast_multiply_fusion.59
  2738.2 31.0 broadcast_multiply_fusion.58
  2806.2 92.8 %pad_add_fusion = f32[64,15,15,256]{3,0,2,1:T(8,128)S(1)} fusion(f32[64,9,9,256]{3,0,2,1:T(8,128)} %get-tuple-element.350, f32[64,9,9,256]{3,0,2,1:T(8,128)} %get-tuple-element.351, f32[64,9,9,256]{3,0,2,1:T(8,128)} %get-tuple-element.352, f32[64,9,9,256]{3,0,2,1:T(8,128)} %get-tuple-element.353, f32[64,9,9,256]{3,0,2,1:T(8,128)} %get-tuple-element.354, ...), kind=kLoop, calls=%fused_computation.132 | loop fusion | flops 154828800 | bytes 243007488 | tf_op jit(solution)/shard_map/transpose(jvp())/add_any | solution.py:44
  2982.4 21.9 convert_element_type.288
  3037.3 124.7 %all-reduce.262.cloned.1.call-done = (bf16[2,512,768]{2,1,0:T(8,128)(2,1)}, bf16[2,256,512]{1,2,0:T(8,128)(2,1)}, bf16[2,512,1024]{2,1,0:T(8,128)(2,1)}, bf16[2,1024,512]{1,2,0:T(8,128)(2,1)}, bf16[2,49,512]{2,0,1:T(2,128)(2,1)}) async-done(((bf16[2,512,768]{2,1,0:T(8,128)(2,1)}, bf16[2,256,512]{1,2,0:T(8,128)(2,1)}, bf16[2,512,1024]{2,1,0:T(8,128)(2,1)}, bf16[2,1024,512]{1,2,0:T(8,128)(2,1)}, ...) | async-done | bytes 6391824 | tf_op jit(solution)/shard_map/psum | solution.py:389
  3482.5 20.5 multiply_reduce_fusion.121
  3503.1 19.1 broadcast_multiply_fusion.111
  3531.4 58.8 %all-reduce.254 = (bf16[2,4,512]{2,1,0:T(4,128)(2,1)S(1)}, bf16[2,9,512]{2,1,0:T(8,128)(2,1)S(1)}) all-reduce(bf16[2,4,512]{2,1,0:T(4,128)(2,1)S(1)} %get-tuple-element.279, bf16[2,9,512]{2,1,0:T(8,128)(2,1)S(1)} %get-tuple-element.280), channel_id=1, replica_groups=mesh['tok'=16,'blk'=2] {'tok'}, use_global_device_ids=true, to_apply=%region_53.54 | all-reduce | flops 13312 | bytes 53248 | tf_op jit(solution)/shard_map/psum | solution.py:401
  (1319 shorter events, 1497.1 us)
Async XLA Ops:
  7.2 102.4 %all-gather.14.cloned.1.call-start = ((), (), s32[]{:S(2)}) async-start(), calls=%async_computation.9 | async-start | bytes 1671168 | tf_op jit(solution)/shard_map/all_gather | solution.py:240
  8.8 132.0 %all-gather.12.cloned.1.call-start = ((), (), s32[]{:S(2)}) async-start(), calls=%async_computation.8 | async-start | bytes 8060928 | tf_op jit(solution)/shard_map/all_gather | solution.py:260
  62.9 466.0 %copy-start.135 = (f32[1,1,512]{2,1,0:T(1,128)}, f32[1,1,512]{2,1,0:T(1,128)S(1)}, u32[]{:S(2)}) copy-start(f32[1,1,512]{2,1,0:T(1,128)S(1)} %get-tuple-element.583) | copy-start | bytes 6148
  68.0 454.7 %reduce-scatter.9.cloned.1.call-start = ((), (), s32[]{:S(2)}) async-start(), calls=%async_computation.10 | async-start | bytes 8060928 | tf_op jit(solution)/shard_map/reduce_scatter | solution.py:269
  68.5 244.8 %copy-start.15 = (f32[64,9,9]{0,2,1:T(8,128)}, f32[64,9,9]{0,2,1:T(8,128)S(1)}, u32[]{:S(2)}) copy-start(f32[64,9,9]{0,2,1:T(8,128)S(1)} %broadcast_multiply_fusion.126) | copy-start | bytes 62212
  70.1 243.1 %copy-start.196 = (f32[256]{0:T(256)}, f32[256]{0:T(256)S(1)}, u32[]{:S(2)}) copy-start(f32[256]{0:T(256)S(1)} %mul.1860) | copy-start | bytes 3076
  70.2 243.0 %copy-start.176 = (f32[256]{0:T(256)}, f32[256]{0:T(256)S(1)}, u32[]{:S(2)}) copy-start(f32[256]{0:T(256)S(1)} %mul.1890) | copy-start | bytes 3076
  70.3 243.0 %copy-start.178 = (f32[256]{0:T(256)}, f32[256]{0:T(256)S(1)}, u32[]{:S(2)}) copy-start(f32[256]{0:T(256)S(1)} %mul.1887) | copy-start | bytes 3076
  70.3 242.9 %copy-start.180 = (f32[256]{0:T(256)}, f32[256]{0:T(256)S(1)}, u32[]{:S(2)}) copy-start(f32[256]{0:T(256)S(1)} %mul.1884) | copy-start | bytes 3076
  70.4 242.8 %copy-start.182 = (f32[256]{0:T(256)}, f32[256]{0:T(256)S(1)}, u32[]{:S(2)}) copy-start(f32[256]{0:T(256)S(1)} %mul.1881) | copy-start | bytes 3076
  70.5 242.8 %copy-start.184 = (f32[256]{0:T(256)}, f32[256]{0:T(256)S(1)}, u32[]{:S(2)}) copy-start(f32[256]{0:T(256)S(1)} %mul.1878) | copy-start | bytes 3076
  70.6 242.7 %copy-start.186 = (f32[256]{0:T(256)}, f32[256]{0:T(256)S(1)}, u32[]{:S(2)}) copy-start(f32[256]{0:T(256)S(1)} %mul.1875) | copy-start | bytes 3076
  70.7 242.6 %copy-start.188 = (f32[256]{0:T(256)}, f32[256]{0:T(256)S(1)}, u32[]{:S(2)}) copy-start(f32[256]{0:T(256)S(1)} %mul.1872) | copy-start | bytes 3076
  70.8 242.5 %copy-start.190 = (f32[256]{0:T(256)}, f32[256]{0:T(256)S(1)}, u32[]{:S(2)}) copy-start(f32[256]{0:T(256)S(1)} %mul.1869) | copy-start | bytes 3076
  70.8 242.5 %copy-start.192 = (f32[256]{0:T(256)}, f32[256]{0:T(256)S(1)}, u32[]{:S(2)}) copy-start(f32[256]{0:T(256)S(1)} %mul.1866) | copy-start | bytes 3076
  70.9 242.4 %copy-start.206 = (f32[256]{0:T(256)}, f32[256]{0:T(256)S(1)}, u32[]{:S(2)}) copy-start(f32[256]{0:T(256)S(1)} %mul.1863) | copy-start | bytes 3076
  72.4 241.0 %copy-start.214 = (f32[256]{0:T(256)}, f32[256]{0:T(256)S(1)}, u32[]{:S(2)}) copy-start(f32[256]{0:T(256)S(1)} %mul.1944) | copy-start | bytes 3076
  72.4 240.9 %copy-start.216 = (f32[256]{0:T(256)}, f32[256]{0:T(256)S(1)}, u32[]{:S(2)}) copy-start(f32[256]{0:T(256)S(1)} %mul.1941) | copy-start | bytes 3076
  72.5 240.8 %copy-start.218 = (f32[256]{0:T(256)}, f32[256]{0:T(256)S(1)}, u32[]{:S(2)}) copy-start(f32[256]{0:T(256)S(1)} %mul.1938) | copy-start | bytes 3076
  72.6 240.7 %copy-start.220 = (f32[256]{0:T(256)}, f32[256]{0:T(256)S(1)}, u32[]{:S(2)}) copy-start(f32[256]{0:T(256)S(1)} %mul.1935) | copy-start | bytes 3076
  72.7 240.7 %copy-start.222 = (f32[256]{0:T(256)}, f32[256]{0:T(256)S(1)}, u32[]{:S(2)}) copy-start(f32[256]{0:T(256)S(1)} %mul.1932) | copy-start | bytes 3076
  72.8 240.6 %copy-start.224 = (f32[256]{0:T(256)}, f32[256]{0:T(256)S(1)}, u32[]{:S(2)}) copy-start(f32[256]{0:T(256)S(1)} %mul.1929) | copy-start | bytes 3076
  72.9 240.5 %copy-start.226 = (f32[256]{0:T(256)}, f32[256]{0:T(256)S(1)}, u32[]{:S(2)}) copy-start(f32[256]{0:T(256)S(1)} %mul.1926) | copy-start | bytes 3076
  72.9 240.4 %copy-start.228 = (f32[256]{0:T(256)}, f32[256]{0:T(256)S(1)}, u32[]{:S(2)}) copy-start(f32[256]{0:T(256)S(1)} %mul.1923) | copy-start | bytes 3076
  109.6 341.8 %copy-start.40 = (bf16[2,256,512]{1,2,0:T(8,128)(2,1)}, bf16[2,256,512]{1,2,0:T(8,128)(2,1)S(1)}, u32[]{:S(2)}) copy-start(bf16[2,256,512]{1,2,0:T(8,128)(2,1)S(1)} %all_gather.38) | copy-start | bytes 1572868
  455.4 111.6 %all-gather.18.cloned.1.call-start = ((), (), s32[]{:S(2)}) async-start(), calls=%async_computation.12 | async-start | bytes 2228224 | tf_op jit(solution)/shard_map/all_gather | solution.py:242
  457.0 180.8 %all-gather.16.cloned.1.call-start = ((), (), s32[]{:S(2)}) async-start(), calls=%async_computation.11 | async-start | bytes 8060928 | tf_op jit(solution)/shard_map/all_gather | solution.py:279
  531.7 160.2 %all-gather.20.cloned.1.call-start = ((), (), s32[]{:S(2)}) async-start(), calls=%async_computation.13 | async-start | bytes 2228224 | tf_op jit(solution)/shard_map/all_gather | solution.py:243
  532.4 237.1 %reduce-scatter.11.cloned.1.call-start = ((), (), s32[]{:S(2)}) async-start(), calls=%async_computation.14 | async-start | bytes 8060928 | tf_op jit(solution)/shard_map/reduce_scatter | solution.py:282
  702.3 201.5 %all-gather.22.cloned.1.call-start = ((), (), s32[]{:S(2)}) async-start(), calls=%async_computation.15 | async-start | bytes 8060928 | tf_op jit(solution)/shard_map/all_gather | solution.py:260
  833.6 453.3 %reduce-scatter.13.cloned.1.call-start = ((), (), s32[]{:S(2)}) async-start(), calls=%async_computation.16 | async-start | bytes 8060928 | tf_op jit(solution)/shard_map/reduce_scatter | solution.py:269
  833.8 240.8 %copy-start.254 = (f32[256]{0:T(256)}, f32[256]{0:T(256)S(1)}, u32[]{:S(2)}) copy-start(f32[256]{0:T(256)S(1)} %mul.4016) | copy-start | bytes 3076
  833.8 240.7 %copy-start.236 = (f32[256]{0:T(256)}, f32[256]{0:T(256)S(1)}, u32[]{:S(2)}) copy-start(f32[256]{0:T(256)S(1)} %mul.4046) | copy-start | bytes 3076
  833.9 240.7 %copy-start.238 = (f32[256]{0:T(256)}, f32[256]{0:T(256)S(1)}, u32[]{:S(2)}) copy-start(f32[256]{0:T(256)S(1)} %mul.4043) | copy-start | bytes 3076
  834.0 240.6 %copy-start.240 = (f32[256]{0:T(256)}, f32[256]{0:T(256)S(1)}, u32[]{:S(2)}) copy-start(f32[256]{0:T(256)S(1)} %mul.4040) | copy-start | bytes 3076
  834.1 240.5 %copy-start.242 = (f32[256]{0:T(256)}, f32[256]{0:T(256)S(1)}, u32[]{:S(2)}) copy-start(f32[256]{0:T(256)S(1)} %mul.4037) | copy-start | bytes 3076
  1219.6 146.5 %all-gather.24.cloned.1.call-start = ((), (), s32[]{:S(2)}) async-start(), calls=%async_computation.17 | async-start | bytes 8060928 | tf_op jit(solution)/shard_map/all_gather | solution.py:279
  1295.9 141.9 %all-gather.26.cloned.1.call-start = ((), (), s32[]{:S(2)}) async-start(), calls=%async_computation.19 | async-start | bytes 8060928 | tf_op jit(solution)/shard_map/all_gather | solution.py:326
  1301.5 239.0 %reduce-scatter.17.cloned.1.call-start = ((), (), s32[]{:S(2)}) async-start(), calls=%async_computation.20 | async-start | bytes 8060928 | tf_op jit(solution)/shard_map/reduce_scatter | solution.py:330
  1473.3 136.7 %reduce-scatter.15.cloned.1.call-start = ((), (), s32[]{:S(2)}) async-start(), calls=%async_computation.18 | async-start | bytes 8060928 | tf_op jit(solution)/shard_map/reduce_scatter | solution.py:282
  1486.9 206.9 %all-gather.28.cloned.1.call-start = ((), (), s32[]{:S(2)}) async-start(), calls=%async_computation.21 | async-start | bytes 8060928 | tf_op jit(solution)/shard_map/all_gather | solution.py:339
  1623.6 551.5 %reduce-scatter.19.cloned.1.call-start = ((), (), s32[]{:S(2)}) async-start(), calls=%async_computation.22 | async-start | bytes 8060928 | tf_op jit(solution)/shard_map/reduce_scatter | solution.py:351
  2107.8 230.8 %all-gather.30.cloned.1.call-start = ((), (), s32[]{:S(2)}) async-start(), calls=%async_computation.23 | async-start | bytes 8060928 | tf_op jit(solution)/shard_map/all_gather | solution.py:326
  2268.4 185.3 %reduce-scatter.21.cloned.1.call-start = ((), (), s32[]{:S(2)}) async-start(), calls=%async_computation.24 | async-start | bytes 8060928 | tf_op jit(solution)/shard_map/reduce_scatter | solution.py:330
  2372.1 168.3 %all-gather.32.cloned.1.call-start = ((), (), s32[]{:S(2)}) async-start(), calls=%async_computation.25 | async-start | bytes 8060928 | tf_op jit(solution)/shard_map/all_gather | solution.py:339
  2470.2 547.5 %all-reduce.260.cloned.1.call-start = ((), (), s32[]{:S(2)}) async-start(), calls=%async_computation.27 | async-start | bytes 200704 | tf_op jit(solution)/shard_map/psum | solution.py:386
  2806.1 355.8 %all-reduce.262.cloned.1.call-start = ((), (), s32[]{:S(2)}) async-start(), calls=%async_computation.28 | async-start | bytes 12783616 | tf_op jit(solution)/shard_map/psum | solution.py:389
  3018.5 425.2 %reduce-scatter.23.cloned.1.call-start = ((), (), s32[]{:S(2)}) async-start(), calls=%async_computation.26 | async-start | bytes 8060928 | tf_op jit(solution)/shard_map/reduce_scatter | solution.py:351
  (373 other events, 16530.9 us)
Sparse Core Ops, SparseCore 0:
  10.9 42.3 all-gather.13
  68.1 72.7 all-gather.11
  455.5 67.0 reduce-scatter.8
  525.5 41.4 all-gather.17
  569.0 68.8 all-gather.15
  640.7 41.3 all-gather.19
  702.4 67.0 reduce-scatter.10
  833.7 70.0 all-gather.21
  1219.7 67.0 reduce-scatter.12
  1296.0 70.0 all-gather.23
  1367.7 70.0 all-gather.25
  1473.4 67.0 reduce-scatter.16
  1542.8 67.0 reduce-scatter.14
  1623.7 70.0 all-gather.27
  2107.9 67.0 reduce-scatter.18
  2268.5 70.0 all-gather.29
  2372.3 67.0 reduce-scatter.20
  2470.4 70.0 all-gather.31
  2806.3 20.4 all-reduce.259
  3018.6 143.3 all-reduce.261
  3164.3 66.8 reduce-scatter.22
where the time goes:
time: 3650 us; the launch traced here: 3630 us
  other arithmetic  1160 us (32%)
  waiting for transfers between devices  958 us (26%)
  matrix products  739 us (20%)
  local copies, waits for them, and re-layouts  659 us (18%)
  blocking collectives  91.9 us (3%)
    mul x8, other arithmetic, depthwise(): padded[:, row_at:row_at + 9, col_at:col_at + 9, :]  209 us
    reduce_sum x9, other arithmetic, depthwise(): padded[:, row_at:row_at + 9, col_at:col_at + 9, :]  206 us
    add_any x4, other arithmetic, depthwise(): padded[:, row_at:row_at + 9, col_at:col_at + 9, :]  199 us
    mul x2, other arithmetic, factor_attention(): depthwise(grid_cells, kernel.reshape(49, head_count * head_dim), 7)  144 us
    reshape x4, local copies, waits for them, and re-layouts, attend(): packed_rows.reshape(images, total_rows // images, head_count, 3, head_dim)  142 us
    all_gather x2, waiting for transfers between devices, on_device(): mid_rows = lax.all_gather(normed_mid, 'blk', axis=0, tiled=True)  135 us
    reduce_scatter x2, waiting for transfers between devices, on_device(): lax.psum_scatter(row_product(mixed_heads, w_proj).astype(jnp.bfloat16), '...  133 us
    reduce_scatter x2, waiting for transfers between devices, on_device(): lax.psum_scatter(row_product(active, w_down).astype(jnp.bfloat16), 'blk',...  131 us
  transfers between devices with their start and end apart: 21, of which 16 were waited for; matrix products, arithmetic and copies ran while one was open for 23% of the time, Pallas kernels for 0%

commit v1 on v0

v1 whole, which is shorter than its diff:
```python
import math

import jax
import jax.numpy as jnp
from jax import lax
from jax.experimental import pallas as pl
from jax.experimental.pallas import tpu as pltpu
from jax.sharding import PartitionSpec as P

HEADS = 8
GROUPS = 8
SLOT = 82
SIDE = 9
LANES = 128
IMGS = 8
ROWS = SLOT * IMGS
SCHULZ_COEFFS = (3.4445, -4.775, 2.0315)
MUON_RATES = (0.8, 0.8, 0.8, 0.4)
SMALL_RATES = (0.3, 0.3, 0.15)
VMEM_BYTES = 60 * 1024 * 1024
F32 = jnp.float32
BF16 = jnp.bfloat16


def mm(a, b):
    return jnp.dot(a, b, preferred_element_type=F32)


def mm_nt(a, b):
    return lax.dot_general(a, b, (((1,), (1,)), ((), ())), preferred_element_type=F32)


def mm_tn(a, b):
    return lax.dot_general(a, b, (((0,), (0,)), ((), ())), preferred_element_type=F32)


def tap_mask(head_ids):
    radius = jnp.where(head_ids < 2, 1, jnp.where(head_ids < 5, 2, 3))
    offsets = jnp.abs(jnp.arange(7, dtype=jnp.int32) - 3)
    within = (offsets[:, None] <= radius[None, :]).astype(F32)
    return (within[:, None, :] * within[None, :, :]).reshape(49, head_ids.shape[0])


def tile_radius(lane_at, head_dim):
    last = ((lane_at + 1) * LANES - 1) // head_dim
    return 1 if last < 2 else (2 if last < 5 else 3)


def normalize(values):
    center = values - jnp.mean(values, axis=-1, keepdims=True)
    spread = jnp.mean(center * center, axis=-1, keepdims=True)
    inv = lax.rsqrt(spread + 1e-06)
    return center * inv, inv


def norm_back(grad, unit, inv, gain):
    scaled = grad * gain
    first = jnp.mean(scaled, axis=-1, keepdims=True)
    second = jnp.mean(scaled * unit, axis=-1, keepdims=True)
    return inv * (scaled - first - unit * second)


def lane(at):
    return slice(at * LANES, (at + 1) * LANES)


def grid_rows(row_at):
    return pl.ds(pl.multiple_of((1 + SIDE * row_at) * IMGS, IMGS), SIDE * IMGS)


def conv_row(padded_ref, kernel_ref, cols, row_at, pad, reach, width, flip):
    mid = width // 2
    acc = [None] * SIDE
    for down in range(-reach, reach + 1):
        line = padded_ref[row_at + pad + down]
        for along in range(-reach, reach + 1):
            tap = (mid - down, mid - along) if flip else (mid + down, mid + along)
            weight = kernel_ref[pl.ds(tap[0] * width + tap[1], 1), cols]
            weight = jnp.broadcast_to(weight, (IMGS, LANES))
            for col in range(SIDE):
                if 0 <= col + along < SIDE:
                    term = line[col + along] * weight
                    acc[col] = term if acc[col] is None else acc[col] + term
    return jnp.concatenate(acc, axis=0)


def conv_kernel_grad(grad_ref, padded_ref, total_ref, cols, pad, reach, width, grad_pad):
    mid = width // 2

    def one(step, carry):
        down = step - reach
        acc = [None] * (2 * reach + 1)
        for row_at in range(SIDE):
            grad_line = grad_ref[row_at + grad_pad]
            line = padded_ref[row_at + pad + down]
            for along in range(-reach, reach + 1):
                for col in range(SIDE):
                    if 0 <= col + along < SIDE:
                        term = grad_line[col] * line[col + along]
                        at = along + reach
                        acc[at] = term if acc[at] is None else acc[at] + term
        for along in range(-reach, reach + 1):
            total_ref[(mid + down) * width + mid + along, :, cols] += acc[along + reach]
        return carry

    lax.fori_loop(0, 2 * reach + 1, one, 0)


def key_softmax(key_tile, mask_tile):
    keys = key_tile.reshape(SLOT, IMGS, LANES)
    live = mask_tile.reshape(SLOT, IMGS, LANES)
    top = jnp.max(jnp.where(live > 0, keys, -1e30), axis=0, keepdims=True)
    raw = jnp.exp(jnp.where(live > 0, keys - top, -60.0)) * live
    return (raw / jnp.sum(raw, axis=0, keepdims=True)).reshape(ROWS, LANES)


def head_mask(size, head_dim):
    down = lax.broadcasted_iota(jnp.int32, (size, size), 0) // head_dim
    along = lax.broadcasted_iota(jnp.int32, (size, size), 1) // head_dim
    return jnp.where(down == along, F32(head_dim ** -0.5), F32(0.0))


def image_rows(ref, quad, image):
    rows = pl.ds(image, SLOT, stride=IMGS)
    return jnp.concatenate([ref[2 * quad, rows, :], ref[2 * quad + 1, rows, :]], axis=1)


def put_image_rows(ref, quad, image, values):
    rows = pl.ds(image, SLOT, stride=IMGS)
    ref[2 * quad, rows, :] = values[:, :LANES]
    ref[2 * quad + 1, rows, :] = values[:, LANES:]


def attend_forward(
    x_ref, mask_ref, qkv_ref, proj_ref, norm_ref, cpe_ref, crpe_ref,
    conv_ref, packed_ref, rel_ref, mixed_ref, att_ref,
    x_pad, v_pad, q_s, k_s, v_s, f_s, c_s,
):
    channels = x_ref.shape[1]
    tiles = channels // LANES
    head_dim = channels // HEADS

    @pl.when(pl.program_id(0) == 0)
    def _():
        x_pad[...] = jnp.zeros_like(x_pad)
        v_pad[...] = jnp.zeros_like(v_pad)

    mask = mask_ref[...]
    for at in range(tiles):
        cols = lane(at)
        masked = x_ref[:, cols] * mask
        x_pad[1 : 1 + SIDE] = masked[IMGS:].reshape(SIDE, SIDE, IMGS, LANES)
        conv_ref[:IMGS, cols] = x_ref[:IMGS, cols]

        def conv_step(row_at, carry):
            rows = grid_rows(row_at)
            out = conv_row(x_pad, cpe_ref, cols, row_at, 1, 1, 3, False)
            conv_ref[rows, cols] = x_ref[rows, cols] + out * mask_ref[rows, :]
            return carry

        lax.fori_loop(0, SIDE, conv_step, 0)
    unit, _ = normalize(conv_ref[...])
    normed = (unit * norm_ref[0:1, :] + norm_ref[1:2, :]).astype(BF16)
    for third, keep in enumerate((q_s, k_s, v_s)):
        part = mm(normed, qkv_ref[:, third * channels : (third + 1) * channels]).astype(BF16)
        packed_ref[:, third * channels : (third + 1) * channels] = part
        part = part.astype(F32)
        for at in range(tiles):
            keep[at] = part[:, lane(at)]
    for at in range(tiles):
        k_s[at] = key_softmax(k_s[at], mask_ref[...])
    block = head_mask(2 * LANES, head_dim)

    def one_image(image, carry):
        for quad in range(tiles // 2):
            keys = image_rows(k_s, quad, image).astype(BF16)
            values = image_rows(v_s, quad, image).astype(BF16)
            query = image_rows(q_s, quad, image).astype(BF16)
            context = (mm_tn(keys, values) * block).astype(BF16)
            put_image_rows(f_s, quad, image, mm(query, context))
        return carry

    lax.fori_loop(0, IMGS, one_image, 0)
    for at in range(tiles):
        cols = lane(at)
        masked = v_s[at] * mask_ref[...]
        v_pad[3 : 3 + SIDE] = masked[IMGS:].reshape(SIDE, SIDE, IMGS, LANES)
        c_s[:IMGS, :] = jnp.zeros((IMGS, LANES), F32)
        reach = tile_radius(at, head_dim)

        def rel_step(row_at, carry):
            rows = grid_rows(row_at)
            out = conv_row(v_pad, crpe_ref, cols, row_at, 3, reach, 7, False)
            c_s[rows, :] = out * mask_ref[rows, :]
            return carry

        lax.fori_loop(0, SIDE, rel_step, 0)
        rel = c_s[...]
        rel_ref[:, cols] = rel.astype(BF16)
        mixed_ref[:, cols] = (f_s[at] + q_s[at] * rel).astype(BF16)
    att_ref[...] = conv_ref[...] + mm_nt(mixed_ref[...], proj_ref[...])


def gelu_parts(values):
    size = jnp.abs(values)
    t = 1.0 / (1.0 + (0.3275911 * 0.7071067811865476) * size)
    bell = jnp.exp(-0.5 * values * values)
    poly = 0.5 * 1.061405429
    for coef in (-1.453152027, 1.421413741, -0.284496736, 0.254829592):
        poly = poly * t + 0.5 * coef
    tail = poly * t * bell
    phi = jnp.where(values >= 0, 1.0 - tail, tail)
    return values * phi, phi + (values * 0.3989422804014327) * bell


def feed_forward(att_ref, up_down_ref, norm_ref, out_ref, act_ref, slope_ref, chunk):
    blks, _, both = up_down_ref.shape
    width = both // 2
    att = att_ref[...]
    unit, _ = normalize(att)
    normed = (unit * norm_ref[2:3, :] + norm_ref[3:4, :]).astype(BF16)
    total = att
    for blk in range(blks):
        for at in range(0, width, chunk):
            hidden = mm(normed, up_down_ref[blk, :, at : at + chunk])
            active, slope = gelu_parts(hidden)
            active = active.astype(BF16)
            cols = slice(blk * width + at, blk * width + at + chunk)
            act_ref[:, cols] = active
            slope_ref[:, cols] = slope.astype(BF16)
            total = total + mm_nt(active, up_down_ref[blk, :, width + at : width + at + chunk])
    out_ref[...] = total.astype(out_ref.dtype)


def feed_back(
    up_ref, att_ref, act_ref, slope_ref, up_down_ref, norm_ref,
    gatt_ref, gweight_ref, gnorm_ref, total_s, chunk,
):
    step, steps = pl.program_id(0), pl.num_programs(0)
    blks, _, both = up_down_ref.shape
    width = both // 2

    @pl.when(step == 0)
    def _():
        total_s[...] = jnp.zeros_like(total_s)
        gnorm_ref[...] = jnp.zeros_like(gnorm_ref)

    upstream = up_ref[...]
    unit, inv = normalize(att_ref[...])
    gain = norm_ref[2:3, :]
    normed_t = (unit * gain + norm_ref[3:4, :]).astype(BF16).T
    down_in = upstream.astype(BF16)
    down_t = down_in.T
    grad_mid = None
    for blk in range(blks):
        for at in range(0, width, chunk):
            cols = slice(blk * width + at, blk * width + at + chunk)
            ups = slice(at, at + chunk)
            downs = slice(width + at, width + at + chunk)
            grad_active = mm(down_in, up_down_ref[blk, :, downs])
            grad_hidden = (grad_active * slope_ref[:, cols].astype(F32)).astype(BF16)
            total_s[blk, :, ups] += mm(normed_t, grad_hidden)
            total_s[blk, :, downs] += mm(down_t, act_ref[:, cols])
            part = mm_nt(grad_hidden, up_down_ref[blk, :, ups])
            grad_mid = part if grad_mid is None else grad_mid + part
    gatt_ref[...] = upstream + norm_back(grad_mid, unit, inv, gain)
    gnorm_ref[0:1, :] += jnp.sum(grad_mid * unit, axis=0, keepdims=True)
    gnorm_ref[1:2, :] += jnp.sum(grad_mid, axis=0, keepdims=True)

    @pl.when(step == steps - 1)
    def _():
        gweight_ref[...] = total_s[...].astype(BF16)


def attend_back(
    gatt_ref, x_ref, conv_ref, packed_ref, rel_ref, mixed_ref, mask_ref,
    qkv_ref, proj_ref, norm_ref, cpe_ref, crpe_ref,
    up_ref, gqkv_ref, gproj_ref, gnorm_ref, gcpe_ref, gcrpe_ref,
    qkv_s, proj_s, x_pad, g_pad, v_pad, c_pad, q_s, k_s, v_s, f_s, dq_s, dk_s, dv_s, c_s, gp_s,
):
    channels = x_ref.shape[1]
    tiles = channels // LANES
    head_dim = channels // HEADS
    step, steps = pl.program_id(0), pl.num_programs(0)

    @pl.when(step == 0)
    def _():
        for ref in (x_pad, g_pad, v_pad, c_pad, qkv_s, proj_s, gnorm_ref, gcpe_ref, gcrpe_ref):
            ref[...] = jnp.zeros_like(ref)

    att_in = gatt_ref[...].astype(BF16)
    proj_s[...] += mm(att_in.T, mixed_ref[...])
    grad_mixed = mm(att_in, proj_ref[...])
    for at in range(tiles):
        f_s[at] = grad_mixed[:, lane(at)]
    for third, keep in enumerate((q_s, k_s, v_s)):
        for at in range(tiles):
            cols = slice(third * channels + at * LANES, third * channels + (at + 1) * LANES)
            keep[at] = packed_ref[:, cols].astype(F32)
    for at in range(tiles):
        k_s[at] = key_softmax(k_s[at], mask_ref[...])
    block = head_mask(2 * LANES, head_dim)

    def one_image(image, carry):
        for quad in range(tiles // 2):
            keys = image_rows(k_s, quad, image).astype(BF16)
            values = image_rows(v_s, quad, image).astype(BF16)
            query = image_rows(q_s, quad, image).astype(BF16)
            grads = image_rows(f_s, quad, image).astype(BF16)
            context = (mm_tn(keys, values) * block).astype(BF16)
            grad_context = (mm_tn(query, grads) * block).astype(BF16)
            put_image_rows(dq_s, quad, image, mm_nt(grads, context))
            put_image_rows(dk_s, quad, image, mm_nt(values, grad_context))
            put_image_rows(dv_s, quad, image, mm(keys, grad_context))
        return carry

    lax.fori_loop(0, IMGS, one_image, 0)
    for at in range(tiles):
        cols = lane(at)
        mask = mask_ref[...]
        weights = k_s[at]
        share = weights * dk_s[at]
        total = jnp.sum(share.reshape(SLOT, IMGS, LANES), axis=0, keepdims=True)
        back = share.reshape(SLOT, IMGS, LANES) - weights.reshape(SLOT, IMGS, LANES) * total
        gp_s[:, channels + at * LANES : channels + (at + 1) * LANES] = back.reshape(
            ROWS, LANES
        ).astype(BF16)
        grads = f_s[at]
        gp_s[:, cols] = (dq_s[at] + grads * rel_ref[:, cols].astype(F32)).astype(BF16)
        reach = tile_radius(at, head_dim)
        masked = v_s[at] * mask
        v_pad[3 : 3 + SIDE] = masked[IMGS:].reshape(SIDE, SIDE, IMGS, LANES)
        cgrad = grads * q_s[at] * mask
        c_pad[3 : 3 + SIDE] = cgrad[IMGS:].reshape(SIDE, SIDE, IMGS, LANES)
        c_s[:IMGS, :] = dv_s[at, :IMGS, :]

        def rel_step(row_at, carry):
            rows = grid_rows(row_at)
            out = conv_row(c_pad, crpe_ref, cols, row_at, 3, reach, 7, True)
            c_s[rows, :] = dv_s[at, rows, :] + out * mask_ref[rows, :]
            return carry

        lax.fori_loop(0, SIDE, rel_step, 0)
        conv_kernel_grad(c_pad, v_pad, gcrpe_ref, cols, 3, reach, 7, 3)
        gp_s[:, 2 * channels + at * LANES : 2 * channels + (at + 1) * LANES] = c_s[...].astype(BF16)
    unit, inv = normalize(conv_ref[...])
    gain = norm_ref[0:1, :]
    normed_t = (unit * gain + norm_ref[1:2, :]).astype(BF16).T
    grad_rows = None
    for third in range(3):
        cols = slice(third * channels, (third + 1) * channels)
        part_in = gp_s[:, cols]
        qkv_s[:, cols] += mm(normed_t, part_in)
        part = mm_nt(part_in, qkv_ref[:, cols])
        grad_rows = part if grad_rows is None else grad_rows + part
    gnorm_ref[0:1, :] += jnp.sum(grad_rows * unit, axis=0, keepdims=True)
    gnorm_ref[1:2, :] += jnp.sum(grad_rows, axis=0, keepdims=True)
    up_ref[...] = gatt_ref[...] + norm_back(grad_rows, unit, inv, gain)
    for at in range(tiles):
        cols = lane(at)
        mask = mask_ref[...]
        masked = x_ref[:, cols] * mask
        x_pad[1 : 1 + SIDE] = masked[IMGS:].reshape(SIDE, SIDE, IMGS, LANES)
        gmasked = up_ref[:, cols] * mask
        g_pad[1 : 1 + SIDE] = gmasked[IMGS:].reshape(SIDE, SIDE, IMGS, LANES)

        def conv_step(row_at, carry):
            rows = grid_rows(row_at)
            out = conv_row(g_pad, cpe_ref, cols, row_at, 1, 1, 3, True)
            up_ref[rows, cols] += out * mask_ref[rows, :]
            return carry

        lax.fori_loop(0, SIDE, conv_step, 0)
        conv_kernel_grad(g_pad, x_pad, gcpe_ref, cols, 1, 1, 3, 1)

    @pl.when(step == steps - 1)
    def _():
        gqkv_ref[...] = qkv_s[...].astype(BF16)
        gproj_ref[...] = proj_s[...].astype(BF16)


def schulz(fresh_ref, out_ref, width):
    def dot3(a, b, dims):
        a_hi = a.astype(BF16)
        b_hi = b.astype(BF16)
        a_lo = (a - a_hi.astype(F32)).astype(BF16)
        b_lo = (b - b_hi.astype(F32)).astype(BF16)
        one = lambda u, v: lax.dot_general(u, v, (dims, ((), ())), preferred_element_type=F32)
        return one(a_hi, b_hi) + (one(a_hi, b_lo) + one(a_lo, b_hi))

    first, second, third = SCHULZ_COEFFS
    parts = range(0, fresh_ref.shape[2], width)
    current = []
    for at in parts:
        value = fresh_ref[0, :, at : at + width].astype(F32)
        level = jnp.sum(jnp.sum(value * value, axis=0, keepdims=True), axis=1, keepdims=True)
        current.append(value / (jnp.sqrt(level) + 1e-07))
    for _ in range(5):
        for at, value in enumerate(current):
            gram = dot3(value, value, ((0,), (0,)))
            poly = second * gram + third * dot3(gram, gram, ((1,), (0,)))
            current[at] = first * value + dot3(value, poly, ((1,), (0,)))
    for at, value in zip(parts, current):
        out_ref[0, :, at : at + width] = value.astype(BF16)


def params_for(**more):
    return pltpu.CompilerParams(vmem_limit_bytes=VMEM_BYTES, **more)


def block_of(cols):
    return pl.BlockSpec((ROWS, cols), lambda g: (g, 0))


def whole(array):
    shape = array.shape
    return pl.BlockSpec(shape, lambda g: (0,) * len(shape), pipeline_mode=pl.Buffered(1))


def whole_out(shape):
    return pl.BlockSpec(shape, lambda g: (0,) * len(shape))


def run_attend_forward(x, mask, qkv, proj, norm, cpe, crpe):
    count, channels = x.shape
    tiles = channels // LANES
    flat = pltpu.VMEM((tiles, ROWS, LANES), F32)
    return pl.pallas_call(
        attend_forward,
        grid=(count // ROWS,),
        in_specs=[block_of(channels), block_of(LANES)]
        + [whole(a) for a in (qkv, proj, norm, cpe, crpe)],
        out_specs=[block_of(channels), block_of(3 * channels)] + [block_of(channels)] * 3,
        out_shape=[
            jax.ShapeDtypeStruct((count, channels), F32),
            jax.ShapeDtypeStruct((count, 3 * channels), BF16),
            jax.ShapeDtypeStruct((count, channels), BF16),
            jax.ShapeDtypeStruct((count, channels), BF16),
            jax.ShapeDtypeStruct((count, channels), F32),
        ],
        scratch_shapes=[
            pltpu.VMEM((SIDE + 2, SIDE, IMGS, LANES), F32),
            pltpu.VMEM((SIDE + 6, SIDE, IMGS, LANES), F32),
            flat, flat, flat, flat,
            pltpu.VMEM((ROWS, LANES), F32),
        ],
        compiler_params=params_for(),
        name="attend_forward",
    )(x, mask, qkv, proj, norm, cpe, crpe)


def run_feed_forward(att, up_down, norm, out_type, chunk=256):
    count, channels = att.shape
    hidden = up_down.shape[0] * up_down.shape[2] // 2
    return pl.pallas_call(
        lambda *refs: feed_forward(*refs, chunk=chunk),
        grid=(count // ROWS,),
        in_specs=[block_of(channels), whole(up_down), whole(norm)],
        out_specs=[block_of(channels), block_of(hidden), block_of(hidden)],
        out_shape=[
            jax.ShapeDtypeStruct((count, channels), out_type),
            jax.ShapeDtypeStruct((count, hidden), BF16),
            jax.ShapeDtypeStruct((count, hidden), BF16),
        ],
        compiler_params=params_for(),
        name="feed_forward",
    )(att, up_down, norm)


def run_feed_back(upstream, att, active, slope, up_down, norm, chunk=256):
    count, channels = att.shape
    hidden = active.shape[1]
    return pl.pallas_call(
        lambda *refs: feed_back(*refs, chunk=chunk),
        grid=(count // ROWS,),
        in_specs=[block_of(channels), block_of(channels), block_of(hidden), block_of(hidden)]
        + [whole(up_down), whole(norm)],
        out_specs=[block_of(channels), whole_out(up_down.shape), whole_out((2, channels))],
        out_shape=[
            jax.ShapeDtypeStruct((count, channels), F32),
            jax.ShapeDtypeStruct(up_down.shape, BF16),
            jax.ShapeDtypeStruct((2, channels), F32),
        ],
        scratch_shapes=[pltpu.VMEM(up_down.shape, F32)],
        compiler_params=params_for(),
        name="feed_back",
    )(upstream, att, active, slope, up_down, norm)


def run_attend_back(gatt, x, conv, packed, rel, mixed, mask, qkv, proj, norm, cpe, crpe):
    count, channels = x.shape
    tiles = channels // LANES
    flat = pltpu.VMEM((tiles, ROWS, LANES), F32)
    three = pltpu.VMEM((SIDE + 2, SIDE, IMGS, LANES), F32)
    seven = pltpu.VMEM((SIDE + 6, SIDE, IMGS, LANES), F32)
    small = [(2, channels), (9, IMGS, channels), (49, IMGS, channels)]
    return pl.pallas_call(
        attend_back,
        grid=(count // ROWS,),
        in_specs=[block_of(channels)] * 3
        + [block_of(3 * channels), block_of(channels), block_of(channels), block_of(LANES)]
        + [whole(a) for a in (qkv, proj, norm, cpe, crpe)],
        out_specs=[block_of(channels), whole_out(qkv.shape), whole_out(proj.shape)]
        + [whole_out(shape) for shape in small],
        out_shape=[
            jax.ShapeDtypeStruct((count, channels), F32),
            jax.ShapeDtypeStruct(qkv.shape, BF16),
            jax.ShapeDtypeStruct(proj.shape, BF16),
        ]
        + [jax.ShapeDtypeStruct(shape, F32) for shape in small],
        scratch_shapes=[
            pltpu.VMEM(qkv.shape, F32),
            pltpu.VMEM(proj.shape, F32),
            three, three, seven, seven,
            flat, flat, flat, flat, flat, flat, flat,
            pltpu.VMEM((ROWS, LANES), F32),
            pltpu.VMEM((ROWS, 3 * channels), BF16),
        ],
        compiler_params=params_for(),
        name="attend_back",
    )(gatt, x, conv, packed, rel, mixed, mask, qkv, proj, norm, cpe, crpe)


def run_schulz(fresh, width):
    units, height, both = fresh.shape
    spec = pl.BlockSpec((1, height, both), lambda g: (g, 0, 0))
    return pl.pallas_call(
        lambda *refs: schulz(*refs, width=width),
        grid=(units,),
        in_specs=[spec],
        out_specs=spec,
        out_shape=jax.ShapeDtypeStruct(fresh.shape, BF16),
        compiler_params=params_for(),
        name="schulz",
    )(fresh)


def token_major(rows):
    count, channels = rows.shape
    split = rows.reshape(count // ROWS, IMGS, SLOT, channels)
    return split.transpose(0, 2, 1, 3).reshape(count, channels)


def image_major(rows):
    count, channels = rows.shape
    split = rows.reshape(count // ROWS, SLOT, IMGS, channels)
    return split.transpose(0, 2, 1, 3).reshape(count, channels)


def key_masks(grid_class):
    extent = 5 + 2 * grid_class
    across = (jnp.arange(SIDE, dtype=jnp.int32)[None, :] < extent[:, None]).astype(F32)
    cells = (across[:, :, None] * across[:, None, :]).reshape(-1, SIDE * SIDE)
    return jnp.concatenate([jnp.ones((cells.shape[0], 1), F32), cells], axis=1)


def split_heads(shard, heads_own, head_dim):
    lead = shard.shape[:-1]
    parts = shard.reshape(lead + (heads_own, 3, head_dim))
    return jnp.swapaxes(parts, -3, -2).reshape(lead + (3 * heads_own * head_dim,))


def join_heads(shard, heads_own, head_dim):
    lead = shard.shape[:-1]
    parts = shard.reshape(lead + (3, heads_own, head_dim))
    return jnp.swapaxes(parts, -3, -2).reshape(lead + (3 * heads_own * head_dim,))


def block_scale(height, breadth):
    return math.sqrt(max(1.0, height / breadth))


def normalized_step(param_vals, moment, grads_in, rate, axes):
    fresh = 0.5 * moment + grads_in
    level = jnp.sqrt(jnp.mean(fresh * fresh, axis=axes, keepdims=True))
    return (fresh, param_vals - rate * fresh / (level + 1e-06))


def on_device(
    tokens, cotangent, grid_class,
    qkv_weight, proj_weight, up_weight, down_weight, norm_params, cpe_weight, crpe_weight,
    qkv_moment, proj_moment, up_moment, down_moment, norm_moment, cpe_moment, crpe_moment,
):
    own_count, channels = tokens.shape
    blk_count = lax.axis_size("blk")
    tok_count = lax.axis_size("tok")
    blk_at = lax.axis_index("blk")
    layers = qkv_weight.shape[0]
    images_own = grid_class.shape[0] // blk_count
    head_dim = channels // HEADS
    heads_own = HEADS // blk_count
    groups_own = GROUPS // blk_count
    group_width = up_weight.shape[2] // groups_own
    own_rows = qkv_weight.shape[1]
    both = ("blk", "tok")

    attn_shard = jnp.concatenate(
        [split_heads(qkv_weight, heads_own, head_dim), jnp.swapaxes(proj_weight, 1, 2)], axis=2
    )
    feed_shard = jnp.concatenate([up_weight, jnp.swapaxes(down_weight, 1, 2)], axis=2)
    qkv_all, proj_all, feed_all = [], [], []
    for layer in range(layers):
        attn = lax.all_gather(attn_shard[layer].astype(BF16), both, axis=0, tiled=True)
        attn = attn.reshape(blk_count, channels, 4, heads_own * head_dim)
        attn = attn.transpose(1, 2, 0, 3).reshape(channels, 4 * channels)
        qkv_all.append(attn[:, : 3 * channels])
        proj_all.append(attn[:, 3 * channels :])
        feed = lax.all_gather(feed_shard[layer].astype(BF16), both, axis=0, tiled=True)
        feed_all.append(feed.reshape(blk_count, channels, feed.shape[1]))

    own_class = lax.dynamic_slice_in_dim(grid_class, blk_at * images_own, images_own)
    keys = key_masks(own_class)
    mask = jnp.broadcast_to(
        token_major(keys.reshape(own_count, 1)), (own_count, LANES)
    )
    taps = jnp.repeat(tap_mask(jnp.arange(HEADS, dtype=jnp.int32)), head_dim, axis=1)

    stream = token_major(tokens).astype(F32)
    saved = []
    for layer in range(layers):
        crpe = crpe_weight[layer] * taps
        conv, packed, rel, mixed, att = run_attend_forward(
            stream, mask, qkv_all[layer], proj_all[layer], norm_params[layer],
            cpe_weight[layer], crpe,
        )
        last = layer == layers - 1
        out, active, slope = run_feed_forward(
            att, feed_all[layer], norm_params[layer], BF16 if last else F32
        )
        saved.append((stream, conv, packed, rel, mixed, att, active, slope, crpe))
        stream = out
    block_out = image_major(stream)

    upstream = token_major(cotangent * keys.reshape(own_count, 1))
    attn_sums, feed_sums = [None] * layers, [None] * layers
    small_rows = 4 + 9 + 49
    for layer in reversed(range(layers)):
        x, conv, packed, rel, mixed, att, active, slope, crpe = saved[layer]
        gatt, gfeed, gmid = run_feed_back(
            upstream, att, active, slope, feed_all[layer], norm_params[layer]
        )
        feed_sums[layer] = lax.psum_scatter(
            gfeed.reshape(blk_count * channels, gfeed.shape[2]), both,
            scatter_dimension=0, tiled=True,
        ).astype(F32)
        upstream, gqkv, gproj, gfront, gcpe, gcrpe = run_attend_back(
            gatt, x, conv, packed, rel, mixed, mask, qkv_all[layer], proj_all[layer],
            norm_params[layer], cpe_weight[layer], crpe,
        )
        small = jnp.concatenate([gfront, gmid, gcpe.sum(1), gcrpe.sum(1) * taps], axis=0)
        small = jnp.pad(small, ((0, LANES - small_rows), (0, 0))).T.astype(BF16)
        grads = jnp.concatenate([gqkv, gproj], axis=1)
        grads = grads.reshape(channels, 4, blk_count, heads_own * head_dim)
        grads = grads.transpose(2, 0, 1, 3).reshape(blk_count, channels, 4 * heads_own * head_dim)
        grads = jnp.concatenate(
            [grads, jnp.broadcast_to(small, (blk_count, channels, LANES))], axis=2
        )
        attn_sums[layer] = lax.psum_scatter(
            grads.reshape(blk_count * channels, grads.shape[2]), both,
            scatter_dimension=0, tiled=True,
        ).astype(F32)
    tokens_grad = image_major(upstream)

    attn_sum = jnp.stack(attn_sums)
    feed_sum = jnp.stack(feed_sums)
    small_sum = attn_sum[:, :, -LANES:][:, :, :small_rows]
    attn_sum = attn_sum[:, :, :-LANES]
    attn_moment = jnp.concatenate(
        [split_heads(qkv_moment, heads_own, head_dim), jnp.swapaxes(proj_moment, 1, 2)], axis=2
    )
    feed_moment = jnp.concatenate([up_moment, jnp.swapaxes(down_moment, 1, 2)], axis=2)
    attn_fresh = 0.5 * attn_moment + attn_sum
    feed_fresh = 0.5 * feed_moment + feed_sum

    units = layers * 2 * groups_own
    per_dev = -(-units // tok_count)
    big = feed_fresh.reshape(layers, own_rows, 2 * groups_own, group_width)
    big = big.transpose(0, 2, 1, 3).reshape(units, own_rows, group_width)
    heads = attn_fresh.reshape(layers, own_rows, 4, heads_own, head_dim).transpose(0, 3, 1, 2, 4)
    heads_qkv = heads[:, :, :, :3].reshape(layers, heads_own, own_rows, 3 * head_dim)
    heads_proj = heads[:, :, :, 3]
    widen = lambda v: jnp.pad(v, ((0, 0), (0, 0), (0, 0), (0, group_width - v.shape[3])))
    little = jnp.concatenate([widen(heads_qkv), widen(heads_proj)], axis=1)
    little = little.reshape(units, own_rows, group_width)
    send = jnp.concatenate([big, little], axis=2).astype(BF16)
    send = jnp.pad(send, ((0, per_dev * tok_count - units), (0, 0), (0, 0)))
    send = send.reshape(tok_count, per_dev, own_rows, 2 * group_width)
    got = lax.all_to_all(send, "tok", 0, 0, tiled=True)
    got = got.transpose(1, 0, 2, 3).reshape(per_dev, channels, 2 * group_width)
    ortho = run_schulz(got, group_width)
    ortho = ortho.reshape(per_dev, tok_count, own_rows, 2 * group_width).transpose(1, 0, 2, 3)
    ortho = lax.all_to_all(ortho, "tok", 0, 0, tiled=True)
    ortho = ortho.reshape(per_dev * tok_count, own_rows, 2 * group_width)[:units].astype(F32)
    big = ortho[:, :, :group_width].reshape(layers, 2, groups_own, own_rows, group_width)
    big = big.transpose(1, 0, 3, 2, 4).reshape(2, layers, own_rows, groups_own * group_width)
    little = ortho[:, :, group_width:].reshape(layers, 2, heads_own, own_rows, group_width)
    little_qkv = little[:, 0, :, :, : 3 * head_dim].transpose(0, 2, 1, 3)
    little_qkv = little_qkv.reshape(layers, own_rows, heads_own * 3 * head_dim)
    little_proj = little[:, 1, :, :, :head_dim].transpose(0, 1, 3, 2)
    little_proj = little_proj.reshape(layers, heads_own * head_dim, own_rows)

    qkv_fresh = join_heads(attn_fresh[:, :, : qkv_weight.shape[2]], heads_own, head_dim)
    proj_fresh = jnp.swapaxes(attn_fresh[:, :, qkv_weight.shape[2] :], 1, 2)
    up_fresh = feed_fresh[:, :, : up_weight.shape[2]]
    down_fresh = jnp.swapaxes(feed_fresh[:, :, up_weight.shape[2] :], 1, 2)
    scales = (
        block_scale(channels, 3 * head_dim),
        block_scale(head_dim, channels),
        block_scale(channels, group_width),
        block_scale(group_width, channels),
    )
    results = []
    for kind, (weight, fresh, turned) in enumerate(
        (
            (qkv_weight, qkv_fresh, little_qkv),
            (proj_weight, proj_fresh, little_proj),
            (up_weight, up_fresh, big[0]),
            (down_weight, down_fresh, jnp.swapaxes(big[1], 1, 2)),
        )
    ):
        new = weight - MUON_RATES[kind] * scales[kind] * turned
        results.extend([fresh, new, new.astype(BF16)])

    small_all = lax.all_gather(small_sum.astype(BF16), "tok", axis=1, tiled=True)
    small_all = jnp.swapaxes(small_all, 1, 2).astype(F32)
    norm_fresh, norm_new = normalized_step(
        norm_params, norm_moment, small_all[:, :4], SMALL_RATES[0], (2,)
    )
    cpe_fresh, cpe_new = normalized_step(
        cpe_weight, cpe_moment, small_all[:, 4:13], SMALL_RATES[1], (1, 2)
    )
    head_shape = (layers, 49, HEADS, head_dim)
    crpe_fresh, crpe_new = normalized_step(
        crpe_weight.reshape(head_shape),
        crpe_moment.reshape(head_shape),
        small_all[:, 13:].reshape(head_shape),
        SMALL_RATES[2],
        (1, 3),
    )
    return (
        (block_out, tokens_grad)
        + tuple(results)
        + (norm_fresh, norm_new, cpe_fresh, cpe_new)
        + (crpe_fresh.reshape(crpe_weight.shape), crpe_new.reshape(crpe_weight.shape))
    )


def solution(mesh):
    rows = P(("tok", "blk"), None)
    down_cols = P(None, "tok", "blk")
    cross = P(None, "blk", "tok")
    mats = (down_cols, cross, down_cols, cross)
    in_specs = (rows, rows, P("tok")) + mats + (P(),) * 3 + mats + (P(),) * 3
    out_specs = (rows, rows) + tuple(spec for spec in mats for _ in range(3)) + (P(),) * 6
    return jax.shard_map(
        on_device, mesh=mesh, in_specs=in_specs, out_specs=out_specs, check_vma=False
    )
```

time: 3650 us -> 1150 us (0.32)
  other arithmetic: 1160 us -> 24.7 us
  matrix products: 739 us -> 0 us
  local copies, waits for them, and re-layouts: 659 us -> 102 us
  Pallas kernels: 0 us -> 446 us
  waiting for transfers between devices: 958 us -> 522 us
  blocking collectives: 91.9 us -> 21.1 us
    dot_general x96 -> x0, matrix products: 739 us -> none  [the longest x2 109 us: on_device(): hidden = jnp.dot(mid_rows, w_up, preferred_element_type=jnp.float32)]
    mul x26 -> x6, other arithmetic: 487 us -> 6.13 us  [the longest x1 5.33 us: on_device(): upstream = token_major(cotangent * keys.reshape(own_count, 1))]
    pallas_call x0 -> x9, Pallas kernels: none -> 446 us  [the longest x2 184 us: run_attend_back(): pl.pallas_call(attend_back, grid=(count // ROWS,), in_specs=[block_of(cha...]
    all_gather x11 -> x4, waiting for transfers between devices: 449 us -> 68.7 us  [the longest x2 68.7 us: on_device(): lax.all_gather(attn_shard[layer].astype(BF16), both, axis=0, tiled=True)]
    reduce_sum x39 -> x4, other arithmetic: 328 us -> 2.6 us  [the longest x2 1.59 us: on_device(): gcrpe.sum(1) * taps]
    reshape x40 -> x21, local copies, waits for them, and re-layouts: 357 us -> 48.2 us  [the longest x2 11 us: image_major(): split = rows.reshape(count // ROWS, SLOT, IMGS, channels)]
    add_any x8 -> x0, other arithmetic: 224 us -> none  [the longest x4 199 us: depthwise(): padded[:, row_at:row_at + 9, col_at:col_at + 9, :]]
    psum x2 -> x0, waiting for transfers between devices: 125 us -> none  [the longest x1 125 us: on_device(): lax.psum(place_moment(stacked[0], qkv_moment, 1, tok_at).astype(jnp.bfloa...]
  transfers between devices with their start and end apart: 21 -> 10, of which waited for: 16 -> 8; matrix products, arithmetic and copies ran while one was open for 23% -> 9% of each run, Pallas kernels for 0% -> 12%
where the time goes in v1:
time: 1150 us; the launch traced here: 1140 us
  waiting for transfers between devices  522 us (45%)
  Pallas kernels  446 us (39%)
  local copies, waits for them, and re-layouts  102 us (9%)
  other arithmetic  24.7 us (2%)
  blocking collectives  21.1 us (2%)
  between operations  15.5 us (1%)
    reduce_scatter x2, waiting for transfers between devices, on_device(): lax.psum_scatter(gfeed.reshape(blk_count * channels, gfeed.shape[2]), bot...  258 us
    pallas_call x2, Pallas kernels, run_attend_back(): pl.pallas_call(attend_back, grid=(count // ROWS,), in_specs=[block_of(cha...  184 us
    reduce_scatter x2, waiting for transfers between devices, on_device(): lax.psum_scatter(grads.reshape(blk_count * channels, grads.shape[2]), bot...  170 us
    pallas_call x2, Pallas kernels, run_attend_forward(): pl.pallas_call(attend_forward, grid=(count // ROWS,), in_specs=[block_of(...  104 us
    pallas_call x2, Pallas kernels, run_feed_back(): pl.pallas_call(lambda *refs: feed_back(*refs, chunk=chunk), grid=(count /...  82.8 us
    all_gather x2, waiting for transfers between devices, on_device(): lax.all_gather(attn_shard[layer].astype(BF16), both, axis=0, tiled=True)  68.7 us
    pallas_call x2, Pallas kernels, run_feed_forward(): pl.pallas_call(lambda *refs: feed_forward(*refs, chunk=chunk), grid=(coun...  64.8 us
  transfers between devices with their start and end apart: 10, of which 8 were waited for; matrix products, arithmetic and copies ran while one was open for 9% of the time, Pallas kernels for 12%

profile of v1, /device:TPU:0, one launch (start us, length us, event | category | flops | bytes accessed | tf_op | source)
XLA Modules:
  0.0 1138.6 jit_solution(4408608046677437828)
XLA Ops:
  7.2 1.3 reshape.359
  13.6 3.0 reshape.389
  16.6 8.2 copy.367
  26.1 5.3 broadcast_multiply_fusion
  31.4 5.6 reshape.370
  37.0 8.1 copy.380
  47.1 23.5 %all-gather.9.cloned.1.call-done = bf16[1,1024,1024]{2,1,0:T(8,128)(2,1)} async-done(((bf16[1,32,1024]{2,1,0:T(8,128)(2,1)}), bf16[1,1024,1024]{2,1,0:T(8,128)(2,1)}) %all-gather.9.cloned.1.call-update) | async-done | bytes 2097168 | tf_op jit(solution)/shard_map/all_gather | solution.py:603
  70.6 3.3 reshape.361
  74.0 4.6 copy.371
  78.5 3.5 reshape.362
  82.0 1.3 slice.148.qkv_ref
  84.2 45.2 %all-gather.13.cloned.1.call-done = bf16[1,1024,1024]{2,1,0:T(8,128)(2,1)} async-done(((bf16[1,32,1024]{2,1,0:T(8,128)(2,1)}), bf16[1,1024,1024]{2,1,0:T(8,128)(2,1)}) %all-gather.13.cloned.1.call-update) | async-done | bytes 2097168 | tf_op jit(solution)/shard_map/all_gather | solution.py:603
  129.4 3.3 reshape.365
  132.7 4.6 copy.375
  137.3 3.3 reshape.366
  140.6 1.3 slice.154.qkv_ref
  142.7 1.5 broadcast_in_dim.45.mask_ref
  144.2 51.9 %attend_forward.2 = (f32[2624,512]{1,0:T(8,128)}, bf16[2624,1536]{1,0:T(8,128)(2,1)}, bf16[2624,512]{1,0:T(8,128)(2,1)}, bf16[2624,512]{1,0:T(8,128)(2,1)}, f32[2624,512]{1,0:T(8,128)}) custom-call(f32[2624,512]{1,0:T(8,128)} %bitcast.128, f32[2624,128]{1,0:T(8,128)} %broadcast_in_dim.45.mask_ref, bf16[512,1536]{1,0:T(8,128)(2,1)} %slice.148.qkv_ref, ...), custom_call_target="tpu_custom_call" | custom-call | tf_op jit(solution)/shard_map/attend_forward/pallas_call | solution.py:428
  196.0 32.7 %feed_forward.2 = (f32[2624,512]{1,0:T(8,128)}, bf16[2624,2048]{1,0:T(8,128)(2,1)}, bf16[2624,2048]{1,0:T(8,128)(2,1)}) custom-call(f32[2624,512]{1,0:T(8,128)} %get-tuple-element.54.refs_0_.refs_1_, bf16[2,512,2048]{2,1,0:T(8,128)(2,1)} %bitcast.134, f32[4,512]{1,0:T(4,128)} %get-tuple-element.303.norm_ref.refs_2_.refs_5_), custom_call_target="tpu_custom_call" | custom-call | tf_op jit(solution)/shard_map/feed_forward/pallas_call | solution.py:455
  228.8 51.8 %attend_forward.3 = (f32[2624,512]{1,0:T(8,128)}, bf16[2624,1536]{1,0:T(8,128)(2,1)}, bf16[2624,512]{1,0:T(8,128)(2,1)}, bf16[2624,512]{1,0:T(8,128)(2,1)}, f32[2624,512]{1,0:T(8,128)}) custom-call(f32[2624,512]{1,0:T(8,128)} %get-tuple-element.55.x_ref, f32[2624,128]{1,0:T(8,128)} %broadcast_in_dim.45.mask_ref, bf16[512,1536]{1,0:T(8,128)(2,1)} %slice.154.qkv_ref, ...), custom_call_target="tpu_custom_call" | custom-call | tf_op jit(solution)/shard_map/attend_forward/pallas_call | solution.py:428
  280.6 32.1 %feed_forward.3 = (bf16[2624,512]{1,0:T(8,128)(2,1)}, bf16[2624,2048]{1,0:T(8,128)(2,1)}, bf16[2624,2048]{1,0:T(8,128)(2,1)}) custom-call(f32[2624,512]{1,0:T(8,128)} %get-tuple-element.56.refs_0_.refs_1_, bf16[2,512,2048]{2,1,0:T(8,128)(2,1)} %bitcast.136, f32[4,512]{1,0:T(4,128)} %get-tuple-element.302.norm_ref.refs_2_.refs_5_), custom_call_target="tpu_custom_call" | custom-call | tf_op jit(solution)/shard_map/feed_forward/pallas_call | solution.py:455
  312.7 41.3 %feed_back.2 = (f32[2624,512]{1,0:T(8,128)}, bf16[2,512,2048]{2,1,0:T(8,128)(2,1)}, f32[2,512]{1,0:T(2,128)}) custom-call(f32[2624,512]{1,0:T(8,128)} %bitcast.133, f32[2624,512]{1,0:T(8,128)} %get-tuple-element.56.refs_0_.refs_1_, bf16[2624,2048]{1,0:T(8,128)(2,1)} %get-tuple-element.58.refs_2_, bf16[2624,2048]{1,0:T(8,128)(2,1)} %get-tuple-element.59.refs_3_, ...), custom_call_target="tpu_custom_call" | custom-call | tf_op jit(solution)/shard_map/feed_back/pallas_call | solution.py:473
  353.9 92.1 %attend_back.2 = (f32[2624,512]{1,0:T(8,128)}, bf16[512,1536]{1,0:T(8,128)(2,1)}, bf16[512,512]{1,0:T(8,128)(2,1)}, f32[2,512]{1,0:T(2,128)}, f32[9,8,512]{2,1,0:T(8,128)}, /*index=5*/f32[49,8,512]{2,1,0:T(8,128)}) custom-call(f32[2624,512]{1,0:T(8,128)} %get-tuple-element.60.gatt_ref, f32[2624,512]{1,0:T(8,128)} %get-tuple-element.55.x_ref, ...), custom_call_target="tpu_custom_call" | custom-call | tf_op jit(solution)/shard_map/attend_back/pallas_call | solution.py:497
  446.0 41.6 %feed_back.3 = (f32[2624,512]{1,0:T(8,128)}, bf16[2,512,2048]{2,1,0:T(8,128)(2,1)}, f32[2,512]{1,0:T(2,128)}) custom-call(f32[2624,512]{1,0:T(8,128)} %get-tuple-element.65.refs_0_, f32[2624,512]{1,0:T(8,128)} %get-tuple-element.54.refs_0_.refs_1_, bf16[2624,2048]{1,0:T(8,128)(2,1)} %get-tuple-element.66.refs_2_, ...), custom_call_target="tpu_custom_call" | custom-call | tf_op jit(solution)/shard_map/feed_back/pallas_call | solution.py:473
  487.6 92.0 %attend_back.3 = (f32[2624,512]{1,0:T(8,128)}, bf16[512,1536]{1,0:T(8,128)(2,1)}, bf16[512,512]{1,0:T(8,128)(2,1)}, f32[2,512]{1,0:T(2,128)}, f32[9,8,512]{2,1,0:T(8,128)}, /*index=5*/f32[49,8,512]{2,1,0:T(8,128)}) custom-call(f32[2624,512]{1,0:T(8,128)} %get-tuple-element.68.gatt_ref, f32[2624,512]{1,0:T(8,128)} %bitcast.129, ...), custom_call_target="tpu_custom_call" | custom-call | tf_op jit(solution)/shard_map/attend_back/pallas_call | solution.py:497
  579.7 1.4 reduce_sum.71
  583.3 1.7 pad_maximum_fusion.3
  585.0 2.8 reshape.377
  587.8 2.4 copy.385
  590.7 1.6 pad_maximum_fusion.1
  592.5 1.7 pad_maximum_fusion.2
  594.2 3.0 reshape.376
  597.2 2.4 copy.383
  600.1 1.6 pad_maximum_fusion
  604.9 2.8 copy.438
  607.6 2.3 reshape.369
  609.9 8.2 copy.437
  618.1 5.7 reshape.373
  623.8 66.4 %reduce-scatter.7.cloned.1.call-done = bf16[32,1152]{1,0:T(8,128)(2,1)} async-done(((bf16[1024,1152]{1,0:T(8,128)(2,1)}), bf16[32,1152]{1,0:T(8,128)(2,1)}) %reduce-scatter.7.cloned.1.call-update) | async-done | bytes 73744 | tf_op jit(solution)/shard_map/reduce_scatter | solution.py:658
  690.3 104.1 %reduce-scatter.5.cloned.1.call-done = bf16[32,1152]{1,0:T(8,128)(2,1)} async-done(((bf16[1024,1152]{1,0:T(8,128)(2,1)}), bf16[32,1152]{1,0:T(8,128)(2,1)}) %reduce-scatter.5.cloned.1.call-update) | async-done | bytes 73744 | tf_op jit(solution)/shard_map/reduce_scatter | solution.py:658
  796.2 21.1 %all_gather.19 = bf16[2,512,62]{2,0,1:T(2,128)(2,1)S(1)} all-gather(bf16[2,32,62]{2,0,1:T(2,128)(2,1)S(1)} %copy.414), channel_id=1, replica_groups=mesh['tok'=16,'blk'=2] {'tok'}, dimensions={1}, use_global_device_ids=true | all-gather | bytes 134912 | tf_op jit(solution)/shard_map/all_gather | solution.py:724
  818.1 118.7 %reduce-scatter.11.cloned.1.call-done = bf16[32,2048]{1,0:T(8,128)(2,1)} async-done(((bf16[1024,2048]{1,0:T(8,128)(2,1)}), bf16[32,2048]{1,0:T(8,128)(2,1)}) %reduce-scatter.11.cloned.1.call-update) | async-done | bytes 131088 | tf_op jit(solution)/shard_map/reduce_scatter | solution.py:642
  937.9 139.1 %reduce-scatter.9.cloned.1.call-done = bf16[32,2048]{1,0:T(8,128)(2,1)} async-done(((bf16[1024,2048]{1,0:T(8,128)(2,1)}), bf16[32,2048]{1,0:T(8,128)(2,1)}) %reduce-scatter.9.cloned.1.call-update) | async-done | bytes 131088 | tf_op jit(solution)/shard_map/reduce_scatter | solution.py:642
  1078.9 4.0 all-to-all-start
  1088.7 8.5 all-to-all-done
  1098.1 10.2 schulz.1
  1108.3 4.0 all-to-all-start.1
  1113.3 13.5 %all-to-all-done.1 = bf16[16,1,32,512]{3,2,1,0:T(8,128)(2,1)S(1)} async-done(((bf16[16,1,32,512]{3,2,1,0:T(8,128)(2,1)}), bf16[16,1,32,512]{3,2,1,0:T(8,128)(2,1)S(1)}, u32[]{:S(2)}, u32[]{:S(2)}) %all-to-all-start.1) | async-done | bytes 524320 | tf_op jit(solution)/shard_map/all_to_all | solution.py:692
  (194 shorter events, 33.9 us)
Async XLA Ops:
  7.2 6.4 copy-start
  7.2 63.4 %all-gather.9.cloned.1.call-start = ((), (), s32[]{:S(2)}) async-start(), calls=%async_computation.10 | async-start | bytes 2162688 | tf_op jit(solution)/shard_map/all_gather | solution.py:603
  10.3 119.0 %all-gather.13.cloned.1.call-start = ((), (), s32[]{:S(2)}) async-start(), calls=%async_computation.12 | async-start | bytes 2162688 | tf_op jit(solution)/shard_map/all_gather | solution.py:603
  11.1 184.9 %all-gather.11.cloned.1.call-start = ((), (), s32[]{:S(2)}) async-start(), calls=%async_computation.11 | async-start | bytes 4325376 | tf_op jit(solution)/shard_map/all_gather | solution.py:608
  12.9 267.7 %all-gather.15.cloned.1.call-start = ((), (), s32[]{:S(2)}) async-start(), calls=%async_computation.13 | async-start | bytes 4325376 | tf_op jit(solution)/shard_map/all_gather | solution.py:608
  13.5 676.7 %reduce-scatter.7.cloned.1.call-start = ((), (), s32[]{:S(2)}) async-start(), calls=%async_computation.7 | async-start | bytes 2433024 | tf_op jit(solution)/shard_map/reduce_scatter | solution.py:658
  16.6 8.2 copy-start.32
  16.6 8.7 copy-start.23
  16.6 9.3 copy-start.9
  37.0 8.1 copy-start.26
  487.6 93.5 %copy-start.8 = (f32[49,8,512]{2,1,0:T(8,128)S(1)}, f32[49,8,512]{2,1,0:T(8,128)}, u32[]{:S(2)}) copy-start(f32[49,8,512]{2,1,0:T(8,128)} %get-tuple-element.85) | copy-start | bytes 2408452
  487.6 94.7 %copy-start.31 = (f32[2,512]{1,0:T(2,128)S(1)}, f32[2,512]{1,0:T(2,128)}, u32[]{:S(2)}) copy-start(f32[2,512]{1,0:T(2,128)} %get-tuple-element.77) | copy-start | bytes 12292
  487.6 95.4 %copy-start.22 = (f32[9,8,512]{2,1,0:T(8,128)S(1)}, f32[9,8,512]{2,1,0:T(8,128)}, u32[]{:S(2)}) copy-start(f32[9,8,512]{2,1,0:T(8,128)} %get-tuple-element.84) | copy-start | bytes 442372
  487.6 95.4 %copy-start.29 = (f32[2,512]{1,0:T(2,128)S(1)}, f32[2,512]{1,0:T(2,128)}, u32[]{:S(2)}) copy-start(f32[2,512]{1,0:T(2,128)} %get-tuple-element.83) | copy-start | bytes 12292
  487.6 95.4 %copy-start.30 = (f32[2,512]{1,0:T(2,128)S(1)}, f32[2,512]{1,0:T(2,128)}, u32[]{:S(2)}) copy-start(f32[2,512]{1,0:T(2,128)} %get-tuple-element.82) | copy-start | bytes 12292
  579.7 3.6 copy-start.15
  590.7 1.8 copy-start.16
  592.3 202.0 %reduce-scatter.5.cloned.1.call-start = ((), (), s32[]{:S(2)}) async-start(), calls=%async_computation.6 | async-start | bytes 2433024 | tf_op jit(solution)/shard_map/reduce_scatter | solution.py:658
  601.8 335.1 %reduce-scatter.11.cloned.1.call-start = ((), (), s32[]{:S(2)}) async-start(), calls=%async_computation.9 | async-start | bytes 4325376 | tf_op jit(solution)/shard_map/reduce_scatter | solution.py:642
  602.5 0.9 copy-start.21
  602.5 474.4 %reduce-scatter.9.cloned.1.call-start = ((), (), s32[]{:S(2)}) async-start(), calls=%async_computation.8 | async-start | bytes 4325376 | tf_op jit(solution)/shard_map/reduce_scatter | solution.py:642
  602.6 2.2 copy-start.4
  602.6 2.2 copy-start.6
  618.1 176.2 %copy-start.12 = (f32[2,32,768]{2,1,0:T(8,128)S(1)}, f32[2,32,768]{2,1,0:T(8,128)}, u32[]{:S(2)}) copy-start(f32[2,32,768]{2,1,0:T(8,128)} %reshape.375) | copy-start | bytes 589828
  618.1 176.2 %copy-start.24 = (f32[2,256,32]{1,2,0:T(8,128)S(1)}, f32[2,256,32]{1,2,0:T(8,128)}, u32[]{:S(2)}) copy-start(f32[2,256,32]{1,2,0:T(8,128)} %param.28) | copy-start | bytes 196612
  623.8 193.7 %copy-start.20 = (f32[2,49,512]{2,0,1:T(2,128)S(1)}, f32[2,49,512]{2,0,1:T(2,128)}, u32[]{:S(2)}) copy-start(f32[2,49,512]{2,0,1:T(2,128)} %param.33) | copy-start | bytes 602116
  690.3 105.9 %copy-start.17 = (bf16[32,1152]{1,0:T(8,128)(2,1)S(1)}, bf16[32,1152]{1,0:T(8,128)(2,1)}, u32[]{:S(2)}) copy-start(bf16[32,1152]{1,0:T(8,128)(2,1)} %reduce-scatter.7.cloned.1.call-done) | copy-start | bytes 221188
  794.3 1.8 copy-start.18
  794.3 23.6 %copy-start.27 = (f32[2,9,512]{2,0,1:T(2,128)S(1)}, f32[2,9,512]{2,0,1:T(2,128)}, u32[]{:S(2)}) copy-start(f32[2,9,512]{2,0,1:T(2,128)} %param.32) | copy-start | bytes 110596
  794.3 23.7 %copy-start.10 = (f32[2,49,512]{2,0,1:T(2,128)S(1)}, f32[2,49,512]{2,0,1:T(2,128)}, u32[]{:S(2)}) copy-start(f32[2,49,512]{2,0,1:T(2,128)} %param.26) | copy-start | bytes 602116
  1078.9 8.4 copy-start.28
  1078.9 18.4 %all-to-all-start = ((bf16[16,1,32,512]{3,2,1,0:T(8,128)(2,1)}), bf16[16,1,32,512]{3,2,1,0:T(8,128)(2,1)S(1)}, u32[]{:S(2)}, u32[]{:S(2)}) async-start(bf16[16,1,32,512]{3,2,1,0:T(8,128)(2,1)} %maximum_bitcast_fusion), calls=%async_computation.4 | async-start | bytes 1048576 | tf_op jit(solution)/shard_map/all_to_all | solution.py:688
  1084.4 27.9 %copy-start.13 = (bf16[32,2048]{1,0:T(8,128)(2,1)S(1)}, bf16[32,2048]{1,0:T(8,128)(2,1)}, u32[]{:S(2)}) copy-start(bf16[32,2048]{1,0:T(8,128)(2,1)} %reduce-scatter.11.cloned.1.call-done) | copy-start | bytes 393220
  1084.4 27.9 %copy-start.14 = (bf16[32,2048]{1,0:T(8,128)(2,1)S(1)}, bf16[32,2048]{1,0:T(8,128)(2,1)}, u32[]{:S(2)}) copy-start(bf16[32,2048]{1,0:T(8,128)(2,1)} %reduce-scatter.9.cloned.1.call-done) | copy-start | bytes 393220
  1084.6 27.7 %copy-start.5 = (f32[2,1024,32]{1,2,0:T(8,128)S(1)}, f32[2,1024,32]{1,2,0:T(8,128)}, u32[]{:S(2)}) copy-start(f32[2,1024,32]{1,2,0:T(8,128)} %param.30) | copy-start | bytes 786436
  1084.7 27.7 %copy-start.7 = (f32[2,32,1024]{2,1,0:T(8,128)S(1)}, f32[2,32,1024]{2,1,0:T(8,128)}, u32[]{:S(2)}) copy-start(f32[2,32,1024]{2,1,0:T(8,128)} %param.29) | copy-start | bytes 786436
  1087.4 25.9 %copy-start.25 = (f32[2,4,512]{2,1,0:T(4,128)}, f32[2,4,512]{2,1,0:T(4,128)S(1)}, u32[]{:S(2)}) copy-start(f32[2,4,512]{2,1,0:T(4,128)S(1)} %get-tuple-element.273) | copy-start | bytes 49156
  1097.3 0.8 copy-start.1
  1108.3 18.5 %all-to-all-start.1 = ((bf16[16,1,32,512]{3,2,1,0:T(8,128)(2,1)}), bf16[16,1,32,512]{3,2,1,0:T(8,128)(2,1)S(1)}, u32[]{:S(2)}, u32[]{:S(2)}) async-start(bf16[16,1,32,512]{3,2,1,0:T(8,128)(2,1)} %bitcast.154), calls=%async_computation.5 | async-start | bytes 1048576 | tf_op jit(solution)/shard_map/all_to_all | solution.py:692
  1113.3 14.2 %copy-start.11 = (f32[2,32,768]{2,1,0:T(8,128)S(1)}, f32[2,32,768]{2,1,0:T(8,128)}, u32[]{:S(2)}) copy-start(f32[2,32,768]{2,1,0:T(8,128)} %param.20) | copy-start | bytes 589828
  1126.9 1.5 copy-start.19
  1127.0 2.4 copy-start.2
  1127.5 3.1 copy-start.3
Sparse Core Ops, SparseCore 0:
  11.4 59.1 all-gather.8
  74.0 55.2 all-gather.12
  132.8 60.8 all-gather.10
  197.0 60.8 all-gather.14
  592.4 97.7 reduce-scatter.6
  696.2 98.0 reduce-scatter.4
  796.6 140.2 reduce-scatter.10
  939.1 137.7 reduce-scatter.8

commit v2 on v1

--- a/solution.py
+++ b/solution.py
@@ -1,3 +1,4 @@
+import functools
 import math
 
 import jax
@@ -131,20 +132,43 @@
     ref[2 * quad + 1, rows, :] = values[:, LANES:]
 
 
-def attend_forward(
-    x_ref, mask_ref, qkv_ref, proj_ref, norm_ref, cpe_ref, crpe_ref,
-    conv_ref, packed_ref, rel_ref, mixed_ref, att_ref,
-    x_pad, v_pad, q_s, k_s, v_s, f_s, c_s,
-):
+def to_token_major(src_ref, put):
+    for token in range(SLOT):
+        put(slice(token * IMGS, (token + 1) * IMGS), src_ref[pl.ds(token, IMGS, stride=SLOT), :])
+
+
+def to_image_major(src_ref, put):
+    for image in range(IMGS):
+        put(slice(image * SLOT, (image + 1) * SLOT), src_ref[pl.ds(image, SLOT, stride=IMGS), :])
+
+
+def attend_forward(*refs, first):
+    if first:
+        tokens_ref, refs = refs[0], refs[1:]
+        (mask_ref, w_ref, norm_ref, cpe_ref, crpe_ref, x_ref, conv_ref, packed_ref, rel_ref,
+         mixed_ref, att_ref, x_pad, v_pad, q_s, k_s, v_s, f_s, c_s) = refs
+    else:
+        (x_ref, mask_ref, w_ref, norm_ref, cpe_ref, crpe_ref, conv_ref, packed_ref, rel_ref,
+         mixed_ref, att_ref, x_pad, v_pad, q_s, k_s, v_s, f_s, c_s) = refs
     channels = x_ref.shape[1]
     tiles = channels // LANES
     head_dim = channels // HEADS
+    half = channels // 2
 
     @pl.when(pl.program_id(0) == 0)
     def _():
         x_pad[...] = jnp.zeros_like(x_pad)
         v_pad[...] = jnp.zeros_like(v_pad)
 
+    if first:
+        for at in range(tiles):
+            cols = lane(at)
+            f_s[at] = tokens_ref[:, cols].astype(F32)
+
+            def put(rows, values, cols=cols):
+                x_ref[rows, cols] = values
+
+            to_token_major(f_s.at[at], put)
     mask = mask_ref[...]
     for at in range(tiles):
         cols = lane(at)
@@ -161,12 +185,14 @@
         lax.fori_loop(0, SIDE, conv_step, 0)
     unit, _ = normalize(conv_ref[...])
     normed = (unit * norm_ref[0:1, :] + norm_ref[1:2, :]).astype(BF16)
-    for third, keep in enumerate((q_s, k_s, v_s)):
-        part = mm(normed, qkv_ref[:, third * channels : (third + 1) * channels]).astype(BF16)
-        packed_ref[:, third * channels : (third + 1) * channels] = part
-        part = part.astype(F32)
-        for at in range(tiles):
-            keep[at] = part[:, lane(at)]
+    for side in range(2):
+        for third, keep in enumerate((q_s, k_s, v_s)):
+            cols = slice(third * half, (third + 1) * half)
+            part = mm(normed, w_ref[side, :, cols]).astype(BF16)
+            packed_ref[:, side * 3 * half + third * half : side * 3 * half + (third + 1) * half] = part
+            part = part.astype(F32)
+            for at in range(tiles // 2):
+                keep[side * (tiles // 2) + at] = part[:, lane(at)]
     for at in range(tiles):
         k_s[at] = key_softmax(k_s[at], mask_ref[...])
     block = head_mask(2 * LANES, head_dim)
@@ -198,7 +224,11 @@
         rel = c_s[...]
         rel_ref[:, cols] = rel.astype(BF16)
         mixed_ref[:, cols] = (f_s[at] + q_s[at] * rel).astype(BF16)
-    att_ref[...] = conv_ref[...] + mm_nt(mixed_ref[...], proj_ref[...])
+    out = conv_ref[...]
+    for side in range(2):
+        cols = slice(side * half, (side + 1) * half)
+        out = out + mm_nt(mixed_ref[:, cols], w_ref[side, :, 3 * half :])
+    att_ref[...] = out
 
 
 def gelu_parts(values):
@@ -213,7 +243,7 @@
     return values * phi, phi + (values * 0.3989422804014327) * bell
 
 
-def feed_forward(att_ref, up_down_ref, norm_ref, out_ref, act_ref, slope_ref, chunk):
+def feed_forward(att_ref, up_down_ref, norm_ref, out_ref, act_ref, slope_ref, *scratch, chunk):
     blks, _, both = up_down_ref.shape
     width = both // 2
     att = att_ref[...]
@@ -229,13 +259,26 @@
             act_ref[:, cols] = active
             slope_ref[:, cols] = slope.astype(BF16)
             total = total + mm_nt(active, up_down_ref[blk, :, width + at : width + at + chunk])
-    out_ref[...] = total.astype(out_ref.dtype)
-
-
-def feed_back(
-    up_ref, att_ref, act_ref, slope_ref, up_down_ref, norm_ref,
-    gatt_ref, gweight_ref, gnorm_ref, total_s, chunk,
-):
+    if not scratch:
+        out_ref[...] = total
+        return
+    turn_s, whole_s = scratch
+    for at in range(att.shape[1] // LANES):
+        cols = lane(at)
+        turn_s[...] = total[:, cols]
+
+        def put(rows, values, cols=cols):
+            whole_s[rows, cols] = values
+
+        to_image_major(turn_s, put)
+    out_ref[...] = whole_s[...].astype(BF16)
+
+
+def feed_back(*refs, first, chunk):
+    if first:
+        mask_ref, refs = refs[0], refs[1:]
+    (up_ref, att_ref, act_ref, slope_ref, up_down_ref, norm_ref,
+     gatt_ref, gweight_ref, gnorm_ref, total_s) = refs[:10]
     step, steps = pl.program_id(0), pl.num_programs(0)
     blks, _, both = up_down_ref.shape
     width = both // 2
@@ -245,7 +288,19 @@
         total_s[...] = jnp.zeros_like(total_s)
         gnorm_ref[...] = jnp.zeros_like(gnorm_ref)
 
-    upstream = up_ref[...]
+    if first:
+        turn_s, whole_s = refs[10:]
+        for at in range(up_ref.shape[1] // LANES):
+            cols = lane(at)
+            turn_s[...] = up_ref[:, cols]
+
+            def put(rows, values, cols=cols):
+                whole_s[rows, cols] = values * mask_ref[rows, :]
+
+            to_token_major(turn_s, put)
+        upstream = whole_s[...]
+    else:
+        upstream = up_ref[...]
     unit, inv = normalize(att_ref[...])
     gain = norm_ref[2:3, :]
     normed_t = (unit * gain + norm_ref[3:4, :]).astype(BF16).T
@@ -274,29 +329,35 @@
 
 def attend_back(
     gatt_ref, x_ref, conv_ref, packed_ref, rel_ref, mixed_ref, mask_ref,
-    qkv_ref, proj_ref, norm_ref, cpe_ref, crpe_ref,
-    up_ref, gqkv_ref, gproj_ref, gnorm_ref, gcpe_ref, gcrpe_ref,
-    qkv_s, proj_s, x_pad, g_pad, v_pad, c_pad, q_s, k_s, v_s, f_s, dq_s, dk_s, dv_s, c_s, gp_s,
+    w_ref, norm_ref, cpe_ref, crpe_ref,
+    out_ref, gw_ref, gnorm_ref, gcpe_ref, gcrpe_ref,
+    w_s, x_pad, g_pad, v_pad, c_pad, q_s, k_s, v_s, f_s, dq_s, dk_s, dv_s, c_s, gp_s,
+    *scratch,
 ):
     channels = x_ref.shape[1]
     tiles = channels // LANES
     head_dim = channels // HEADS
+    half = channels // 2
     step, steps = pl.program_id(0), pl.num_programs(0)
+    up_ref = scratch[0] if scratch else out_ref
 
     @pl.when(step == 0)
     def _():
-        for ref in (x_pad, g_pad, v_pad, c_pad, qkv_s, proj_s, gnorm_ref, gcpe_ref, gcrpe_ref):
+        for ref in (x_pad, g_pad, v_pad, c_pad, w_s, gnorm_ref, gcpe_ref, gcrpe_ref):
             ref[...] = jnp.zeros_like(ref)
 
     att_in = gatt_ref[...].astype(BF16)
-    proj_s[...] += mm(att_in.T, mixed_ref[...])
-    grad_mixed = mm(att_in, proj_ref[...])
-    for at in range(tiles):
-        f_s[at] = grad_mixed[:, lane(at)]
-    for third, keep in enumerate((q_s, k_s, v_s)):
-        for at in range(tiles):
-            cols = slice(third * channels + at * LANES, third * channels + (at + 1) * LANES)
-            keep[at] = packed_ref[:, cols].astype(F32)
+    att_t = att_in.T
+    for side in range(2):
+        cols = slice(side * half, (side + 1) * half)
+        w_s[side, :, 3 * half :] += mm(att_t, mixed_ref[:, cols])
+        grad_mixed = mm(att_in, w_ref[side, :, 3 * half :])
+        for at in range(tiles // 2):
+            f_s[side * (tiles // 2) + at] = grad_mixed[:, lane(at)]
+        for third, keep in enumerate((q_s, k_s, v_s)):
+            for at in range(tiles // 2):
+                start = (3 * side + third) * half + at * LANES
+                keep[side * (tiles // 2) + at] = packed_ref[:, start : start + LANES].astype(F32)
     for at in range(tiles):
         k_s[at] = key_softmax(k_s[at], mask_ref[...])
     block = head_mask(2 * LANES, head_dim)
@@ -317,16 +378,16 @@
     lax.fori_loop(0, IMGS, one_image, 0)
     for at in range(tiles):
         cols = lane(at)
+        start = (3 * (at // (tiles // 2))) * half + (at % (tiles // 2)) * LANES
+        place = lambda third: slice(start + third * half, start + third * half + LANES)
         mask = mask_ref[...]
         weights = k_s[at]
         share = weights * dk_s[at]
         total = jnp.sum(share.reshape(SLOT, IMGS, LANES), axis=0, keepdims=True)
         back = share.reshape(SLOT, IMGS, LANES) - weights.reshape(SLOT, IMGS, LANES) * total
-        gp_s[:, channels + at * LANES : channels + (at + 1) * LANES] = back.reshape(
-            ROWS, LANES
-        ).astype(BF16)
+        gp_s[:, place(1)] = back.reshape(ROWS, LANES).astype(BF16)
         grads = f_s[at]
-        gp_s[:, cols] = (dq_s[at] + grads * rel_ref[:, cols].astype(F32)).astype(BF16)
+        gp_s[:, place(0)] = (dq_s[at] + grads * rel_ref[:, cols].astype(F32)).astype(BF16)
         reach = tile_radius(at, head_dim)
         masked = v_s[at] * mask
         v_pad[3 : 3 + SIDE] = masked[IMGS:].reshape(SIDE, SIDE, IMGS, LANES)
@@ -342,16 +403,15 @@
 
         lax.fori_loop(0, SIDE, rel_step, 0)
         conv_kernel_grad(c_pad, v_pad, gcrpe_ref, cols, 3, reach, 7, 3)
-        gp_s[:, 2 * channels + at * LANES : 2 * channels + (at + 1) * LANES] = c_s[...].astype(BF16)
+        gp_s[:, place(2)] = c_s[...].astype(BF16)
     unit, inv = normalize(conv_ref[...])
     gain = norm_ref[0:1, :]
     normed_t = (unit * gain + norm_ref[1:2, :]).astype(BF16).T
     grad_rows = None
-    for third in range(3):
-        cols = slice(third * channels, (third + 1) * channels)
-        part_in = gp_s[:, cols]
-        qkv_s[:, cols] += mm(normed_t, part_in)
-        part = mm_nt(part_in, qkv_ref[:, cols])
+    for side in range(2):
+        part_in = gp_s[:, side * 3 * half : (side + 1) * 3 * half]
+        w_s[side, :, : 3 * half] += mm(normed_t, part_in)
+        part = mm_nt(part_in, w_ref[side, :, : 3 * half])
         grad_rows = part if grad_rows is None else grad_rows + part
     gnorm_ref[0:1, :] += jnp.sum(grad_rows * unit, axis=0, keepdims=True)
     gnorm_ref[1:2, :] += jnp.sum(grad_rows, axis=0, keepdims=True)
@@ -372,11 +432,17 @@
 
         lax.fori_loop(0, SIDE, conv_step, 0)
         conv_kernel_grad(g_pad, x_pad, gcpe_ref, cols, 1, 1, 3, 1)
+        if scratch:
+            c_s[...] = up_ref[:, cols]
+
+            def put(rows, values, cols=cols):
+                out_ref[rows, cols] = values
+
+            to_image_major(c_s, put)
 
     @pl.when(step == steps - 1)
     def _():
-        gqkv_ref[...] = qkv_s[...].astype(BF16)
-        gproj_ref[...] = proj_s[...].astype(BF16)
+        gw_ref[...] = w_s[...].astype(BF16)
 
 
 def schulz(fresh_ref, out_ref, width):
@@ -417,27 +483,35 @@
     return pl.BlockSpec(shape, lambda g: (0,) * len(shape), pipeline_mode=pl.Buffered(1))
 
 
+def some_columns(weights):
+    array, width, at = weights
+    shape = array.shape[:2] + (width,)
+    return pl.BlockSpec(shape, lambda g: (0, 0, at), pipeline_mode=pl.Buffered(1))
+
+
 def whole_out(shape):
     return pl.BlockSpec(shape, lambda g: (0,) * len(shape))
 
 
-def run_attend_forward(x, mask, qkv, proj, norm, cpe, crpe):
+def cost(us):
+    return pl.CostEstimate(flops=int(us * 1e9), bytes_accessed=int(us * 1e5), transcendentals=0)
+
+
+def run_attend_forward(x, mask, weights, norm, cpe, crpe, first):
     count, channels = x.shape
     tiles = channels // LANES
     flat = pltpu.VMEM((tiles, ROWS, LANES), F32)
+    out = lambda cols, kind: jax.ShapeDtypeStruct((count, cols), kind)
+    outs = [out(channels, F32), out(3 * channels, BF16)] + [out(channels, BF16)] * 2
+    outs = [out(channels, F32)] * first + outs + [out(channels, F32)]
     return pl.pallas_call(
-        attend_forward,
+        functools.partial(attend_forward, first=first),
         grid=(count // ROWS,),
         in_specs=[block_of(channels), block_of(LANES)]
-        + [whole(a) for a in (qkv, proj, norm, cpe, crpe)],
-        out_specs=[block_of(channels), block_of(3 * channels)] + [block_of(channels)] * 3,
-        out_shape=[
-            jax.ShapeDtypeStruct((count, channels), F32),
-            jax.ShapeDtypeStruct((count, 3 * channels), BF16),
-            jax.ShapeDtypeStruct((count, channels), BF16),
-            jax.ShapeDtypeStruct((count, channels), BF16),
-            jax.ShapeDtypeStruct((count, channels), F32),
-        ],
+        + [some_columns(weights)]
+        + [whole(a) for a in (norm, cpe, crpe)],
+        out_specs=[block_of(array.shape[1]) for array in outs],
+        out_shape=outs,
         scratch_shapes=[
             pltpu.VMEM((SIDE + 2, SIDE, IMGS, LANES), F32),
             pltpu.VMEM((SIDE + 6, SIDE, IMGS, LANES), F32),
@@ -445,91 +519,309 @@
             pltpu.VMEM((ROWS, LANES), F32),
         ],
         compiler_params=params_for(),
+        cost_estimate=cost(50),
         name="attend_forward",
-    )(x, mask, qkv, proj, norm, cpe, crpe)
-
-
-def run_feed_forward(att, up_down, norm, out_type, chunk=256):
+    )(x, mask, weights[0], norm, cpe, crpe)
+
+
+def run_feed_forward(att, up_down, norm, last, chunk=256):
     count, channels = att.shape
-    hidden = up_down.shape[0] * up_down.shape[2] // 2
+    hidden = up_down[0].shape[0] * up_down[1] // 2
+    turn = [pltpu.VMEM((ROWS, LANES), F32), pltpu.VMEM((ROWS, channels), F32)]
     return pl.pallas_call(
-        lambda *refs: feed_forward(*refs, chunk=chunk),
+        functools.partial(feed_forward, chunk=chunk),
         grid=(count // ROWS,),
-        in_specs=[block_of(channels), whole(up_down), whole(norm)],
+        in_specs=[block_of(channels), some_columns(up_down), whole(norm)],
         out_specs=[block_of(channels), block_of(hidden), block_of(hidden)],
         out_shape=[
-            jax.ShapeDtypeStruct((count, channels), out_type),
+            jax.ShapeDtypeStruct((count, channels), BF16 if last else F32),
             jax.ShapeDtypeStruct((count, hidden), BF16),
             jax.ShapeDtypeStruct((count, hidden), BF16),
         ],
+        scratch_shapes=turn if last else [],
         compiler_params=params_for(),
+        cost_estimate=cost(32),
         name="feed_forward",
-    )(att, up_down, norm)
-
-
-def run_feed_back(upstream, att, active, slope, up_down, norm, chunk=256):
+    )(att, up_down[0], norm)
+
+
+def run_feed_back(mask, upstream, att, active, slope, up_down, norm, first, chunk=256):
     count, channels = att.shape
     hidden = active.shape[1]
+    turn = [pltpu.VMEM((ROWS, LANES), F32), pltpu.VMEM((ROWS, channels), F32)]
+    shape = up_down[0].shape[:2] + (up_down[1],)
     return pl.pallas_call(
-        lambda *refs: feed_back(*refs, chunk=chunk),
+        functools.partial(feed_back, first=first, chunk=chunk),
         grid=(count // ROWS,),
-        in_specs=[block_of(channels), block_of(channels), block_of(hidden), block_of(hidden)]
-        + [whole(up_down), whole(norm)],
-        out_specs=[block_of(channels), whole_out(up_down.shape), whole_out((2, channels))],
+        in_specs=[block_of(LANES)] * first
+        + [block_of(channels), block_of(channels), block_of(hidden), block_of(hidden)]
+        + [some_columns(up_down), whole(norm)],
+        out_specs=[block_of(channels), whole_out(shape), whole_out((2, channels))],
         out_shape=[
             jax.ShapeDtypeStruct((count, channels), F32),
-            jax.ShapeDtypeStruct(up_down.shape, BF16),
+            jax.ShapeDtypeStruct(shape, BF16),
             jax.ShapeDtypeStruct((2, channels), F32),
         ],
-        scratch_shapes=[pltpu.VMEM(up_down.shape, F32)],
+        scratch_shapes=[pltpu.VMEM(shape, F32)] + turn * first,
         compiler_params=params_for(),
+        cost_estimate=cost(41),
         name="feed_back",
-    )(upstream, att, active, slope, up_down, norm)
-
-
-def run_attend_back(gatt, x, conv, packed, rel, mixed, mask, qkv, proj, norm, cpe, crpe):
+    )(*(([mask] if first else []) + [upstream, att, active, slope, up_down[0], norm]))
+
+
+def run_attend_back(gatt, x, conv, packed, rel, mixed, mask, weights, norm, cpe, crpe, last):
     count, channels = x.shape
     tiles = channels // LANES
     flat = pltpu.VMEM((tiles, ROWS, LANES), F32)
     three = pltpu.VMEM((SIDE + 2, SIDE, IMGS, LANES), F32)
     seven = pltpu.VMEM((SIDE + 6, SIDE, IMGS, LANES), F32)
     small = [(2, channels), (9, IMGS, channels), (49, IMGS, channels)]
+    shape = weights[0].shape[:2] + (weights[1],)
     return pl.pallas_call(
         attend_back,
         grid=(count // ROWS,),
         in_specs=[block_of(channels)] * 3
         + [block_of(3 * channels), block_of(channels), block_of(channels), block_of(LANES)]
-        + [whole(a) for a in (qkv, proj, norm, cpe, crpe)],
-        out_specs=[block_of(channels), whole_out(qkv.shape), whole_out(proj.shape)]
-        + [whole_out(shape) for shape in small],
+        + [some_columns(weights)]
+        + [whole(a) for a in (norm, cpe, crpe)],
+        out_specs=[block_of(channels), whole_out(shape)]
+        + [whole_out(each) for each in small],
         out_shape=[
             jax.ShapeDtypeStruct((count, channels), F32),
-            jax.ShapeDtypeStruct(qkv.shape, BF16),
-            jax.ShapeDtypeStruct(proj.shape, BF16),
+            jax.ShapeDtypeStruct(shape, BF16),
         ]
-        + [jax.ShapeDtypeStruct(shape, F32) for shape in small],
+        + [jax.ShapeDtypeStruct(each, F32) for each in small],
         scratch_shapes=[
-            pltpu.VMEM(qkv.shape, F32),
-            pltpu.VMEM(proj.shape, F32),
+            pltpu.VMEM(shape, F32),
             three, three, seven, seven,
             flat, flat, flat, flat, flat, flat, flat,
             pltpu.VMEM((ROWS, LANES), F32),
             pltpu.VMEM((ROWS, 3 * channels), BF16),
+        ]
+        + [pltpu.VMEM((ROWS, channels), F32)] * last,
+        compiler_params=params_for(),
+        cost_estimate=cost(92),
+        name="attend_back",
+    )(gatt, x, conv, packed, rel, mixed, mask, weights[0], norm, cpe, crpe)
+
+
+def where_am_i():
+    tok, blk = lax.axis_index("tok"), lax.axis_index("blk")
+    core, x, z = lax.rem(tok, 2), lax.rem(tok // 2, 2), tok // 4
+    return blk, z, x, core
+
+
+def device_at(y, z, x, core):
+    return (z * 4 + x * 2 + core, y)
+
+
+def neighbours(y, z, x, core):
+    fx, fy = 1 - core, core
+    flip = lambda value, by: value + by - 2 * value * by
+    first = (flip(y, fy), flip(x, fx))
+    second = (flip(y, fx), flip(x, fy))
+    cross = (1 - y, 1 - x)
+    return first, second, cross
+
+
+def greet(targets):
+    barrier = pltpu.get_barrier_semaphore()
+    for target in targets:
+        pl.semaphore_signal(barrier, inc=1, device_id=target, device_id_type=pl.DeviceIdType.MESH)
+    pl.semaphore_wait(barrier, len(targets))
+
+
+def spread_kernel(shard_ref, out_ref, send_sem, recv_sem, own_sem):
+    y, z, x, core = where_am_i()
+    first, second, cross = neighbours(y, z, x, core)
+    line = [lax.rem(z + d, 4) for d in range(4)]
+    back = [lax.rem(z + 4 - d, 4) for d in range(4)]
+    to_first = device_at(first[0], z, first[1], core)
+    to_second = device_at(second[0], z, second[1], core)
+    to_core = device_at(y, z, x, 1 - core)
+    greet([to_first, to_second, to_core] + [device_at(y, line[d], x, core) for d in (1, 2, 3)])
+    slot = lambda at, layer, side: at[0] * 16 + layer * 4 + at[1] * 2 + side
+    own = pltpu.make_async_copy(shard_ref, out_ref.at[slot((y, x), z, core)], own_sem)
+    own.start()
+    copies = []
+
+    def send(src, at, layer, side, target, number):
+        copy = pltpu.make_async_remote_copy(
+            src_ref=src, dst_ref=out_ref.at[slot(at, layer, side)],
+            send_sem=send_sem.at[number], recv_sem=recv_sem.at[number],
+            device_id=target, device_id_type=pl.DeviceIdType.MESH,
+        )
+        copy.start()
+        copies.append(copy)
+
+    def arrive(at, layer, side, number):
+        here = out_ref.at[slot(at, layer, side)]
+        pltpu.make_async_remote_copy(
+            src_ref=here, dst_ref=here, send_sem=send_sem.at[number], recv_sem=recv_sem.at[number],
+            device_id=to_core, device_id_type=pl.DeviceIdType.MESH,
+        ).wait_recv()
+
+    me = (y, x)
+    for d in (1, 2, 3):
+        send(shard_ref, me, z, core, device_at(y, line[d], x, core), d - 1)
+    for d in range(4):
+        layer = back[d]
+        if d:
+            arrive(me, layer, core, d - 1)
+        src = out_ref.at[slot(me, layer, core)] if d else shard_ref
+        send(src, me, layer, core, to_first, 3 + d)
+        send(src, me, layer, core, to_second, 7 + d)
+        send(src, me, layer, core, to_core, 15 + d)
+    for d in range(4):
+        arrive(first, back[d], core, 3 + d)
+        src = out_ref.at[slot(first, back[d], core)]
+        send(src, first, back[d], core, to_second, 11 + d)
+        send(src, first, back[d], core, to_core, 19 + d)
+    for d in range(4):
+        arrive(second, back[d], core, 7 + d)
+        send(out_ref.at[slot(second, back[d], core)], second, back[d], core, to_core, 23 + d)
+    for d in range(4):
+        arrive(cross, back[d], core, 11 + d)
+        send(out_ref.at[slot(cross, back[d], core)], cross, back[d], core, to_core, 27 + d)
+    for d in range(4):
+        arrive(me, back[d], 1 - core, 15 + d)
+        arrive(second, back[d], 1 - core, 19 + d)
+        arrive(first, back[d], 1 - core, 23 + d)
+        arrive(cross, back[d], 1 - core, 27 + d)
+    own.wait()
+    for copy in copies:
+        copy.wait_send()
+
+
+def spread(shard, collective_id):
+    return pl.pallas_call(
+        spread_kernel,
+        in_specs=[pl.BlockSpec(memory_space=pl.ANY)],
+        out_specs=pl.BlockSpec(memory_space=pl.ANY),
+        out_shape=jax.ShapeDtypeStruct((32,) + shard.shape, shard.dtype),
+        scratch_shapes=[
+            pltpu.SemaphoreType.DMA((31,)), pltpu.SemaphoreType.DMA((31,)), pltpu.SemaphoreType.DMA,
         ],
-        compiler_params=params_for(),
-        name="attend_back",
-    )(gatt, x, conv, packed, rel, mixed, mask, qkv, proj, norm, cpe, crpe)
+        compiler_params=pltpu.CompilerParams(
+            collective_id=collective_id, has_side_effects=True, vmem_limit_bytes=VMEM_BYTES
+        ),
+        name="spread",
+    )(shard)
+
+
+def collect_kernel(*refs, widths):
+    parts = len(widths)
+    grads, out_ref = refs[:parts], refs[parts]
+    own_s, chip_s, second_s, first_s, line_s, send_sem, recv_sem, load_sem = refs[parts + 1 :]
+    y, z, x, core = where_am_i()
+    first, second, cross = neighbours(y, z, x, core)
+    line = [lax.rem(z + d, 4) for d in range(4)]
+    back = [lax.rem(z + 4 - d, 4) for d in range(4)]
+    to_first = device_at(first[0], z, first[1], core)
+    to_second = device_at(second[0], z, second[1], core)
+    to_core = device_at(y, z, x, 1 - core)
+    greet([to_first, to_second, to_core] + [device_at(y, line[d], x, core) for d in (1, 2, 3)])
+    slot = lambda at, layer, side: at[0] * 16 + layer * 4 + at[1] * 2 + side
+    loads = []
+    start = 0
+    for number, (grad, width) in enumerate(zip(grads, widths)):
+        copy = pltpu.make_async_copy(
+            grad, own_s.at[:, :, start : start + width], load_sem.at[number]
+        )
+        copy.start()
+        loads.append(copy)
+        start += width
+    for copy in loads:
+        copy.wait()
+    copies = []
+
+    def send(src, dst, target, number):
+        copy = pltpu.make_async_remote_copy(
+            src_ref=src, dst_ref=dst, send_sem=send_sem.at[number], recv_sem=recv_sem.at[number],
+            device_id=target, device_id_type=pl.DeviceIdType.MESH,
+        )
+        copy.start()
+        copies.append(copy)
+
+    def arrive(ref, number):
+        pltpu.make_async_remote_copy(
+            src_ref=ref, dst_ref=ref, send_sem=send_sem.at[number], recv_sem=recv_sem.at[number],
+            device_id=to_core, device_id_type=pl.DeviceIdType.MESH,
+        ).wait_recv()
+
+    def add(ref, *others):
+        total = ref[...].astype(F32)
+        for other in others:
+            total = total + other[...].astype(F32)
+        ref[...] = total.astype(BF16)
+
+    me = (y, x)
+    order = [(cross, 0), (second, 1), (first, 2), (me, 3)]
+    theirs = {0: 0, 1: 2, 2: 1, 3: 3}
+    for place, kind in order:
+        for d in range(4):
+            number = theirs[kind] * 4 + d
+            send(own_s.at[slot(place, line[d], 1 - core)], chip_s.at[number], to_core, number)
+    for place, kind, there in ((cross, 0, 0), (second, 1, 4)):
+        for d in range(4):
+            here = chip_s.at[kind * 4 + d]
+            arrive(here, kind * 4 + d)
+            add(here, own_s.at[slot(place, line[d], core)])
+            send(here, second_s.at[there + d], to_second, 16 + there + d)
+    for d in range(4):
+        here = chip_s.at[8 + d]
+        arrive(here, 8 + d)
+        arrive(second_s.at[d], 16 + d)
+        add(here, own_s.at[slot(first, line[d], core)], second_s.at[d])
+        send(here, first_s.at[d], to_first, 24 + d)
+    for d in (1, 2, 3, 0):
+        here = chip_s.at[12 + d]
+        arrive(here, 12 + d)
+        arrive(second_s.at[4 + d], 20 + d)
+        arrive(first_s.at[d], 24 + d)
+        if d:
+            add(here, own_s.at[slot(me, line[d], core)], second_s.at[4 + d], first_s.at[d])
+            send(here, line_s.at[d - 1], device_at(y, line[d], x, core), 27 + d)
+    for d in (1, 2, 3):
+        arrive(line_s.at[d - 1], 27 + d)
+    total = chip_s[12].astype(F32) + own_s[slot(me, z, core)].astype(F32)
+    for ref in (second_s.at[4], first_s.at[0], line_s.at[0], line_s.at[1], line_s.at[2]):
+        total = total + ref[...].astype(F32)
+    out_ref[...] = total
+    for copy in copies:
+        copy.wait_send()
+
+
+def collect(grads, collective_id):
+    rows = grads[0].shape[1]
+    widths = tuple(grad.shape[2] for grad in grads)
+    block = lambda count: pltpu.VMEM((count, rows, sum(widths)), BF16)
+    return pl.pallas_call(
+        functools.partial(collect_kernel, widths=widths),
+        in_specs=[pl.BlockSpec(memory_space=pl.ANY)] * len(grads),
+        out_specs=pl.BlockSpec(memory_space=pltpu.VMEM),
+        out_shape=jax.ShapeDtypeStruct((rows, sum(widths)), F32),
+        scratch_shapes=[
+            block(32), block(16), block(8), block(4), block(3),
+            pltpu.SemaphoreType.DMA((31,)), pltpu.SemaphoreType.DMA((31,)),
+            pltpu.SemaphoreType.DMA((len(widths),)),
+        ],
+        compiler_params=pltpu.CompilerParams(
+            collective_id=collective_id, has_side_effects=True, vmem_limit_bytes=VMEM_BYTES
+        ),
+        name="collect",
+    )(*grads)
 
 
 def run_schulz(fresh, width):
-    units, height, both = fresh.shape
-    spec = pl.BlockSpec((1, height, both), lambda g: (g, 0, 0))
+    units, height, _ = fresh.shape
+    spec = pl.BlockSpec((1, height, 2 * width), lambda g: (g, 0, 0))
     return pl.pallas_call(
         lambda *refs: schulz(*refs, width=width),
         grid=(units,),
         in_specs=[spec],
         out_specs=spec,
-        out_shape=jax.ShapeDtypeStruct(fresh.shape, BF16),
+        out_shape=jax.ShapeDtypeStruct((units, height, 2 * width), BF16),
         compiler_params=params_for(),
         name="schulz",
     )(fresh)
@@ -594,72 +886,109 @@
     own_rows = qkv_weight.shape[1]
     both = ("blk", "tok")
 
-    attn_shard = jnp.concatenate(
-        [split_heads(qkv_weight, heads_own, head_dim), jnp.swapaxes(proj_weight, 1, 2)], axis=2
-    )
-    feed_shard = jnp.concatenate([up_weight, jnp.swapaxes(down_weight, 1, 2)], axis=2)
-    qkv_all, proj_all, feed_all = [], [], []
+    attn_cols, feed_cols = 4 * heads_own * head_dim, 2 * up_weight.shape[2]
+    shard = jnp.concatenate(
+        [
+            up_weight,
+            jnp.swapaxes(down_weight, 1, 2),
+            split_heads(qkv_weight, heads_own, head_dim),
+            jnp.swapaxes(proj_weight, 1, 2),
+        ],
+        axis=2,
+    ).astype(BF16)
+    near = (tok_count, blk_count) == (16, 2)
+
+    def gather(piece, kernel):
+        if kernel:
+            return spread(piece, 1).reshape(blk_count, channels, piece.shape[1])
+        full = lax.all_gather(piece, both, axis=0, tiled=True)
+        return full.reshape(blk_count, channels, piece.shape[1])
+
+    def halves(full):
+        full = full.reshape(blk_count, channels, 4, heads_own * head_dim).transpose(1, 2, 0, 3)
+        full = full.reshape(channels, 4, 2, channels // 2).transpose(2, 0, 1, 3)
+        return full.reshape(2, channels, 2 * channels)
+
+    def shares(grads):
+        if blk_count == 2:
+            return grads
+        full = grads.reshape(2, channels, 4, channels // 2).transpose(1, 2, 0, 3)
+        full = full.reshape(channels, 4, blk_count, heads_own * head_dim).transpose(2, 0, 1, 3)
+        return full.reshape(blk_count, channels, attn_cols)
+
+    attn_all, feed_all = [], []
     for layer in range(layers):
-        attn = lax.all_gather(attn_shard[layer].astype(BF16), both, axis=0, tiled=True)
-        attn = attn.reshape(blk_count, channels, 4, heads_own * head_dim)
-        attn = attn.transpose(1, 2, 0, 3).reshape(channels, 4 * channels)
-        qkv_all.append(attn[:, : 3 * channels])
-        proj_all.append(attn[:, 3 * channels :])
-        feed = lax.all_gather(feed_shard[layer].astype(BF16), both, axis=0, tiled=True)
-        feed_all.append(feed.reshape(blk_count, channels, feed.shape[1]))
+        piece = shard[layer]
+        if layer and near:
+            piece, full = lax.optimization_barrier((piece, full))
+            attn_all[0], feed_all[0] = (full, attn_cols, 2), (full, feed_cols, 0)
+        full = gather(piece, near and layer == 0)
+        if blk_count == 2:
+            attn_all.append((full, attn_cols, 2))
+            feed_all.append((full, feed_cols, 0))
+        else:
+            attn_all.append((halves(full[:, :, feed_cols:]), 2 * channels, 0))
+            feed_all.append((full[:, :, :feed_cols], feed_cols, 0))
 
     own_class = lax.dynamic_slice_in_dim(grid_class, blk_at * images_own, images_own)
     keys = key_masks(own_class)
-    mask = jnp.broadcast_to(
-        token_major(keys.reshape(own_count, 1)), (own_count, LANES)
-    )
+    mask = jnp.broadcast_to(token_major(keys.reshape(own_count, 1)), (own_count, LANES))
     taps = jnp.repeat(tap_mask(jnp.arange(HEADS, dtype=jnp.int32)), head_dim, axis=1)
 
-    stream = token_major(tokens).astype(F32)
+    stream = tokens
     saved = []
     for layer in range(layers):
         crpe = crpe_weight[layer] * taps
-        conv, packed, rel, mixed, att = run_attend_forward(
-            stream, mask, qkv_all[layer], proj_all[layer], norm_params[layer],
-            cpe_weight[layer], crpe,
+        outs = run_attend_forward(
+            stream, mask, attn_all[layer], norm_params[layer], cpe_weight[layer], crpe, layer == 0
         )
-        last = layer == layers - 1
-        out, active, slope = run_feed_forward(
-            att, feed_all[layer], norm_params[layer], BF16 if last else F32
+        if layer:
+            outs = [stream] + list(outs)
+        stream, active, slope = run_feed_forward(
+            outs[-1], feed_all[layer], norm_params[layer], layer == layers - 1
         )
-        saved.append((stream, conv, packed, rel, mixed, att, active, slope, crpe))
-        stream = out
-    block_out = image_major(stream)
-
-    upstream = token_major(cotangent * keys.reshape(own_count, 1))
+        saved.append(tuple(outs) + (active, slope, crpe))
+    block_out = stream
+
+    upstream = cotangent
     attn_sums, feed_sums = [None] * layers, [None] * layers
     small_rows = 4 + 9 + 49
     for layer in reversed(range(layers)):
         x, conv, packed, rel, mixed, att, active, slope, crpe = saved[layer]
         gatt, gfeed, gmid = run_feed_back(
-            upstream, att, active, slope, feed_all[layer], norm_params[layer]
+            mask, upstream, att, active, slope, feed_all[layer], norm_params[layer],
+            layer == layers - 1,
         )
-        feed_sums[layer] = lax.psum_scatter(
-            gfeed.reshape(blk_count * channels, gfeed.shape[2]), both,
-            scatter_dimension=0, tiled=True,
-        ).astype(F32)
-        upstream, gqkv, gproj, gfront, gcpe, gcrpe = run_attend_back(
-            gatt, x, conv, packed, rel, mixed, mask, qkv_all[layer], proj_all[layer],
-            norm_params[layer], cpe_weight[layer], crpe,
+        if near and layer == 0:
+            early, gatt = lax.optimization_barrier((early, gatt))
+        upstream, gattn, gfront, gcpe, gcrpe = run_attend_back(
+            gatt, x, conv, packed, rel, mixed, mask, attn_all[layer],
+            norm_params[layer], cpe_weight[layer], crpe, layer == 0,
         )
+        if near and layer == layers - 1:
+            early = lax.psum_scatter(
+                gfeed.reshape(blk_count * channels, gfeed.shape[2]), both,
+                scatter_dimension=0, tiled=True,
+            )
         small = jnp.concatenate([gfront, gmid, gcpe.sum(1), gcrpe.sum(1) * taps], axis=0)
         small = jnp.pad(small, ((0, LANES - small_rows), (0, 0))).T.astype(BF16)
-        grads = jnp.concatenate([gqkv, gproj], axis=1)
-        grads = grads.reshape(channels, 4, blk_count, heads_own * head_dim)
-        grads = grads.transpose(2, 0, 1, 3).reshape(blk_count, channels, 4 * heads_own * head_dim)
-        grads = jnp.concatenate(
-            [grads, jnp.broadcast_to(small, (blk_count, channels, LANES))], axis=2
-        )
-        attn_sums[layer] = lax.psum_scatter(
-            grads.reshape(blk_count * channels, grads.shape[2]), both,
-            scatter_dimension=0, tiled=True,
-        ).astype(F32)
-    tokens_grad = image_major(upstream)
+        small = jnp.broadcast_to(small, (blk_count, channels, LANES))
+        gattn = shares(gattn)
+        pieces = [g.reshape(blk_count * tok_count, own_rows, -1) for g in (gattn, small, gfeed)]
+        if near:
+            waiting = pieces[:2] if layer else waiting + pieces
+        else:
+            scatter = lambda g: lax.psum_scatter(
+                g.reshape(blk_count * channels, g.shape[2]), both, scatter_dimension=0, tiled=True
+            ).astype(F32)
+            feed_sums[layer] = scatter(pieces[2])
+            attn_sums[layer] = scatter(jnp.concatenate(pieces[:2], axis=2))
+    if near:
+        total = collect(waiting, 2)
+        cut = attn_cols + LANES
+        attn_sums = [total[:, cut : 2 * cut], total[:, :cut]]
+        feed_sums = [total[:, 2 * cut :], early.astype(F32)]
+    tokens_grad = upstream
 
     attn_sum = jnp.stack(attn_sums)
     feed_sum = jnp.stack(feed_sums)
@@ -685,8 +1014,13 @@
     send = jnp.concatenate([big, little], axis=2).astype(BF16)
     send = jnp.pad(send, ((0, per_dev * tok_count - units), (0, 0), (0, 0)))
     send = send.reshape(tok_count, per_dev, own_rows, 2 * group_width)
-    got = lax.all_to_all(send, "tok", 0, 0, tiled=True)
-    got = got.transpose(1, 0, 2, 3).reshape(per_dev, channels, 2 * group_width)
+    small_own = jnp.swapaxes(small_sum, 0, 1).reshape(own_rows, layers * small_rows)
+    small_own = jnp.pad(small_own, ((0, 0), (0, LANES - layers * small_rows))).astype(BF16)
+    small_own = jnp.broadcast_to(small_own, (tok_count, per_dev, own_rows, LANES))
+    got = lax.all_to_all(jnp.concatenate([send, small_own], axis=3), "tok", 0, 0, tiled=True)
+    got = got.transpose(1, 0, 2, 3).reshape(per_dev, channels, 2 * group_width + LANES)
+    small_all = got[0, :, 2 * group_width :].astype(F32).T[: layers * small_rows]
+    small_all = small_all.reshape(layers, small_rows, channels)
     ortho = run_schulz(got, group_width)
     ortho = ortho.reshape(per_dev, tok_count, own_rows, 2 * group_width).transpose(1, 0, 2, 3)
     ortho = lax.all_to_all(ortho, "tok", 0, 0, tiled=True)
@@ -721,8 +1055,6 @@
         new = weight - MUON_RATES[kind] * scales[kind] * turned
         results.extend([fresh, new, new.astype(BF16)])
 
-    small_all = lax.all_gather(small_sum.astype(BF16), "tok", axis=1, tiled=True)
-    small_all = jnp.swapaxes(small_all, 1, 2).astype(F32)
     norm_fresh, norm_new = normalized_step(
         norm_params, norm_moment, small_all[:, :4], SMALL_RATES[0], (2,)
     )

time: 1150 us -> 651 us (0.57)
  waiting for transfers between devices: 522 us -> 31 us
  Pallas kernels: 446 us -> 549 us
  local copies, waits for them, and re-layouts: 102 us -> 21.9 us
  blocking collectives: 21.1 us -> 0 us
    reduce_scatter x2 -> x1, waiting for transfers between devices: 258 us -> 7.63 us  [on_device(): lax.psum_scatter(gfeed.reshape(blk_count * channels, gfeed.shape[2]), bot...]
    reduce_scatter x2 -> x0, waiting for transfers between devices: 170 us -> none  [on_device(): lax.psum_scatter(grads.reshape(blk_count * channels, grads.shape[2]), bot...]
    pallas_call x6 -> x8, Pallas kernels: 251 us -> 354 us  [the longest x2 106 us: run_attend_forward(): pl.pallas_call(functools.partial(attend_forward, first=first), grid=(coun...]
    all_gather x4 -> x1, waiting for transfers between devices: 68.7 us -> 0.01 us  [gather(): full = lax.all_gather(piece, both, axis=0, tiled=True)]
    reshape x11 -> x3, local copies, waits for them, and re-layouts: 43.7 us -> 0.27 us  [the longest x2 0.18 us: on_device(): small_all = small_all.reshape(layers, small_rows, channels)]
    all_gather x1 -> x0, blocking collectives: 21.1 us -> none  [on_device(): lax.all_gather(small_sum.astype(BF16), 'tok', axis=1, tiled=True)]
    transpose x4 -> x3, local copies, waits for them, and re-layouts: 13.9 us -> 0.98 us  [the longest x1 0.91 us: on_device(): small_all = got[0, :, 2 * group_width:].astype(F32).T[:layers * small_rows]]
  transfers between devices with their start and end apart: 10 -> 4, of which waited for: 8 -> 3; matrix products, arithmetic and copies ran while one was open for 9% -> 3% of each run, Pallas kernels for 12% -> 34%
where the time goes in v2:
time: 651 us; the launch traced here: 648 us
  Pallas kernels  549 us (84%)
  waiting for transfers between devices  31 us (5%)
  local copies, waits for them, and re-layouts  21.9 us (3%)
  other arithmetic  17.2 us (3%)
  between operations  15 us (2%)
  starting transfers between devices  13.4 us (2%)
    pallas_call x2, Pallas kernels, run_attend_back(): pl.pallas_call(attend_back, grid=(count // ROWS,), in_specs=[block_of(cha...  185 us
    pallas_call x2, Pallas kernels, run_attend_forward(): pl.pallas_call(functools.partial(attend_forward, first=first), grid=(coun...  106 us
    pallas_call x2, Pallas kernels, run_feed_back(): pl.pallas_call(functools.partial(feed_back, first=first, chunk=chunk), gr...  84.7 us
    pallas_call x2, Pallas kernels, run_feed_forward(): pl.pallas_call(functools.partial(feed_forward, chunk=chunk), grid=(count...  64.8 us
    pallas_call x1, Pallas kernels, collect(): pl.pallas_call(functools.partial(collect_kernel, widths=widths), in_specs...  58.9 us
    pallas_call x1, Pallas kernels, spread(): pl.pallas_call(spread_kernel, in_specs=[pl.BlockSpec(memory_space=pl.ANY)...  39.8 us
    all_to_all x1, waiting for transfers between devices, on_device(): lax.all_to_all(jnp.concatenate([send, small_own], axis=3), 'tok', 0, 0, t...  13.6 us
  transfers between devices with their start and end apart: 4, of which 3 were waited for; matrix products, arithmetic and copies ran while one was open for 3% of the time, Pallas kernels for 34%

profile of v2, /device:TPU:0, one launch (start us, length us, event | category | flops | bytes accessed | tf_op | source)
XLA Modules:
  0.0 647.7 jit_solution(1695978660913809903)
XLA Ops:
  7.2 0.8 convert_bitcast_fusion.2
  8.1 0.9 convert.78
  9.5 1.0 convert_bitcast_fusion
  10.5 1.0 convert.76
  11.5 0.8 slice_bitcast_fusion.1
  12.3 39.8 %spread.1 = bf16[32,32,3072]{2,1,0:T(8,128)(2,1)} custom-call(bf16[32,3072]{1,0:T(8,128)(2,1)} %get-tuple-element.200.shard_ref), custom_call_target="tpu_custom_call" | custom-call | tf_op jit(solution)/shard_map/spread/pallas_call | solution.py:697
  53.8 0.9 reshape.334
  54.8 0.8 concatenate.56
  55.6 0.8 concatenate.55
  57.6 0.7 fusion.27
  58.3 1.5 broadcast_in_dim.48.refs_1_.refs_0_.mask_ref
  59.9 53.4 %attend_forward.2 = (f32[2624,512]{1,0:T(8,128)}, f32[2624,512]{1,0:T(8,128)}, bf16[2624,1536]{1,0:T(8,128)(2,1)}, bf16[2624,512]{1,0:T(8,128)(2,1)}, bf16[2624,512]{1,0:T(8,128)(2,1)}, /*index=5*/f32[2624,512]{1,0:T(8,128)}) custom-call(bf16[2624,512]{1,0:T(8,128)(2,1)} %refs_0_.1, f32[2624,128]{1,0:T(8,128)} %broadcast_in_dim.48.refs_1_.refs_0_.mask_ref, ...), custom_call_target="tpu_custom_call" | custom-call | flops 49999998976 | bytes 5000000 | tf_op jit(solution)/shard_map/attend_forward/pallas_call | solution.py:507
  113.3 32.2 %feed_forward.2 = (f32[2624,512]{1,0:T(8,128)}, bf16[2624,2048]{1,0:T(8,128)(2,1)}, bf16[2624,2048]{1,0:T(8,128)(2,1)}) custom-call(f32[2624,512]{1,0:T(8,128)} %get-tuple-element.58.att_ref.refs_1_, bf16[2,512,3072]{2,1,0:T(8,128)(2,1)} %bitcast.114, f32[4,512]{1,0:T(4,128)} %get-tuple-element.209.refs_3_.norm_ref.refs_5_), custom_call_target="tpu_custom_call" | custom-call | flops 32000000000 | bytes 3200000 | tf_op jit(solution)/shard_map/feed_forward/pallas_call | solution.py:531
  145.5 52.2 %attend_forward.3 = (f32[2624,512]{1,0:T(8,128)}, bf16[2624,1536]{1,0:T(8,128)(2,1)}, bf16[2624,512]{1,0:T(8,128)(2,1)}, bf16[2624,512]{1,0:T(8,128)(2,1)}, f32[2624,512]{1,0:T(8,128)}) custom-call(f32[2624,512]{1,0:T(8,128)} %get-tuple-element.59.refs_0_.x_ref, f32[2624,128]{1,0:T(8,128)} %broadcast_in_dim.48.refs_1_.refs_0_.mask_ref, ...), custom_call_target="tpu_custom_call" | custom-call | flops 49999998976 | bytes 5000000 | tf_op jit(solution)/shard_map/attend_forward/pallas_call | solution.py:507
  197.7 32.6 %feed_forward.3 = (bf16[2624,512]{1,0:T(8,128)(2,1)}, bf16[2624,2048]{1,0:T(8,128)(2,1)}, bf16[2624,2048]{1,0:T(8,128)(2,1)}) custom-call(f32[2624,512]{1,0:T(8,128)} %get-tuple-element.61.att_ref.refs_2_, bf16[2,512,3072]{2,1,0:T(8,128)(2,1)} %bitcast.144, f32[4,512]{1,0:T(4,128)} %get-tuple-element.208.refs_3_.norm_ref.refs_6_), custom_call_target="tpu_custom_call" | custom-call | flops 32000000000 | bytes 3200000 | tf_op jit(solution)/shard_map/feed_forward/pallas_call | solution.py:531
  230.2 43.3 %feed_back.2 = (f32[2624,512]{1,0:T(8,128)}, bf16[2,512,2048]{2,1,0:T(8,128)(2,1)}, f32[2,512]{1,0:T(2,128)}) custom-call(f32[2624,128]{1,0:T(8,128)} %broadcast_in_dim.48.refs_1_.refs_0_.mask_ref, f32[2624,512]{1,0:T(8,128)} %refs_1_.1, f32[2624,512]{1,0:T(8,128)} %get-tuple-element.61.att_ref.refs_2_, bf16[2624,2048]{1,0:T(8,128)(2,1)} %get-tuple-element.63.refs_3_, ...), custom_call_target="tpu_custom_call" | custom-call | flops 41000001536 | bytes 4100000 | tf_op jit(solution)/shard_map/feed_back/pallas_call | solution.py:553
  273.6 91.5 %attend_back.2 = (f32[2624,512]{1,0:T(8,128)}, bf16[2,512,1024]{2,1,0:T(8,128)(2,1)}, f32[2,512]{1,0:T(2,128)}, f32[9,8,512]{2,1,0:T(8,128)}, f32[49,8,512]{2,1,0:T(8,128)}) custom-call(f32[2624,512]{1,0:T(8,128)} %get-tuple-element.66.gatt_ref, f32[2624,512]{1,0:T(8,128)} %get-tuple-element.59.refs_0_.x_ref, f32[2624,512]{1,0:T(8,128)} %get-tuple-element.67.conv_ref, ...), custom_call_target="tpu_custom_call" | custom-call | flops 92000002048 | bytes 9200000 | tf_op jit(solution)/shard_map/attend_back/pallas_call | solution.py:580
  365.1 1.3 reduce_sum.71
  366.5 1.0 reduce_sum.70
  367.5 0.7 convert.80
  368.2 41.4 %feed_back.3 = (f32[2624,512]{1,0:T(8,128)}, bf16[2,512,2048]{2,1,0:T(8,128)(2,1)}, f32[2,512]{1,0:T(2,128)}) custom-call(f32[2624,512]{1,0:T(8,128)} %get-tuple-element.71.refs_0_, f32[2624,512]{1,0:T(8,128)} %get-tuple-element.58.att_ref.refs_1_, bf16[2624,2048]{1,0:T(8,128)(2,1)} %get-tuple-element.72.refs_2_, ...), custom_call_target="tpu_custom_call" | custom-call | flops 41000001536 | bytes 4100000 | tf_op jit(solution)/shard_map/feed_back/pallas_call | solution.py:553
  409.5 0.7 convert.85
  410.2 7.6 %reduce-scatter.2.cloned.1.call-done = bf16[32,2048]{1,0:T(8,128)(2,1)} async-done(((bf16[1024,2048]{1,0:T(8,128)(2,1)}), bf16[32,2048]{1,0:T(8,128)(2,1)}) %reduce-scatter.2.cloned.1.call-update) | async-done | bytes 131088 | tf_op jit(solution)/shard_map/reduce_scatter | solution.py:969
  417.8 93.9 %attend_back.3 = (f32[2624,512]{1,0:T(8,128)}, bf16[2,512,1024]{2,1,0:T(8,128)(2,1)}, f32[2,512]{1,0:T(2,128)}, f32[9,8,512]{2,1,0:T(8,128)}, f32[49,8,512]{2,1,0:T(8,128)}) custom-call(f32[2624,512]{1,0:T(8,128)} %get-tuple-element.75.gatt_ref, f32[2624,512]{1,0:T(8,128)} %get-tuple-element.76.x_ref, f32[2624,512]{1,0:T(8,128)} %get-tuple-element.77.conv_ref, ...), custom_call_target="tpu_custom_call" | custom-call | flops 92000002048 | bytes 9200000 | tf_op jit(solution)/shard_map/attend_back/pallas_call | solution.py:580
  511.7 1.3 reduce_sum.73
  513.1 1.0 reduce_sum.72
  514.0 0.7 convert.84
  515.1 0.7 broadcast_in_dim.52
  515.8 0.7 broadcast_in_dim.53
  516.5 58.9 %collect.1 = f32[32,4352]{1,0:T(8,128)} custom-call(bf16[32,32,1024]{2,1,0:T(8,128)(2,1)} %bitcast.125, bf16[32,32,128]{2,1,0:T(8,128)(2,1)} %bitcast.132, bf16[32,32,1024]{2,1,0:T(8,128)(2,1)} %bitcast.126, bf16[32,32,128]{2,1,0:T(8,128)(2,1)} %bitcast.133, bf16[32,32,2048]{2,1,0:T(8,128)(2,1)} %bitcast.117), custom_call_target="tpu_custom_call" | custom-call | tf_op jit(solution)/shard_map/collect/pallas_call | solution.py:799
  575.4 1.0 slice_bitcast_fusion.4
  576.8 1.0 slice_bitcast_fusion.14
  578.8 0.9 pad_maximum_fusion
  579.7 8.2 %all-to-all-start = ((bf16[16,1,32,640]{3,2,1,0:T(8,128)(2,1)}), bf16[16,1,32,640]{3,2,1,0:T(8,128)(2,1)S(1)}, u32[]{:S(2)}, u32[]{:S(2)}) async-start(bf16[16,1,32,640]{3,2,1,0:T(8,128)(2,1)} %pad_maximum_fusion), calls=%async_computation.1 | async-start | bytes 1310720 | tf_op jit(solution)/shard_map/all_to_all | solution.py:1020
  588.4 1.0 reshape.341
  590.1 0.8 slice_bitcast_fusion
  591.0 13.6 %all-to-all-done = bf16[16,1,32,640]{3,2,1,0:T(8,128)(2,1)S(1)} async-done(((bf16[16,1,32,640]{3,2,1,0:T(8,128)(2,1)}), bf16[16,1,32,640]{3,2,1,0:T(8,128)(2,1)S(1)}, u32[]{:S(2)}, u32[]{:S(2)}) %all-to-all-start) | async-done | bytes 655392 | tf_op jit(solution)/shard_map/all_to_all | solution.py:1020
  604.6 0.9 copy-done
  605.4 10.3 %schulz.1 = bf16[1,512,512]{2,1,0:T(8,128)(2,1)} custom-call(bf16[1,512,640]{2,1,0:T(8,128)(2,1)} %bitcast.119), custom_call_target="tpu_custom_call" | custom-call | tf_op jit(solution)/shard_map/schulz/pallas_call | solution.py:819
  615.7 0.9 slice_bitcast_fusion.5
  616.6 5.1 all-to-all-start.1
  623.7 0.8 copy.170
  624.8 0.8 copy.171
  625.7 0.7 divide_subtract_fusion.2
  626.4 9.7 %all-to-all-done.1 = bf16[16,1,32,512]{3,2,1,0:T(8,128)(2,1)S(1)} async-done(((bf16[16,1,32,512]{3,2,1,0:T(8,128)(2,1)}), bf16[16,1,32,512]{3,2,1,0:T(8,128)(2,1)S(1)}, u32[]{:S(2)}, u32[]{:S(2)}) %all-to-all-start.1) | async-done | bytes 524320 | tf_op jit(solution)/shard_map/all_to_all | solution.py:1026
  636.8 0.7 fusion.35
  638.8 0.8 fusion.33
  639.9 0.8 fusion.32
  (147 shorter events, 10.4 us)
Async XLA Ops:
  7.2 45.0 %copy-start.28 = (s32[64]{0:T(128)S(1)}, s32[64]{0:T(128)}, u32[]{:S(2)}) copy-start(s32[64]{0:T(128)} %param.19) | copy-start | bytes 772
  7.2 138.3 %all-gather.2.cloned.1.call-start = ((), (), s32[]{:S(2)}) async-start(), calls=%async_computation.3 | async-start | bytes 6488064 | tf_op jit(solution)/shard_map/all_gather | solution.py:904
  9.0 43.7 %copy-start.19 = (f32[2,9,512]{2,0,1:T(2,128)S(1)}, f32[2,9,512]{2,0,1:T(2,128)}, u32[]{:S(2)}) copy-start(f32[2,9,512]{2,0,1:T(2,128)} %param.25) | copy-start | bytes 110596
  9.3 44.0 %copy-start.11 = (f32[2,49,512]{2,0,1:T(2,128)S(1)}, f32[2,49,512]{2,0,1:T(2,128)}, u32[]{:S(2)}) copy-start(f32[2,49,512]{2,0,1:T(2,128)} %param.26) | copy-start | bytes 602116
  10.5 42.9 %copy-start.18 = (f32[2,32,768]{2,1,0:T(8,128)S(1)}, f32[2,32,768]{2,1,0:T(8,128)}, u32[]{:S(2)}) copy-start(f32[2,32,768]{2,1,0:T(8,128)} %param.27) | copy-start | bytes 589828
  12.3 42.4 %copy-start.5 = (f32[2,1024,32]{1,2,0:T(8,128)S(1)}, f32[2,1024,32]{1,2,0:T(8,128)}, u32[]{:S(2)}) copy-start(f32[2,1024,32]{1,2,0:T(8,128)} %param.30) | copy-start | bytes 786436
  12.3 43.3 %copy-start.7 = (f32[2,32,1024]{2,1,0:T(8,128)S(1)}, f32[2,32,1024]{2,1,0:T(8,128)}, u32[]{:S(2)}) copy-start(f32[2,32,1024]{2,1,0:T(8,128)} %param.29) | copy-start | bytes 786436
  12.3 44.1 %copy-start.22 = (f32[2,4,512]{2,1,0:T(4,128)S(1)}, f32[2,4,512]{2,1,0:T(4,128)}, u32[]{:S(2)}) copy-start(f32[2,4,512]{2,1,0:T(4,128)} %param.24) | copy-start | bytes 49156
  52.1 365.7 %reduce-scatter.2.cloned.1.call-start = ((), (), s32[]{:S(2)}) async-start(), calls=%async_computation.4 | async-start | bytes 4325376 | tf_op jit(solution)/shard_map/reduce_scatter | solution.py:969
  53.3 59.9 %copy-start.9 = (f32[49,512]{1,0:T(8,128)}, f32[49,512]{1,0:T(8,128)S(1)}, u32[]{:S(2)}) copy-start(f32[49,512]{1,0:T(8,128)S(1)} %reshape.330) | copy-start | bytes 301060
  273.6 93.9 %copy-start.27 = (f32[2,512]{1,0:T(2,128)S(1)}, f32[2,512]{1,0:T(2,128)}, u32[]{:S(2)}) copy-start(f32[2,512]{1,0:T(2,128)} %get-tuple-element.84) | copy-start | bytes 12292
  417.8 96.9 %copy-start.10 = (f32[49,512]{1,0:T(8,128)S(1)}, f32[49,512]{1,0:T(8,128)}, u32[]{:S(2)}) copy-start(f32[49,512]{1,0:T(8,128)} %copy-done.9) | copy-start | bytes 301060
  515.8 60.6 %copy-start.14 = (f32[2,32,768]{2,1,0:T(8,128)S(1)}, f32[2,32,768]{2,1,0:T(8,128)}, u32[]{:S(2)}) copy-start(f32[2,32,768]{2,1,0:T(8,128)} %reshape.334) | copy-start | bytes 589828
  515.8 60.6 %copy-start.24 = (f32[2,256,32]{1,2,0:T(8,128)S(1)}, f32[2,256,32]{1,2,0:T(8,128)}, u32[]{:S(2)}) copy-start(f32[2,256,32]{1,2,0:T(8,128)} %param.28) | copy-start | bytes 196612
  516.5 61.8 %copy-start.15 = (bf16[32,2048]{1,0:T(8,128)(2,1)S(1)}, bf16[32,2048]{1,0:T(8,128)(2,1)}, u32[]{:S(2)}) copy-start(bf16[32,2048]{1,0:T(8,128)(2,1)} %reduce-scatter.2.cloned.1.call-done) | copy-start | bytes 393220
  516.5 61.9 %copy-start.3 = (f32[2,32,4,256]{3,2,1,0:T(4,128)S(1)}, f32[2,32,4,256]{3,2,1,0:T(4,128)}, u32[]{:S(2)}) copy-start(f32[2,32,4,256]{3,2,1,0:T(4,128)} %concatenate.56) | copy-start | bytes 786436
  516.5 62.0 %copy-start.4 = (f32[2,32,4,256]{3,2,1,0:T(4,128)S(1)}, f32[2,32,4,256]{3,2,1,0:T(4,128)}, u32[]{:S(2)}) copy-start(f32[2,32,4,256]{3,2,1,0:T(4,128)} %concatenate.55) | copy-start | bytes 786436
  576.8 13.3 %copy-start.6 = (f32[2,1024,32]{1,2,0:T(8,128)S(1)}, f32[2,1024,32]{1,2,0:T(8,128)}, u32[]{:S(2)}) copy-start(f32[2,1024,32]{1,2,0:T(8,128)} %param.30) | copy-start | bytes 786436
  576.8 13.3 %copy-start.8 = (f32[2,32,1024]{2,1,0:T(8,128)S(1)}, f32[2,32,1024]{2,1,0:T(8,128)}, u32[]{:S(2)}) copy-start(f32[2,32,1024]{2,1,0:T(8,128)} %param.29) | copy-start | bytes 786436
  579.7 42.2 %copy-start.25 = (f32[2,9,512]{2,0,1:T(2,128)S(1)}, f32[2,9,512]{2,0,1:T(2,128)}, u32[]{:S(2)}) copy-start(f32[2,9,512]{2,0,1:T(2,128)} %param.32) | copy-start | bytes 110596
  579.7 42.4 %copy-start.17 = (f32[2,49,512]{2,0,1:T(2,128)S(1)}, f32[2,49,512]{2,0,1:T(2,128)}, u32[]{:S(2)}) copy-start(f32[2,49,512]{2,0,1:T(2,128)} %param.33) | copy-start | bytes 602116
  579.7 24.8 %all-to-all-start = ((bf16[16,1,32,640]{3,2,1,0:T(8,128)(2,1)}), bf16[16,1,32,640]{3,2,1,0:T(8,128)(2,1)S(1)}, u32[]{:S(2)}, u32[]{:S(2)}) async-start(bf16[16,1,32,640]{3,2,1,0:T(8,128)(2,1)} %pad_maximum_fusion), calls=%async_computation.1 | async-start | bytes 1310720 | tf_op jit(solution)/shard_map/all_to_all | solution.py:1020
  587.9 34.4 %copy-start.20 = (f32[2,9,512]{2,0,1:T(2,128)S(1)}, f32[2,9,512]{2,0,1:T(2,128)}, u32[]{:S(2)}) copy-start(f32[2,9,512]{2,0,1:T(2,128)} %param.25) | copy-start | bytes 110596
  588.0 36.7 %copy-start.12 = (f32[2,49,512]{2,0,1:T(2,128)S(1)}, f32[2,49,512]{2,0,1:T(2,128)}, u32[]{:S(2)}) copy-start(f32[2,49,512]{2,0,1:T(2,128)} %param.26) | copy-start | bytes 602116
  588.3 37.3 %copy-start.26 = (f32[2,4,512]{2,1,0:T(4,128)S(1)}, f32[2,4,512]{2,1,0:T(4,128)}, u32[]{:S(2)}) copy-start(f32[2,4,512]{2,1,0:T(4,128)} %param.31) | copy-start | bytes 49156
  588.4 37.4 %copy-start.23 = (f32[2,4,512]{2,1,0:T(4,128)S(1)}, f32[2,4,512]{2,1,0:T(4,128)}, u32[]{:S(2)}) copy-start(f32[2,4,512]{2,1,0:T(4,128)} %param.24) | copy-start | bytes 49156
  604.5 0.9 copy-start
  616.6 20.2 %copy-start.13 = (f32[2,32,768]{2,1,0:T(8,128)S(1)}, f32[2,32,768]{2,1,0:T(8,128)}, u32[]{:S(2)}) copy-start(f32[2,32,768]{2,1,0:T(8,128)} %param.20) | copy-start | bytes 589828
  616.6 19.5 %all-to-all-start.1 = ((bf16[16,1,32,512]{3,2,1,0:T(8,128)(2,1)}), bf16[16,1,32,512]{3,2,1,0:T(8,128)(2,1)S(1)}, u32[]{:S(2)}, u32[]{:S(2)}) async-start(bf16[16,1,32,512]{3,2,1,0:T(8,128)(2,1)} %bitcast.123), calls=%async_computation.2 | async-start | bytes 1048576 | tf_op jit(solution)/shard_map/all_to_all | solution.py:1026
  621.7 16.1 %copy-start.16 = (f32[2,256,32]{1,2,0:T(8,128)S(1)}, f32[2,256,32]{1,2,0:T(8,128)}, u32[]{:S(2)}) copy-start(f32[2,256,32]{1,2,0:T(8,128)} %param.21) | copy-start | bytes 196612
  622.4 16.4 %copy-start.1 = (f32[2,32,1024]{2,1,0:T(8,128)S(1)}, f32[2,32,1024]{2,1,0:T(8,128)}, u32[]{:S(2)}) copy-start(f32[2,32,1024]{2,1,0:T(8,128)} %param.22) | copy-start | bytes 786436
  625.7 14.2 %copy-start.21 = (f32[2,4,512]{2,1,0:T(4,128)}, f32[2,4,512]{2,1,0:T(4,128)S(1)}, u32[]{:S(2)}) copy-start(f32[2,4,512]{2,1,0:T(4,128)S(1)} %get-tuple-element.179) | copy-start | bytes 49156
  626.4 13.5 %copy-start.2 = (f32[2,1024,32]{1,2,0:T(8,128)S(1)}, f32[2,1024,32]{1,2,0:T(8,128)}, u32[]{:S(2)}) copy-start(f32[2,1024,32]{1,2,0:T(8,128)} %param.23) | copy-start | bytes 786436
Sparse Core Ops, SparseCore 0:
  52.2 72.5 all-gather.1
  273.7 144.0 reduce-scatter.1

commit v3 on v2

--- a/solution.py
+++ b/solution.py
@@ -66,45 +66,70 @@
 
 
 def grid_rows(row_at):
-    return pl.ds(pl.multiple_of((1 + SIDE * row_at) * IMGS, IMGS), SIDE * IMGS)
-
-
-def conv_row(padded_ref, kernel_ref, cols, row_at, pad, reach, width, flip):
+    return slice((1 + SIDE * row_at) * IMGS, (1 + SIDE * (row_at + 1)) * IMGS)
+
+
+def lane_pair(low, high):
+    cells = lambda tile: tile[IMGS:].reshape(SIDE, SIDE, IMGS, LANES)
+    return jnp.concatenate([cells(low), cells(high)], axis=2).astype(BF16)
+
+
+def split_pair(line):
+    line = line.astype(F32)
+    turn = lambda part: part.reshape(SIDE * IMGS, LANES)
+    return turn(line[:, :IMGS]), turn(line[:, IMGS:])
+
+
+def conv_row(cells_ref, kernel_ref, pair, row_at, reach, width, flip):
     mid = width // 2
-    acc = [None] * SIDE
+    total = [None] * SIDE
     for down in range(-reach, reach + 1):
-        line = padded_ref[row_at + pad + down]
+        if not 0 <= row_at + down < SIDE:
+            continue
+        line = cells_ref[row_at + down]
+        acc = [None] * SIDE
         for along in range(-reach, reach + 1):
             tap = (mid - down, mid - along) if flip else (mid + down, mid + along)
-            weight = kernel_ref[pl.ds(tap[0] * width + tap[1], 1), cols]
-            weight = jnp.broadcast_to(weight, (IMGS, LANES))
+            weight = kernel_ref[pair, tap[0] * width + tap[1]]
             for col in range(SIDE):
                 if 0 <= col + along < SIDE:
                     term = line[col + along] * weight
                     acc[col] = term if acc[col] is None else acc[col] + term
-    return jnp.concatenate(acc, axis=0)
-
-
-def conv_kernel_grad(grad_ref, padded_ref, total_ref, cols, pad, reach, width, grad_pad):
+        total = [new if old is None else old + new for old, new in zip(total, acc)]
+    return jnp.stack(total, axis=0)
+
+
+def conv_kernel_grad(grad_ref, cells_ref, total_ref, pair, reach, width):
     mid = width // 2
-
-    def one(step, carry):
-        down = step - reach
-        acc = [None] * (2 * reach + 1)
-        for row_at in range(SIDE):
-            grad_line = grad_ref[row_at + grad_pad]
-            line = padded_ref[row_at + pad + down]
-            for along in range(-reach, reach + 1):
-                for col in range(SIDE):
-                    if 0 <= col + along < SIDE:
-                        term = grad_line[col] * line[col + along]
-                        at = along + reach
-                        acc[at] = term if acc[at] is None else acc[at] + term
+    for down in range(-reach, reach + 1):
+        rows = [at for at in range(SIDE) if 0 <= at + down < SIDE]
+        whole_sum = [None] * (2 * reach + 1)
+        for start in range(0, len(rows), 3):
+            acc = [None] * (2 * reach + 1)
+            for row_at in rows[start : start + 3]:
+                grad_line = grad_ref[row_at]
+                line = cells_ref[row_at + down]
+                for along in range(-reach, reach + 1):
+                    for col in range(SIDE):
+                        if 0 <= col + along < SIDE:
+                            term = grad_line[col] * line[col + along]
+                            at = along + reach
+                            acc[at] = term if acc[at] is None else acc[at] + term
+            acc = [value.astype(F32) for value in acc]
+            whole_sum = [new if old is None else old + new for old, new in zip(whole_sum, acc)]
         for along in range(-reach, reach + 1):
-            total_ref[(mid + down) * width + mid + along, :, cols] += acc[along + reach]
-        return carry
-
-    lax.fori_loop(0, 2 * reach + 1, one, 0)
+            tap = (mid + down) * width + mid + along
+            value = whole_sum[along + reach]
+            total_ref[tap, :, lane(2 * pair)] += value[:IMGS]
+            total_ref[tap, :, lane(2 * pair + 1)] += value[IMGS:]
+
+
+def pair_kernel(kernel):
+    taps, channels = kernel.shape
+    kernel = kernel.reshape(taps, channels // (2 * LANES), 2, 1, LANES)
+    kernel = jnp.broadcast_to(kernel, (taps, channels // (2 * LANES), 2, IMGS, LANES))
+    kernel = kernel.transpose(1, 0, 2, 3, 4).astype(BF16)
+    return kernel.reshape(channels // (2 * LANES), taps, 2 * IMGS, LANES)
 
 
 def key_softmax(key_tile, mask_tile):
@@ -146,20 +171,15 @@
     if first:
         tokens_ref, refs = refs[0], refs[1:]
         (mask_ref, w_ref, norm_ref, cpe_ref, crpe_ref, x_ref, conv_ref, packed_ref, rel_ref,
-         mixed_ref, att_ref, x_pad, v_pad, q_s, k_s, v_s, f_s, c_s) = refs
+         mixed_ref, att_ref, x_cells, v_cells, q_s, k_s, v_s, f_s, c_s) = refs
     else:
         (x_ref, mask_ref, w_ref, norm_ref, cpe_ref, crpe_ref, conv_ref, packed_ref, rel_ref,
-         mixed_ref, att_ref, x_pad, v_pad, q_s, k_s, v_s, f_s, c_s) = refs
+         mixed_ref, att_ref, x_cells, v_cells, q_s, k_s, v_s, f_s, c_s) = refs
     channels = x_ref.shape[1]
     tiles = channels // LANES
     head_dim = channels // HEADS
     half = channels // 2
 
-    @pl.when(pl.program_id(0) == 0)
-    def _():
-        x_pad[...] = jnp.zeros_like(x_pad)
-        v_pad[...] = jnp.zeros_like(v_pad)
-
     if first:
         for at in range(tiles):
             cols = lane(at)
@@ -169,20 +189,17 @@
                 x_ref[rows, cols] = values
 
             to_token_major(f_s.at[at], put)
-    mask = mask_ref[...]
-    for at in range(tiles):
-        cols = lane(at)
-        masked = x_ref[:, cols] * mask
-        x_pad[1 : 1 + SIDE] = masked[IMGS:].reshape(SIDE, SIDE, IMGS, LANES)
-        conv_ref[:IMGS, cols] = x_ref[:IMGS, cols]
-
-        def conv_step(row_at, carry):
+    for pair in range(tiles // 2):
+        both = (lane(2 * pair), lane(2 * pair + 1))
+        mask = mask_ref[...]
+        x_cells[...] = lane_pair(*[x_ref[:, cols] * mask for cols in both])
+        for cols in both:
+            conv_ref[:IMGS, cols] = x_ref[:IMGS, cols]
+        for row_at in range(SIDE):
             rows = grid_rows(row_at)
-            out = conv_row(x_pad, cpe_ref, cols, row_at, 1, 1, 3, False)
-            conv_ref[rows, cols] = x_ref[rows, cols] + out * mask_ref[rows, :]
-            return carry
-
-        lax.fori_loop(0, SIDE, conv_step, 0)
+            out = split_pair(conv_row(x_cells, cpe_ref, pair, row_at, 1, 3, False))
+            for cols, value in zip(both, out):
+                conv_ref[rows, cols] = x_ref[rows, cols] + value * mask_ref[rows, :]
     unit, _ = normalize(conv_ref[...])
     normed = (unit * norm_ref[0:1, :] + norm_ref[1:2, :]).astype(BF16)
     for side in range(2):
@@ -206,24 +223,22 @@
             put_image_rows(f_s, quad, image, mm(query, context))
         return carry
 
-    lax.fori_loop(0, IMGS, one_image, 0)
-    for at in range(tiles):
-        cols = lane(at)
-        masked = v_s[at] * mask_ref[...]
-        v_pad[3 : 3 + SIDE] = masked[IMGS:].reshape(SIDE, SIDE, IMGS, LANES)
-        c_s[:IMGS, :] = jnp.zeros((IMGS, LANES), F32)
-        reach = tile_radius(at, head_dim)
-
-        def rel_step(row_at, carry):
+    lax.fori_loop(0, IMGS, one_image, 0, unroll=True)
+    c_s[:, :IMGS, :] = jnp.zeros((2, IMGS, LANES), F32)
+    for pair in range(tiles // 2):
+        mask = mask_ref[...]
+        v_cells[...] = lane_pair(v_s[2 * pair] * mask, v_s[2 * pair + 1] * mask)
+        reach = tile_radius(2 * pair + 1, head_dim)
+        for row_at in range(SIDE):
             rows = grid_rows(row_at)
-            out = conv_row(v_pad, crpe_ref, cols, row_at, 3, reach, 7, False)
-            c_s[rows, :] = out * mask_ref[rows, :]
-            return carry
-
-        lax.fori_loop(0, SIDE, rel_step, 0)
-        rel = c_s[...]
-        rel_ref[:, cols] = rel.astype(BF16)
-        mixed_ref[:, cols] = (f_s[at] + q_s[at] * rel).astype(BF16)
+            out = split_pair(conv_row(v_cells, crpe_ref, pair, row_at, reach, 7, False))
+            for half_at, value in enumerate(out):
+                c_s[half_at, rows, :] = value * mask_ref[rows, :]
+        for half_at in range(2):
+            at = 2 * pair + half_at
+            rel = c_s[half_at]
+            rel_ref[:, lane(at)] = rel.astype(BF16)
+            mixed_ref[:, lane(at)] = (f_s[at] + q_s[at] * rel).astype(BF16)
     out = conv_ref[...]
     for side in range(2):
         cols = slice(side * half, (side + 1) * half)
@@ -231,21 +246,25 @@
     att_ref[...] = out
 
 
-def gelu_parts(values):
-    size = jnp.abs(values)
-    t = 1.0 / (1.0 + (0.3275911 * 0.7071067811865476) * size)
-    bell = jnp.exp(-0.5 * values * values)
-    poly = 0.5 * 1.061405429
+def gelu_parts(hidden):
+    number = lambda value: jnp.asarray(value, BF16)
+    values = hidden.astype(BF16)
+    t = pl.reciprocal(
+        number(1.0) + number(0.3275911 * 0.7071067811865476) * jnp.abs(values), approx=True
+    )
+    bell = jnp.exp2(number(-0.5 * 1.4426950408889634) * (values * values))
+    poly = number(0.5 * 1.061405429)
     for coef in (-1.453152027, 1.421413741, -0.284496736, 0.254829592):
-        poly = poly * t + 0.5 * coef
+        poly = poly * t + number(0.5 * coef)
     tail = poly * t * bell
-    phi = jnp.where(values >= 0, 1.0 - tail, tail)
-    return values * phi, phi + (values * 0.3989422804014327) * bell
+    phi = jnp.where(values >= 0, number(1.0) - tail, tail)
+    return values * phi, phi + (values * number(0.3989422804014327)) * bell
 
 
 def feed_forward(att_ref, up_down_ref, norm_ref, out_ref, act_ref, slope_ref, *scratch, chunk):
     blks, _, both = up_down_ref.shape
     width = both // 2
+    chunk = min(chunk, width)
     att = att_ref[...]
     unit, _ = normalize(att)
     normed = (unit * norm_ref[2:3, :] + norm_ref[3:4, :]).astype(BF16)
@@ -254,10 +273,9 @@
         for at in range(0, width, chunk):
             hidden = mm(normed, up_down_ref[blk, :, at : at + chunk])
             active, slope = gelu_parts(hidden)
-            active = active.astype(BF16)
             cols = slice(blk * width + at, blk * width + at + chunk)
             act_ref[:, cols] = active
-            slope_ref[:, cols] = slope.astype(BF16)
+            slope_ref[:, cols] = slope
             total = total + mm_nt(active, up_down_ref[blk, :, width + at : width + at + chunk])
     if not scratch:
         out_ref[...] = total
@@ -282,6 +300,7 @@
     step, steps = pl.program_id(0), pl.num_programs(0)
     blks, _, both = up_down_ref.shape
     width = both // 2
+    chunk = min(chunk, width)
 
     @pl.when(step == 0)
     def _():
@@ -331,7 +350,7 @@
     gatt_ref, x_ref, conv_ref, packed_ref, rel_ref, mixed_ref, mask_ref,
     w_ref, norm_ref, cpe_ref, crpe_ref,
     out_ref, gw_ref, gnorm_ref, gcpe_ref, gcrpe_ref,
-    w_s, x_pad, g_pad, v_pad, c_pad, q_s, k_s, v_s, f_s, dq_s, dk_s, dv_s, c_s, gp_s,
+    w_s, x_cells, g_cells, v_cells, c_cells, q_s, k_s, v_s, f_s, dq_s, dk_s, dv_s, c_s, gp_s,
     *scratch,
 ):
     channels = x_ref.shape[1]
@@ -343,7 +362,7 @@
 
     @pl.when(step == 0)
     def _():
-        for ref in (x_pad, g_pad, v_pad, c_pad, w_s, gnorm_ref, gcpe_ref, gcrpe_ref):
+        for ref in (w_s, gnorm_ref, gcpe_ref, gcrpe_ref):
             ref[...] = jnp.zeros_like(ref)
 
     att_in = gatt_ref[...].astype(BF16)
@@ -375,35 +394,34 @@
             put_image_rows(dv_s, quad, image, mm(keys, grad_context))
         return carry
 
-    lax.fori_loop(0, IMGS, one_image, 0)
-    for at in range(tiles):
-        cols = lane(at)
-        start = (3 * (at // (tiles // 2))) * half + (at % (tiles // 2)) * LANES
-        place = lambda third: slice(start + third * half, start + third * half + LANES)
+    lax.fori_loop(0, IMGS, one_image, 0, unroll=True)
+    for pair in range(tiles // 2):
         mask = mask_ref[...]
-        weights = k_s[at]
-        share = weights * dk_s[at]
-        total = jnp.sum(share.reshape(SLOT, IMGS, LANES), axis=0, keepdims=True)
-        back = share.reshape(SLOT, IMGS, LANES) - weights.reshape(SLOT, IMGS, LANES) * total
-        gp_s[:, place(1)] = back.reshape(ROWS, LANES).astype(BF16)
-        grads = f_s[at]
-        gp_s[:, place(0)] = (dq_s[at] + grads * rel_ref[:, cols].astype(F32)).astype(BF16)
-        reach = tile_radius(at, head_dim)
-        masked = v_s[at] * mask
-        v_pad[3 : 3 + SIDE] = masked[IMGS:].reshape(SIDE, SIDE, IMGS, LANES)
-        cgrad = grads * q_s[at] * mask
-        c_pad[3 : 3 + SIDE] = cgrad[IMGS:].reshape(SIDE, SIDE, IMGS, LANES)
-        c_s[:IMGS, :] = dv_s[at, :IMGS, :]
-
-        def rel_step(row_at, carry):
+        place = lambda at, third: slice(
+            (3 * pair + third) * half + at * LANES, (3 * pair + third) * half + (at + 1) * LANES
+        )
+        for half_at in range(2):
+            at = 2 * pair + half_at
+            weights = k_s[at]
+            share = weights * dk_s[at]
+            total = jnp.sum(share.reshape(SLOT, IMGS, LANES), axis=0, keepdims=True)
+            back = share.reshape(SLOT, IMGS, LANES) - weights.reshape(SLOT, IMGS, LANES) * total
+            gp_s[:, place(half_at, 1)] = back.reshape(ROWS, LANES).astype(BF16)
+            rel = rel_ref[:, lane(at)].astype(F32)
+            gp_s[:, place(half_at, 0)] = (dq_s[at] + f_s[at] * rel).astype(BF16)
+        reach = tile_radius(2 * pair + 1, head_dim)
+        v_cells[...] = lane_pair(v_s[2 * pair] * mask, v_s[2 * pair + 1] * mask)
+        c_cells[...] = lane_pair(
+            *[f_s[at] * q_s[at] * mask for at in (2 * pair, 2 * pair + 1)]
+        )
+        for row_at in range(SIDE):
             rows = grid_rows(row_at)
-            out = conv_row(c_pad, crpe_ref, cols, row_at, 3, reach, 7, True)
-            c_s[rows, :] = dv_s[at, rows, :] + out * mask_ref[rows, :]
-            return carry
-
-        lax.fori_loop(0, SIDE, rel_step, 0)
-        conv_kernel_grad(c_pad, v_pad, gcrpe_ref, cols, 3, reach, 7, 3)
-        gp_s[:, place(2)] = c_s[...].astype(BF16)
+            out = split_pair(conv_row(c_cells, crpe_ref, pair, row_at, reach, 7, True))
+            for half_at, value in enumerate(out):
+                dv_s[2 * pair + half_at, rows, :] += value * mask_ref[rows, :]
+        conv_kernel_grad(c_cells, v_cells, gcrpe_ref, pair, reach, 7)
+        for half_at in range(2):
+            gp_s[:, place(half_at, 2)] = dv_s[2 * pair + half_at].astype(BF16)
     unit, inv = normalize(conv_ref[...])
     gain = norm_ref[0:1, :]
     normed_t = (unit * gain + norm_ref[1:2, :]).astype(BF16).T
@@ -416,29 +434,25 @@
     gnorm_ref[0:1, :] += jnp.sum(grad_rows * unit, axis=0, keepdims=True)
     gnorm_ref[1:2, :] += jnp.sum(grad_rows, axis=0, keepdims=True)
     up_ref[...] = gatt_ref[...] + norm_back(grad_rows, unit, inv, gain)
-    for at in range(tiles):
+    for pair in range(tiles // 2):
+        both = (lane(2 * pair), lane(2 * pair + 1))
+        mask = mask_ref[...]
+        x_cells[...] = lane_pair(*[x_ref[:, cols] * mask for cols in both])
+        g_cells[...] = lane_pair(*[up_ref[:, cols] * mask for cols in both])
+        for row_at in range(SIDE):
+            rows = grid_rows(row_at)
+            out = split_pair(conv_row(g_cells, cpe_ref, pair, row_at, 1, 3, True))
+            for cols, value in zip(both, out):
+                up_ref[rows, cols] += value * mask_ref[rows, :]
+        conv_kernel_grad(g_cells, x_cells, gcpe_ref, pair, 1, 3)
+    for at in range(tiles if scratch else 0):
         cols = lane(at)
-        mask = mask_ref[...]
-        masked = x_ref[:, cols] * mask
-        x_pad[1 : 1 + SIDE] = masked[IMGS:].reshape(SIDE, SIDE, IMGS, LANES)
-        gmasked = up_ref[:, cols] * mask
-        g_pad[1 : 1 + SIDE] = gmasked[IMGS:].reshape(SIDE, SIDE, IMGS, LANES)
-
-        def conv_step(row_at, carry):
-            rows = grid_rows(row_at)
-            out = conv_row(g_pad, cpe_ref, cols, row_at, 1, 1, 3, True)
-            up_ref[rows, cols] += out * mask_ref[rows, :]
-            return carry
-
-        lax.fori_loop(0, SIDE, conv_step, 0)
-        conv_kernel_grad(g_pad, x_pad, gcpe_ref, cols, 1, 1, 3, 1)
-        if scratch:
-            c_s[...] = up_ref[:, cols]
-
-            def put(rows, values, cols=cols):
-                out_ref[rows, cols] = values
-
-            to_image_major(c_s, put)
+        c_s[...] = up_ref[:, cols]
+
+        def put(rows, values, cols=cols):
+            out_ref[rows, cols] = values
+
+        to_image_major(c_s, put)
 
     @pl.when(step == steps - 1)
     def _():
@@ -501,6 +515,7 @@
     count, channels = x.shape
     tiles = channels // LANES
     flat = pltpu.VMEM((tiles, ROWS, LANES), F32)
+    cells = pltpu.VMEM((SIDE, SIDE, 2 * IMGS, LANES), BF16)
     out = lambda cols, kind: jax.ShapeDtypeStruct((count, cols), kind)
     outs = [out(channels, F32), out(3 * channels, BF16)] + [out(channels, BF16)] * 2
     outs = [out(channels, F32)] * first + outs + [out(channels, F32)]
@@ -513,10 +528,8 @@
         out_specs=[block_of(array.shape[1]) for array in outs],
         out_shape=outs,
         scratch_shapes=[
-            pltpu.VMEM((SIDE + 2, SIDE, IMGS, LANES), F32),
-            pltpu.VMEM((SIDE + 6, SIDE, IMGS, LANES), F32),
-            flat, flat, flat, flat,
-            pltpu.VMEM((ROWS, LANES), F32),
+            cells, cells, flat, flat, flat, flat,
+            pltpu.VMEM((2, ROWS, LANES), F32),
         ],
         compiler_params=params_for(),
         cost_estimate=cost(50),
@@ -524,7 +537,7 @@
     )(x, mask, weights[0], norm, cpe, crpe)
 
 
-def run_feed_forward(att, up_down, norm, last, chunk=256):
+def run_feed_forward(att, up_down, norm, last, chunk=512):
     count, channels = att.shape
     hidden = up_down[0].shape[0] * up_down[1] // 2
     turn = [pltpu.VMEM((ROWS, LANES), F32), pltpu.VMEM((ROWS, channels), F32)]
@@ -545,7 +558,7 @@
     )(att, up_down[0], norm)
 
 
-def run_feed_back(mask, upstream, att, active, slope, up_down, norm, first, chunk=256):
+def run_feed_back(mask, upstream, att, active, slope, up_down, norm, first, chunk=512):
     count, channels = att.shape
     hidden = active.shape[1]
     turn = [pltpu.VMEM((ROWS, LANES), F32), pltpu.VMEM((ROWS, channels), F32)]
@@ -573,8 +586,7 @@
     count, channels = x.shape
     tiles = channels // LANES
     flat = pltpu.VMEM((tiles, ROWS, LANES), F32)
-    three = pltpu.VMEM((SIDE + 2, SIDE, IMGS, LANES), F32)
-    seven = pltpu.VMEM((SIDE + 6, SIDE, IMGS, LANES), F32)
+    cells = pltpu.VMEM((SIDE, SIDE, 2 * IMGS, LANES), BF16)
     small = [(2, channels), (9, IMGS, channels), (49, IMGS, channels)]
     shape = weights[0].shape[:2] + (weights[1],)
     return pl.pallas_call(
@@ -593,7 +605,7 @@
         + [jax.ShapeDtypeStruct(each, F32) for each in small],
         scratch_shapes=[
             pltpu.VMEM(shape, F32),
-            three, three, seven, seven,
+            cells, cells, cells, cells,
             flat, flat, flat, flat, flat, flat, flat,
             pltpu.VMEM((ROWS, LANES), F32),
             pltpu.VMEM((ROWS, 3 * channels), BF16),
@@ -756,32 +768,39 @@
         ref[...] = total.astype(BF16)
 
     me = (y, x)
-    order = [(cross, 0), (second, 1), (first, 2), (me, 3)]
-    theirs = {0: 0, 1: 2, 2: 1, 3: 3}
-    for place, kind in order:
-        for d in range(4):
+    places = (cross, first, second, me)
+    theirs = (0, 2, 1, 3)
+    turns = (2, 1, 3, 0)
+    for d in turns:
+        for kind in (0, 2, 1, 3):
             number = theirs[kind] * 4 + d
-            send(own_s.at[slot(place, line[d], 1 - core)], chip_s.at[number], to_core, number)
-    for place, kind, there in ((cross, 0, 0), (second, 1, 4)):
-        for d in range(4):
-            here = chip_s.at[kind * 4 + d]
-            arrive(here, kind * 4 + d)
-            add(here, own_s.at[slot(place, line[d], core)])
+            send(own_s.at[slot(places[kind], line[d], 1 - core)], chip_s.at[number], to_core, number)
+
+    def fold(kind, d):
+        here = chip_s.at[kind * 4 + d]
+        arrive(here, kind * 4 + d)
+        own = own_s.at[slot(places[kind], line[d], core)]
+        if kind in (0, 2):
+            there = 0 if kind == 0 else 4
+            add(here, own)
             send(here, second_s.at[there + d], to_second, 16 + there + d)
-    for d in range(4):
-        here = chip_s.at[8 + d]
-        arrive(here, 8 + d)
-        arrive(second_s.at[d], 16 + d)
-        add(here, own_s.at[slot(first, line[d], core)], second_s.at[d])
-        send(here, first_s.at[d], to_first, 24 + d)
-    for d in (1, 2, 3, 0):
-        here = chip_s.at[12 + d]
-        arrive(here, 12 + d)
-        arrive(second_s.at[4 + d], 20 + d)
-        arrive(first_s.at[d], 24 + d)
-        if d:
-            add(here, own_s.at[slot(me, line[d], core)], second_s.at[4 + d], first_s.at[d])
-            send(here, line_s.at[d - 1], device_at(y, line[d], x, core), 27 + d)
+        elif kind == 1:
+            arrive(second_s.at[d], 16 + d)
+            add(here, own, second_s.at[d])
+            send(here, first_s.at[d], to_first, 24 + d)
+        else:
+            arrive(second_s.at[4 + d], 20 + d)
+            arrive(first_s.at[d], 24 + d)
+            if d:
+                add(here, own, second_s.at[4 + d], first_s.at[d])
+                send(here, line_s.at[d - 1], device_at(y, line[d], x, core), 27 + d)
+
+    stages = [(0, 2), (1,), (3,)]
+    for turn in range(len(turns) + 2):
+        for stage, kinds in enumerate(stages):
+            if 0 <= turn - stage < len(turns):
+                for kind in kinds:
+                    fold(kind, turns[turn - stage])
     for d in (1, 2, 3):
         arrive(line_s.at[d - 1], 27 + d)
     total = chip_s[12].astype(F32) + own_s[slot(me, z, core)].astype(F32)
@@ -938,32 +957,30 @@
     stream = tokens
     saved = []
     for layer in range(layers):
-        crpe = crpe_weight[layer] * taps
+        cpe, crpe = pair_kernel(cpe_weight[layer]), pair_kernel(crpe_weight[layer] * taps)
         outs = run_attend_forward(
-            stream, mask, attn_all[layer], norm_params[layer], cpe_weight[layer], crpe, layer == 0
+            stream, mask, attn_all[layer], norm_params[layer], cpe, crpe, layer == 0
         )
         if layer:
             outs = [stream] + list(outs)
         stream, active, slope = run_feed_forward(
             outs[-1], feed_all[layer], norm_params[layer], layer == layers - 1
         )
-        saved.append(tuple(outs) + (active, slope, crpe))
+        saved.append(tuple(outs) + (active, slope, cpe, crpe))
     block_out = stream
 
     upstream = cotangent
     attn_sums, feed_sums = [None] * layers, [None] * layers
     small_rows = 4 + 9 + 49
     for layer in reversed(range(layers)):
-        x, conv, packed, rel, mixed, att, active, slope, crpe = saved[layer]
+        x, conv, packed, rel, mixed, att, active, slope, cpe, crpe = saved[layer]
         gatt, gfeed, gmid = run_feed_back(
             mask, upstream, att, active, slope, feed_all[layer], norm_params[layer],
             layer == layers - 1,
         )
-        if near and layer == 0:
-            early, gatt = lax.optimization_barrier((early, gatt))
         upstream, gattn, gfront, gcpe, gcrpe = run_attend_back(
             gatt, x, conv, packed, rel, mixed, mask, attn_all[layer],
-            norm_params[layer], cpe_weight[layer], crpe, layer == 0,
+            norm_params[layer], cpe, crpe, layer == 0,
         )
         if near and layer == layers - 1:
             early = lax.psum_scatter(
@@ -984,6 +1001,7 @@
             feed_sums[layer] = scatter(pieces[2])
             attn_sums[layer] = scatter(jnp.concatenate(pieces[:2], axis=2))
     if near:
+        early, waiting = lax.optimization_barrier((early, waiting))
         total = collect(waiting, 2)
         cut = attn_cols + LANES
         attn_sums = [total[:, cut : 2 * cut], total[:, :cut]]

time: 651 us -> 518 us (0.80)
  Pallas kernels: 549 us -> 424 us
    pallas_call x2, Pallas kernels: 185 us -> 135 us  [run_attend_back(): pl.pallas_call(attend_back, grid=(count // ROWS,), in_specs=[block_of(cha...]
    pallas_call x2, Pallas kernels: 106 us -> 68.1 us  [run_attend_forward(): pl.pallas_call(functools.partial(attend_forward, first=first), grid=(coun...]
    pallas_call x2, Pallas kernels: 64.8 us -> 47.5 us  [run_feed_forward(): pl.pallas_call(functools.partial(feed_forward, chunk=chunk), grid=(count...]
    pallas_call x2, Pallas kernels: 84.7 us -> 73.3 us  [run_feed_back(): pl.pallas_call(functools.partial(feed_back, first=first, chunk=chunk), gr...]
    pallas_call x1, Pallas kernels: 58.9 us -> 49.7 us  [collect(): pl.pallas_call(functools.partial(collect_kernel, widths=widths), in_specs...]
    reduce_scatter x1, waiting for transfers between devices: 7.63 us -> 0.02 us  [on_device(): lax.psum_scatter(gfeed.reshape(blk_count * channels, gfeed.shape[2]), bot...]
  transfers between devices with their start and end apart: 4 -> 4, of which waited for: 3 -> 3; matrix products, arithmetic and copies ran while one was open for 3% -> 4% of each run, Pallas kernels for 34% -> 45%
where the time goes in v3:
time: 518 us; the launch traced here: 515 us
  Pallas kernels  424 us (82%)
  waiting for transfers between devices  27.4 us (5%)
  local copies, waits for them, and re-layouts  25.2 us (5%)
  between operations  15.1 us (3%)
  other arithmetic  13.1 us (3%)
  starting transfers between devices  9.97 us (2%)
    pallas_call x2, Pallas kernels, run_attend_back(): pl.pallas_call(attend_back, grid=(count // ROWS,), in_specs=[block_of(cha...  135 us
    pallas_call x2, Pallas kernels, run_feed_back(): pl.pallas_call(functools.partial(feed_back, first=first, chunk=chunk), gr...  73.3 us
    pallas_call x2, Pallas kernels, run_attend_forward(): pl.pallas_call(functools.partial(attend_forward, first=first), grid=(coun...  68.1 us
    pallas_call x1, Pallas kernels, collect(): pl.pallas_call(functools.partial(collect_kernel, widths=widths), in_specs...  49.7 us
    pallas_call x2, Pallas kernels, run_feed_forward(): pl.pallas_call(functools.partial(feed_forward, chunk=chunk), grid=(count...  47.5 us
    pallas_call x1, Pallas kernels, spread(): pl.pallas_call(spread_kernel, in_specs=[pl.BlockSpec(memory_space=pl.ANY)...  39.8 us
    all_to_all x1, waiting for transfers between devices, on_device(): lax.all_to_all(jnp.concatenate([send, small_own], axis=3), 'tok', 0, 0, t...  13.6 us
  transfers between devices with their start and end apart: 4, of which 3 were waited for; matrix products, arithmetic and copies ran while one was open for 4% of the time, Pallas kernels for 45%

profile of v3, /device:TPU:0, one launch (start us, length us, event | category | flops | bytes accessed | tf_op | source)
XLA Modules:
  0.0 514.6 jit_solution(10385825922496918529)
XLA Ops:
  7.2 0.8 convert_bitcast_fusion.2
  8.1 0.9 convert.82
  9.5 1.0 convert_bitcast_fusion
  10.5 1.0 convert.80
  11.5 0.8 slice_bitcast_fusion.1
  12.3 39.8 %spread.1 = bf16[32,32,3072]{2,1,0:T(8,128)(2,1)} custom-call(bf16[32,3072]{1,0:T(8,128)(2,1)} %get-tuple-element.210.shard_ref), custom_call_target="tpu_custom_call" | custom-call | tf_op jit(solution)/shard_map/spread/pallas_call | solution.py:709
  52.8 0.8 reshape.376
  54.7 0.9 reshape.373
  55.6 0.8 concatenate.56
  56.5 0.8 concatenate.55
  57.9 0.7 broadcast_bitcast_fusion.3.refs_4_.cpe_ref
  58.5 0.7 broadcast_bitcast_fusion.2.refs_4_.cpe_ref
  59.5 0.9 broadcast_bitcast_fusion.1.refs_5_.crpe_ref
  60.3 0.8 broadcast_bitcast_fusion.refs_5_.crpe_ref
  61.1 1.5 broadcast_in_dim.68.refs_1_.refs_0_.mask_ref
  62.6 35.1 %attend_forward.2 = (f32[2624,512]{1,0:T(8,128)}, f32[2624,512]{1,0:T(8,128)}, bf16[2624,1536]{1,0:T(8,128)(2,1)}, bf16[2624,512]{1,0:T(8,128)(2,1)}, bf16[2624,512]{1,0:T(8,128)(2,1)}, /*index=5*/f32[2624,512]{1,0:T(8,128)}) custom-call(bf16[2624,512]{1,0:T(8,128)(2,1)} %refs_0_.1, f32[2624,128]{1,0:T(8,128)} %broadcast_in_dim.68.refs_1_.refs_0_.mask_ref, ...), custom_call_target="tpu_custom_call" | custom-call | flops 49999998976 | bytes 5000000 | tf_op jit(solution)/shard_map/attend_forward/pallas_call | solution.py:522
  97.7 23.2 %feed_forward.2 = (f32[2624,512]{1,0:T(8,128)}, bf16[2624,2048]{1,0:T(8,128)(2,1)}, bf16[2624,2048]{1,0:T(8,128)(2,1)}) custom-call(f32[2624,512]{1,0:T(8,128)} %get-tuple-element.62.att_ref.refs_1_, bf16[2,512,3072]{2,1,0:T(8,128)(2,1)} %bitcast.120, f32[4,512]{1,0:T(4,128)} %get-tuple-element.219.refs_3_.norm_ref.refs_5_), custom_call_target="tpu_custom_call" | custom-call | flops 32000000000 | bytes 3200000 | tf_op jit(solution)/shard_map/feed_forward/pallas_call | solution.py:544
  120.9 4.0 all-gather.2.cloned.1.call-done
  124.9 33.0 %attend_forward.3 = (f32[2624,512]{1,0:T(8,128)}, bf16[2624,1536]{1,0:T(8,128)(2,1)}, bf16[2624,512]{1,0:T(8,128)(2,1)}, bf16[2624,512]{1,0:T(8,128)(2,1)}, f32[2624,512]{1,0:T(8,128)}) custom-call(f32[2624,512]{1,0:T(8,128)} %get-tuple-element.63.refs_0_.x_ref, f32[2624,128]{1,0:T(8,128)} %broadcast_in_dim.68.refs_1_.refs_0_.mask_ref, ...), custom_call_target="tpu_custom_call" | custom-call | flops 49999998976 | bytes 5000000 | tf_op jit(solution)/shard_map/attend_forward/pallas_call | solution.py:522
  157.9 24.3 %feed_forward.3 = (bf16[2624,512]{1,0:T(8,128)(2,1)}, bf16[2624,2048]{1,0:T(8,128)(2,1)}, bf16[2624,2048]{1,0:T(8,128)(2,1)}) custom-call(f32[2624,512]{1,0:T(8,128)} %get-tuple-element.65.att_ref.refs_2_, bf16[2,512,3072]{2,1,0:T(8,128)(2,1)} %bitcast.152, f32[4,512]{1,0:T(4,128)} %get-tuple-element.218.refs_3_.norm_ref.refs_6_), custom_call_target="tpu_custom_call" | custom-call | flops 32000000000 | bytes 3200000 | tf_op jit(solution)/shard_map/feed_forward/pallas_call | solution.py:544
  182.2 37.3 %feed_back.2 = (f32[2624,512]{1,0:T(8,128)}, bf16[2,512,2048]{2,1,0:T(8,128)(2,1)}, f32[2,512]{1,0:T(2,128)}) custom-call(f32[2624,128]{1,0:T(8,128)} %broadcast_in_dim.68.refs_1_.refs_0_.mask_ref, f32[2624,512]{1,0:T(8,128)} %refs_1_.1, f32[2624,512]{1,0:T(8,128)} %get-tuple-element.65.att_ref.refs_2_, bf16[2624,2048]{1,0:T(8,128)(2,1)} %get-tuple-element.67.refs_3_, ...), custom_call_target="tpu_custom_call" | custom-call | flops 41000001536 | bytes 4100000 | tf_op jit(solution)/shard_map/feed_back/pallas_call | solution.py:566
  219.6 66.2 %attend_back.2 = (f32[2624,512]{1,0:T(8,128)}, bf16[2,512,1024]{2,1,0:T(8,128)(2,1)}, f32[2,512]{1,0:T(2,128)}, f32[9,8,512]{2,1,0:T(8,128)}, f32[49,8,512]{2,1,0:T(8,128)}) custom-call(f32[2624,512]{1,0:T(8,128)} %get-tuple-element.69.gatt_ref, f32[2624,512]{1,0:T(8,128)} %get-tuple-element.63.refs_0_.x_ref, f32[2624,512]{1,0:T(8,128)} %get-tuple-element.70.conv_ref, ...), custom_call_target="tpu_custom_call" | custom-call | flops 92000002048 | bytes 9200000 | tf_op jit(solution)/shard_map/attend_back/pallas_call | solution.py:592
  285.8 36.0 %feed_back.3 = (f32[2624,512]{1,0:T(8,128)}, bf16[2,512,2048]{2,1,0:T(8,128)(2,1)}, f32[2,512]{1,0:T(2,128)}) custom-call(f32[2624,512]{1,0:T(8,128)} %get-tuple-element.74.refs_0_, f32[2624,512]{1,0:T(8,128)} %get-tuple-element.62.att_ref.refs_1_, bf16[2624,2048]{1,0:T(8,128)(2,1)} %get-tuple-element.75.refs_2_, ...), custom_call_target="tpu_custom_call" | custom-call | flops 41000001536 | bytes 4100000 | tf_op jit(solution)/shard_map/feed_back/pallas_call | solution.py:566
  321.8 69.0 %attend_back.3 = (f32[2624,512]{1,0:T(8,128)}, bf16[2,512,1024]{2,1,0:T(8,128)(2,1)}, f32[2,512]{1,0:T(2,128)}, f32[9,8,512]{2,1,0:T(8,128)}, f32[49,8,512]{2,1,0:T(8,128)}) custom-call(f32[2624,512]{1,0:T(8,128)} %get-tuple-element.77.gatt_ref, f32[2624,512]{1,0:T(8,128)} %get-tuple-element.78.x_ref, f32[2624,512]{1,0:T(8,128)} %get-tuple-element.79.conv_ref, ...), custom_call_target="tpu_custom_call" | custom-call | flops 92000002048 | bytes 9200000 | tf_op jit(solution)/shard_map/attend_back/pallas_call | solution.py:592
  390.8 1.3 reduce_sum.73
  392.5 1.0 reduce_sum.72
  393.5 0.7 convert.89
  394.5 0.7 broadcast_in_dim.76
  395.3 0.7 broadcast_in_dim.77
  396.0 49.7 %collect.1 = f32[32,4352]{1,0:T(8,128)} custom-call(bf16[32,32,1024]{2,1,0:T(8,128)(2,1)} %bitcast.131, bf16[32,32,128]{2,1,0:T(8,128)(2,1)} %bitcast.138, bf16[32,32,1024]{2,1,0:T(8,128)(2,1)} %bitcast.132, bf16[32,32,128]{2,1,0:T(8,128)(2,1)} %bitcast.139, bf16[32,32,2048]{2,1,0:T(8,128)(2,1)} %bitcast.124), custom_call_target="tpu_custom_call" | custom-call | tf_op jit(solution)/shard_map/collect/pallas_call | solution.py:818
  445.7 1.0 slice_bitcast_fusion.4
  447.1 1.0 slice_bitcast_fusion.10
  449.1 0.9 pad_maximum_fusion
  450.0 4.8 all-to-all-start
  455.2 1.0 reshape.382
  456.9 0.8 slice_bitcast_fusion
  457.8 13.6 %all-to-all-done = bf16[16,1,32,640]{3,2,1,0:T(8,128)(2,1)S(1)} async-done(((bf16[16,1,32,640]{3,2,1,0:T(8,128)(2,1)}), bf16[16,1,32,640]{3,2,1,0:T(8,128)(2,1)S(1)}, u32[]{:S(2)}, u32[]{:S(2)}) %all-to-all-start) | async-done | bytes 655392 | tf_op jit(solution)/shard_map/all_to_all | solution.py:1038
  471.4 0.8 copy-done
  472.2 10.3 %schulz.1 = bf16[1,512,512]{2,1,0:T(8,128)(2,1)} custom-call(bf16[1,512,640]{2,1,0:T(8,128)(2,1)} %bitcast.125), custom_call_target="tpu_custom_call" | custom-call | tf_op jit(solution)/shard_map/schulz/pallas_call | solution.py:838
  482.5 0.9 slice_bitcast_fusion.5
  483.4 5.1 all-to-all-start.1
  490.6 0.8 copy.179
  491.6 0.8 copy.180
  492.6 0.7 divide_subtract_fusion
  493.3 9.7 %all-to-all-done.1 = bf16[16,1,32,512]{3,2,1,0:T(8,128)(2,1)S(1)} async-done(((bf16[16,1,32,512]{3,2,1,0:T(8,128)(2,1)}), bf16[16,1,32,512]{3,2,1,0:T(8,128)(2,1)S(1)}, u32[]{:S(2)}, u32[]{:S(2)}) %all-to-all-start.1) | async-done | bytes 524320 | tf_op jit(solution)/shard_map/all_to_all | solution.py:1044
  503.7 0.7 fusion.33
  505.7 0.8 fusion.31
  506.8 0.8 fusion.30
  (160 shorter events, 10.5 us)
Async XLA Ops:
  7.2 117.7 %all-gather.2.cloned.1.call-start = ((), (), s32[]{:S(2)}) async-start(), calls=%async_computation.3 | async-start | bytes 6488064 | tf_op jit(solution)/shard_map/all_gather | solution.py:923
  9.2 44.4 %copy-start.31 = (s32[64]{0:T(128)S(1)}, s32[64]{0:T(128)}, u32[]{:S(2)}) copy-start(s32[64]{0:T(128)} %param.19) | copy-start | bytes 772
  9.5 44.6 %copy-start.20 = (f32[2,9,512]{2,0,1:T(2,128)S(1)}, f32[2,9,512]{2,0,1:T(2,128)}, u32[]{:S(2)}) copy-start(f32[2,9,512]{2,0,1:T(2,128)} %param.25) | copy-start | bytes 110596
  9.5 44.8 %copy-start.18 = (f32[2,32,768]{2,1,0:T(8,128)S(1)}, f32[2,32,768]{2,1,0:T(8,128)}, u32[]{:S(2)}) copy-start(f32[2,32,768]{2,1,0:T(8,128)} %param.27) | copy-start | bytes 589828
  12.3 43.3 %copy-start.5 = (f32[2,1024,32]{1,2,0:T(8,128)S(1)}, f32[2,1024,32]{1,2,0:T(8,128)}, u32[]{:S(2)}) copy-start(f32[2,1024,32]{1,2,0:T(8,128)} %param.30) | copy-start | bytes 786436
  12.3 44.2 %copy-start.7 = (f32[2,32,1024]{2,1,0:T(8,128)S(1)}, f32[2,32,1024]{2,1,0:T(8,128)}, u32[]{:S(2)}) copy-start(f32[2,32,1024]{2,1,0:T(8,128)} %param.29) | copy-start | bytes 786436
  12.3 45.0 %copy-start.23 = (f32[2,4,512]{2,1,0:T(4,128)S(1)}, f32[2,4,512]{2,1,0:T(4,128)}, u32[]{:S(2)}) copy-start(f32[2,4,512]{2,1,0:T(4,128)} %param.24) | copy-start | bytes 49156
  12.3 46.9 %copy-start.10 = (f32[2,49,512]{2,0,1:T(2,128)S(1)}, f32[2,49,512]{2,0,1:T(2,128)}, u32[]{:S(2)}) copy-start(f32[2,49,512]{2,0,1:T(2,128)} %param.26) | copy-start | bytes 602116
  52.1 342.4 %reduce-scatter.2.cloned.1.call-start = ((), (), s32[]{:S(2)}) async-start(), calls=%async_computation.4 | async-start | bytes 4325376 | tf_op jit(solution)/shard_map/reduce_scatter | solution.py:986
  321.8 70.4 %copy-start.9 = (f32[49,8,512]{2,1,0:T(8,128)S(1)}, f32[49,8,512]{2,1,0:T(8,128)}, u32[]{:S(2)}) copy-start(f32[49,8,512]{2,1,0:T(8,128)} %get-tuple-element.89) | copy-start | bytes 2408452
  321.8 70.6 %copy-start.19 = (f32[9,8,512]{2,1,0:T(8,128)S(1)}, f32[9,8,512]{2,1,0:T(8,128)}, u32[]{:S(2)}) copy-start(f32[9,8,512]{2,1,0:T(8,128)} %get-tuple-element.88) | copy-start | bytes 442372
  321.8 70.6 %copy-start.28 = (f32[2,512]{1,0:T(2,128)S(1)}, f32[2,512]{1,0:T(2,128)}, u32[]{:S(2)}) copy-start(f32[2,512]{1,0:T(2,128)} %get-tuple-element.87) | copy-start | bytes 12292
  321.8 70.6 %copy-start.29 = (f32[2,512]{1,0:T(2,128)S(1)}, f32[2,512]{1,0:T(2,128)}, u32[]{:S(2)}) copy-start(f32[2,512]{1,0:T(2,128)} %get-tuple-element.86) | copy-start | bytes 12292
  321.8 71.6 %copy-start.30 = (f32[2,512]{1,0:T(2,128)S(1)}, f32[2,512]{1,0:T(2,128)}, u32[]{:S(2)}) copy-start(f32[2,512]{1,0:T(2,128)} %get-tuple-element.92) | copy-start | bytes 12292
  321.8 72.3 %copy-start.15 = (f32[49,512]{1,0:T(8,128)S(1)}, f32[49,512]{1,0:T(8,128)}, u32[]{:S(2)}) copy-start(f32[49,512]{1,0:T(8,128)} %reshape.376) | copy-start | bytes 301060
  395.2 51.5 %copy-start.13 = (f32[2,32,768]{2,1,0:T(8,128)S(1)}, f32[2,32,768]{2,1,0:T(8,128)}, u32[]{:S(2)}) copy-start(f32[2,32,768]{2,1,0:T(8,128)} %reshape.373) | copy-start | bytes 589828
  395.3 51.5 %copy-start.25 = (f32[2,256,32]{1,2,0:T(8,128)S(1)}, f32[2,256,32]{1,2,0:T(8,128)}, u32[]{:S(2)}) copy-start(f32[2,256,32]{1,2,0:T(8,128)} %param.28) | copy-start | bytes 196612
  396.0 52.6 %copy-start.14 = (bf16[32,2048]{1,0:T(8,128)(2,1)S(1)}, bf16[32,2048]{1,0:T(8,128)(2,1)}, u32[]{:S(2)}) copy-start(bf16[32,2048]{1,0:T(8,128)(2,1)} %reduce-scatter.2.cloned.1.call-done) | copy-start | bytes 393220
  396.0 52.8 %copy-start.3 = (f32[2,32,4,256]{3,2,1,0:T(4,128)S(1)}, f32[2,32,4,256]{3,2,1,0:T(4,128)}, u32[]{:S(2)}) copy-start(f32[2,32,4,256]{3,2,1,0:T(4,128)} %concatenate.56) | copy-start | bytes 786436
  396.0 52.8 %copy-start.4 = (f32[2,32,4,256]{3,2,1,0:T(4,128)S(1)}, f32[2,32,4,256]{3,2,1,0:T(4,128)}, u32[]{:S(2)}) copy-start(f32[2,32,4,256]{3,2,1,0:T(4,128)} %concatenate.55) | copy-start | bytes 786436
  447.1 9.8 %copy-start.6 = (f32[2,1024,32]{1,2,0:T(8,128)S(1)}, f32[2,1024,32]{1,2,0:T(8,128)}, u32[]{:S(2)}) copy-start(f32[2,1024,32]{1,2,0:T(8,128)} %param.30) | copy-start | bytes 786436
  447.1 9.8 %copy-start.8 = (f32[2,32,1024]{2,1,0:T(8,128)S(1)}, f32[2,32,1024]{2,1,0:T(8,128)}, u32[]{:S(2)}) copy-start(f32[2,32,1024]{2,1,0:T(8,128)} %param.29) | copy-start | bytes 786436
  450.0 38.8 %copy-start.26 = (f32[2,9,512]{2,0,1:T(2,128)S(1)}, f32[2,9,512]{2,0,1:T(2,128)}, u32[]{:S(2)}) copy-start(f32[2,9,512]{2,0,1:T(2,128)} %param.32) | copy-start | bytes 110596
  450.0 38.9 %copy-start.17 = (f32[2,49,512]{2,0,1:T(2,128)S(1)}, f32[2,49,512]{2,0,1:T(2,128)}, u32[]{:S(2)}) copy-start(f32[2,49,512]{2,0,1:T(2,128)} %param.33) | copy-start | bytes 602116
  450.0 21.4 %all-to-all-start = ((bf16[16,1,32,640]{3,2,1,0:T(8,128)(2,1)}), bf16[16,1,32,640]{3,2,1,0:T(8,128)(2,1)S(1)}, u32[]{:S(2)}, u32[]{:S(2)}) async-start(bf16[16,1,32,640]{3,2,1,0:T(8,128)(2,1)} %pad_maximum_fusion), calls=%async_computation.1 | async-start | bytes 1310720 | tf_op jit(solution)/shard_map/all_to_all | solution.py:1038
  454.7 34.4 %copy-start.21 = (f32[2,9,512]{2,0,1:T(2,128)S(1)}, f32[2,9,512]{2,0,1:T(2,128)}, u32[]{:S(2)}) copy-start(f32[2,9,512]{2,0,1:T(2,128)} %param.25) | copy-start | bytes 110596
  454.8 36.8 %copy-start.11 = (f32[2,49,512]{2,0,1:T(2,128)S(1)}, f32[2,49,512]{2,0,1:T(2,128)}, u32[]{:S(2)}) copy-start(f32[2,49,512]{2,0,1:T(2,128)} %param.26) | copy-start | bytes 602116
  455.1 37.3 %copy-start.27 = (f32[2,4,512]{2,1,0:T(4,128)S(1)}, f32[2,4,512]{2,1,0:T(4,128)}, u32[]{:S(2)}) copy-start(f32[2,4,512]{2,1,0:T(4,128)} %param.31) | copy-start | bytes 49156
  455.2 37.4 %copy-start.24 = (f32[2,4,512]{2,1,0:T(4,128)S(1)}, f32[2,4,512]{2,1,0:T(4,128)}, u32[]{:S(2)}) copy-start(f32[2,4,512]{2,1,0:T(4,128)} %param.24) | copy-start | bytes 49156
  471.4 0.8 copy-start
  483.4 20.3 %copy-start.12 = (f32[2,32,768]{2,1,0:T(8,128)S(1)}, f32[2,32,768]{2,1,0:T(8,128)}, u32[]{:S(2)}) copy-start(f32[2,32,768]{2,1,0:T(8,128)} %param.20) | copy-start | bytes 589828
  483.4 19.6 %all-to-all-start.1 = ((bf16[16,1,32,512]{3,2,1,0:T(8,128)(2,1)}), bf16[16,1,32,512]{3,2,1,0:T(8,128)(2,1)S(1)}, u32[]{:S(2)}, u32[]{:S(2)}) async-start(bf16[16,1,32,512]{3,2,1,0:T(8,128)(2,1)} %bitcast.129), calls=%async_computation.2 | async-start | bytes 1048576 | tf_op jit(solution)/shard_map/all_to_all | solution.py:1044
  488.5 16.1 %copy-start.16 = (f32[2,256,32]{1,2,0:T(8,128)S(1)}, f32[2,256,32]{1,2,0:T(8,128)}, u32[]{:S(2)}) copy-start(f32[2,256,32]{1,2,0:T(8,128)} %param.21) | copy-start | bytes 196612
  489.3 16.4 %copy-start.1 = (f32[2,32,1024]{2,1,0:T(8,128)S(1)}, f32[2,32,1024]{2,1,0:T(8,128)}, u32[]{:S(2)}) copy-start(f32[2,32,1024]{2,1,0:T(8,128)} %param.22) | copy-start | bytes 786436
  492.6 14.2 %copy-start.22 = (f32[2,4,512]{2,1,0:T(4,128)}, f32[2,4,512]{2,1,0:T(4,128)S(1)}, u32[]{:S(2)}) copy-start(f32[2,4,512]{2,1,0:T(4,128)S(1)} %get-tuple-element.189) | copy-start | bytes 49156
  493.3 13.5 %copy-start.2 = (f32[2,1024,32]{1,2,0:T(8,128)S(1)}, f32[2,1024,32]{1,2,0:T(8,128)}, u32[]{:S(2)}) copy-start(f32[2,1024,32]{1,2,0:T(8,128)} %param.23) | copy-start | bytes 786436
Sparse Core Ops, SparseCore 0:
  52.3 72.5 all-gather.1
  219.7 140.7 reduce-scatter.1
